TPU v7x, 128 devices: a whole 4x4x4 slice. The times are simulated.
128 devices in a mesh: sec: 2 (over y_hi), row: 32 (over x, y_lo, z), col: 2 (over core).
Axes of the slice: x: 4, y: 4 (y_hi: 2, y_lo: 2; y = y_hi * 2 + y_lo), z: 4, core: 2. Of those that a mesh axis runs over, the one named last changes fastest.
Arguments:
- populations: float32 [19, 2048, 256], P(None, ('sec', 'row', 'col')), may hold values from 0.01 to 0.1
- relaxation: float32 [2048, 256], P(('sec', 'row', 'col')), may hold values from 0.6 to 1.9
- send_lists: int32 [128, 32], P(('sec', 'row', 'col')), may hold values from 0 to 31, as said below
- lift_weight: bfloat16 [320, 81], replicated, may hold values from -0.625 to 0.625
- norm_gain: float32 [320], replicated, may hold values from 0.1 to 1.9
- norm_shift: float32 [320], replicated, may hold values from -3 to 3
- mix_master: float32 [1280, 320], P(('row', 'col')), may hold values from -0.3125 to 0.3125
- mix_first: float32 [1280, 320], P(('row', 'col')), may hold values from -1.5 to 1.5
- mix_second: float32 [1280, 320], P(('row', 'col')), may hold values from 0.1 to 1
- out_weight: bfloat16 [3, 320], replicated, may hold values from -0.3125 to 0.3125
Outputs:
- after: float32 [19, 2048, 256], P(None, ('sec', 'row', 'col'))
- new_master: float32 [1280, 320], P(('row', 'col'))
- new_first: float32 [1280, 320], P(('row', 'col'))
- new_second: float32 [1280, 320], P(('row', 'col'))
Inputs may be any that keep to these rules, and one draw needn't show every extreme that they name: `send_lists`: within each sec and col index, a device sends exactly 2 of its 32 bricks to each of 16 distinct trainers along row, and every trainer receives exactly 32 bricks.
All inputs are finite; a program needn't handle non-finite values.
Results may differ from a plain program's by a relative error of at most 0.0003.
The roundings to bfloat16 on the way count: a program that leaves them out, or rounds other values in their place, can miss the bound.
Values may be sent and summed in bfloat16 or wider, within the bound.
No kernel may reach another device: no remote copies, remote signals or barrier semaphores. Data moves between devices by JAX's collectives and lax.ppermute only.
A program may use at most 64 MiB of HBM per device.

v0:
```python
import jax
import jax.numpy as jnp
from jax import lax
from jax.sharding import PartitionSpec as P

BRK_X = 4
BRK_Y = 4
BRK_Z = 8
CY = 16
CZ = 16
CYZ = 256
V = 128
BRICKS = 32


VELOCITIES = (
    (0, 0, 0),
    (1, 0, 0),
    (-1, 0, 0),
    (0, 1, 0),
    (0, -1, 0),
    (0, 0, 1),
    (0, 0, -1),
    (1, 1, 0),
    (-1, -1, 0),
    (1, -1, 0),
    (-1, 1, 0),
    (1, 0, 1),
    (-1, 0, -1),
    (1, 0, -1),
    (-1, 0, 1),
    (0, 1, 1),
    (0, -1, -1),
    (0, 1, -1),
    (0, -1, 1),
)
LATTICE_WEIGHTS = (1.0 / 3.0,) + (1.0 / 18.0,) * 6 + (1.0 / 36.0,) * 12


def extended(shard, sides, width):
    for axis, dim in sides:
        size, length = (lax.axis_size(axis), shard.shape[dim])
        up = [(i, (i + 1) % size) for i in range(size)]
        down = [(j, i) for i, j in up]
        last = lax.slice_in_dim(shard, length - width, length, axis=dim)
        initial = lax.slice_in_dim(shard, 0, width, axis=dim)
        before = lax.ppermute(last, axis, up)
        after = lax.ppermute(initial, axis, down)
        shard = jnp.concatenate([before, shard, after], axis=dim)
    return shard


def moments(read):
    density = read[0]
    moment_x = jnp.zeros_like(density)
    moment_y = jnp.zeros_like(density)
    moment_z = jnp.zeros_like(density)
    for index in range(1, 19):
        along_x, along_y, along_z = VELOCITIES[index]
        density = density + read[index]
        moment_x = moment_x + along_x * read[index]
        moment_y = moment_y + along_y * read[index]
        moment_z = moment_z + along_z * read[index]
    return (density, (moment_x / density, moment_y / density, moment_z / density))


def collide(read, density, flow, relaxation):
    speed = flow[0] * flow[0] + flow[1] * flow[1] + flow[2] * flow[2]
    result = []
    for index in range(19):
        along_x, along_y, along_z = VELOCITIES[index]
        project = along_x * flow[0] + along_y * flow[1] + along_z * flow[2]
        balance = (
            LATTICE_WEIGHTS[index]
            * density
            * (1.0 + 3.0 * project + 4.5 * project * project - 1.5 * speed)
        )
        result.append(read[index] - relaxation * (read[index] - balance))
    return jnp.stack(result)


def gelu_value(value):
    return 0.5 * value * (1.0 + lax.erf(value * 0.7071067811865476))


def gelu_slope(value):
    return (
        0.5 * (1.0 + lax.erf(value * 0.7071067811865476))
        + value * jnp.exp(-0.5 * value * value) * 0.3989422804014327
    )


def unfold(brick):
    inputs = brick[:3].reshape(3, BRK_X, BRK_Y, BRK_Z)
    padded = jnp.pad(inputs, ((0, 0), (1, 1), (1, 1), (1, 1)))
    taps = []
    for shift_x in range(3):
        for shift_y in range(3):
            for shift_z in range(3):
                taps.append(
                    padded[
                        :,
                        shift_x : shift_x + BRK_X,
                        shift_y : shift_y + BRK_Y,
                        shift_z : shift_z + BRK_Z,
                    ]
                )
    return jnp.stack(taps, axis=1).reshape(81, V)


def brick_sums(brick, lift_weight):
    lifted = jnp.dot(lift_weight, unfold(brick), preferred_element_type=jnp.float32)
    return jnp.stack([jnp.sum(lifted, axis=1), jnp.sum(lifted * lifted, axis=1)])


def normalizers(totals):
    count = BRICKS * V
    mean = totals[..., 0, :] / count
    spread = totals[..., 1, :] / count - mean * mean
    return (mean, lax.rsqrt(spread + 1e-05))


def train_bricks(bricks, means, scales, lift_weight, norm_gain, norm_shift, mixing, out_weight):
    layers = mixing.shape[0]

    def one_brick(total, inputs):
        brick, mean, scale = inputs
        lifted = jnp.dot(lift_weight, unfold(brick), preferred_element_type=jnp.float32)
        normed = (lifted - mean[:, None]) * (scale * norm_gain)[:, None] + norm_shift[:, None]
        current = gelu_value(normed).astype(jnp.bfloat16)
        states = []
        befores = []
        for layer in range(layers):
            mixed = jnp.dot(mixing[layer], current, preferred_element_type=jnp.float32)
            states.append(current)
            befores.append(mixed)
            current = (current.astype(jnp.float32) + gelu_value(mixed)).astype(jnp.bfloat16)
        output = jnp.dot(out_weight, current, preferred_element_type=jnp.float32)
        target = brick[3:].astype(jnp.float32)
        delta = ((output - target) * (2.0 / (3.0 * V))).astype(jnp.bfloat16)
        back = lax.dot_general(
            out_weight, delta, (((0,), (0,)), ((), ())), preferred_element_type=jnp.float32
        )
        terms = [None] * layers
        for layer in range(layers - 1, -1, -1):
            inner = (back * gelu_slope(befores[layer])).astype(jnp.bfloat16)
            terms[layer] = lax.dot_general(
                inner, states[layer], (((1,), (1,)), ((), ())), preferred_element_type=jnp.float32
            )
            if layer > 0:
                back = back + lax.dot_general(
                    mixing[layer],
                    inner,
                    (((0,), (0,)), ((), ())),
                    preferred_element_type=jnp.float32,
                )
        return (total + jnp.stack(terms), None)

    start = jnp.zeros(mixing.shape, jnp.float32)
    total, unused = lax.scan(one_brick, start, (bricks, means, scales))
    return total


def adamw(master, gradient, first, second):
    first_next = 0.9 * first + 0.1 * gradient
    second_next = 0.999 * second + 0.001 * gradient * gradient
    ratio = first_next / (1.0 - 0.9**10) / (jnp.sqrt(second_next / (1.0 - 0.999**10)) + 1e-08)
    return (master - 0.01 * (ratio + 0.1 * master), first_next, second_next)


def body(
    populations,
    relaxation,
    send_lists,
    lift_weight,
    norm_gain,
    norm_shift,
    mix_master,
    mix_first,
    mix_second,
    out_weight,
):
    width = populations.shape[1]
    channels = lift_weight.shape[0]
    shifted_x = []
    padded = extended(populations, ((("sec", "row", "col"), 1),), 1)
    for index in range(19):
        along_x = VELOCITIES[index][0]
        shifted_x.append(padded[index, 1 - along_x : 1 - along_x + width])
    planes = []
    for index in range(19):
        along_x, along_y, along_z = VELOCITIES[index]
        moved = jnp.roll(shifted_x[index].reshape(width, CY, CZ), (along_y, along_z), (1, 2))
        planes.append(moved.reshape(width, CYZ))
    read = jnp.stack(planes)
    density, flow = moments(read)
    after = collide(read, density, flow, relaxation)
    old_density, old_flow = moments(populations)
    field = jnp.stack(list(old_flow) + list(flow)).astype(jnp.bfloat16)
    bricks = (
        field.reshape(6, 4, BRK_X, 4, BRK_Y, 2, BRK_Z)
        .transpose(1, 3, 5, 0, 2, 4, 6)
        .reshape(BRICKS, 6, V)
    )
    gathered = lax.all_gather(mix_master.astype(jnp.bfloat16), ("row", "col"), axis=0, tiled=True)
    mixing = gathered.reshape(-1, channels, channels)
    targets = send_lists[0]
    trainers = lax.axis_size("row")
    capacity = max(2, BRICKS // trainers)
    order = jnp.arange(BRICKS, dtype=jnp.int32)
    same = (targets[:, None] == targets[None, :]) & (order[:, None] < order[None, :])
    ranks = jnp.sum(same.astype(jnp.int32), axis=0)
    select = (
        (targets[None, None, :] == jnp.arange(trainers, dtype=jnp.int32)[:, None, None])
        & (ranks[None, None, :] == jnp.arange(capacity, dtype=jnp.int32)[None, :, None])
    ).astype(jnp.float32)
    flags_out = jnp.sum(select, axis=2)
    flat = bricks.reshape(BRICKS, 6 * V)
    outgoing = jnp.einsum(
        "scj,jm->scm", select.astype(jnp.bfloat16), flat, preferred_element_type=jnp.float32
    ).astype(jnp.bfloat16)
    arrived, arrived_flags = (
        lax.all_to_all(outgoing, "row", split_axis=0, concat_axis=0, tiled=True),
        lax.all_to_all(
            flags_out.astype(jnp.bfloat16), "row", split_axis=0, concat_axis=0, tiled=True
        ),
    )
    live = arrived_flags.reshape(-1).astype(jnp.float32)
    position = jnp.cumsum(live) - live
    pick = (
        live[None, :] * (position[None, :] == jnp.arange(BRICKS, dtype=jnp.float32)[:, None])
    ).astype(jnp.bfloat16)
    held = (
        jnp.dot(pick, arrived.reshape(-1, 6 * V), preferred_element_type=jnp.float32)
        .astype(jnp.bfloat16)
        .reshape(BRICKS, 6, V)
    )
    sums = lax.map(lambda single: brick_sums(single, lift_weight), held)
    mean, scale = normalizers(jnp.sum(sums, axis=0))
    means = jnp.broadcast_to(mean, (BRICKS, channels))
    scales = jnp.broadcast_to(scale, (BRICKS, channels))
    gradient_term = train_bricks(
        held, means, scales, lift_weight, norm_gain, norm_shift, mixing, out_weight
    )
    flat_term = gradient_term.reshape(-1, channels)
    across = lax.psum(flat_term, "sec")
    gradient = lax.psum_scatter(across, ("row", "col"), scatter_dimension=0, tiled=True)
    new_master, new_first, new_second = adamw(mix_master, gradient, mix_first, mix_second)
    return (after, new_master, new_first, new_second)


def solution(mesh):
    in_specs = (
        P(None, ("sec", "row", "col"), None),
        P(("sec", "row", "col"), None),
        P(("sec", "row", "col"), None),
        P(),
        P(),
        P(),
        P(("row", "col"), None),
        P(("row", "col"), None),
        P(("row", "col"), None),
        P(),
    )
    out_specs = (
        P(None, ("sec", "row", "col"), None),
        P(("row", "col"), None),
        P(("row", "col"), None),
        P(("row", "col"), None),
    )
    return jax.shard_map(body, mesh=mesh, in_specs=in_specs, out_specs=out_specs, check_vma=False)
```

profile of v0, /device:TPU:0, one launch (start us, length us, event | category | flops | bytes accessed | tf_op | source)
XLA Modules:
  0.0 1544.3 jit_solution(16220101323327105868)
XLA Ops:
  8.8 8.2 collective-permute-start.1
  19.3 3.8 all-to-all-start
  30.4 85.5 %all-gather = bf16[64,20,320]{2,1,0:T(8,128)(2,1)S(1)} all-gather(bf16[1,20,320]{2,1,0:T(8,128)(2,1)S(1)} %convert_bitcast_fusion), channel_id=1, replica_groups=mesh['sec'=2,'row'=32,'col'=2] {'row','col'}, dimensions={0}, use_global_device_ids=true | all-gather | bytes 832000 | tf_op jit(solution)/shard_map/all_gather | solution.py:205
  159.8 3.9 all-to-all-start.1
  164.5 7.8 all-to-all-done.1
  173.2 148.0 %while.25 = (s32[]{:T(128)}, f32[32,2,320]{2,1,0:T(2,128)S(1)}, bf16[32,6,128]{2,1,0:T(8,128)(2,1)}, bf16[320,81]{0,1:T(8,128)(2,1)}, s32[]{:T(128)}) while((s32[]{:T(128)}, f32[32,2,320]{2,1,0:T(2,128)S(1)}, bf16[32,6,128]{2,1,0:T(8,128)(2,1)}, bf16[320,81]{0,1:T(8,128)(2,1)}, s32[]{:T(128)}) %tuple.110), condition=%wide.region_6.7_spmd, body=%wide.region_3.6_spmd.sunk | while | flops 6758402 | bytes 829133 | solution.py:238
  322.6 657.2 %while.26 = (s32[]{:T(128)}, f32[4,320,320]{2,1,0:T(8,128)S(1)}, bf16[32,6,128]{2,1,0:T(8,128)(2,1)}, bf16[320,81]{0,1:T(8,128)(2,1)}, f32[32,320]{1,0:T(8,128)}...) while((s32[]{:T(128)}, f32[4,320,320]{2,1,0:T(8,128)S(1)}, ...), condition=%wide.region_9.10_spmd.clone, body=%wide.region_8.9_spmd.clone.sunk | while | flops 301180736 | bytes 15499135 | solution.py:160
  329.7 1.9 add_convert_fusion.11
  339.1 2.5 convolution_bitcast_fusion.22
  350.2 1.9 add_convert_fusion.11
  359.6 2.5 convolution_bitcast_fusion.22
  370.8 1.9 add_convert_fusion.11
  380.2 2.5 convolution_bitcast_fusion.22
  391.3 1.9 add_convert_fusion.11
  400.7 2.5 convolution_bitcast_fusion.22
  411.9 1.9 add_convert_fusion.11
  421.2 2.5 convolution_bitcast_fusion.22
  432.4 1.9 add_convert_fusion.11
  441.8 2.6 convolution_bitcast_fusion.22
  452.9 1.9 add_convert_fusion.11
  462.3 2.5 convolution_bitcast_fusion.22
  482.8 2.5 convolution_bitcast_fusion.22
  494.0 1.9 add_convert_fusion.11
  503.4 2.6 convolution_bitcast_fusion.22
  514.5 1.9 add_convert_fusion.11
  523.9 2.5 convolution_bitcast_fusion.22
  535.1 1.9 add_convert_fusion.11
  544.5 2.6 convolution_bitcast_fusion.22
  555.6 1.9 add_convert_fusion.11
  565.0 2.5 convolution_bitcast_fusion.22
  576.2 1.9 add_convert_fusion.11
  585.5 2.5 convolution_bitcast_fusion.22
  596.7 1.9 add_convert_fusion.11
  606.1 2.5 convolution_bitcast_fusion.22
  626.6 2.5 convolution_bitcast_fusion.22
  647.2 2.5 convolution_bitcast_fusion.22
  658.4 1.9 add_convert_fusion.11
  667.7 2.5 convolution_bitcast_fusion.22
  678.9 1.9 add_convert_fusion.11
  688.3 2.6 convolution_bitcast_fusion.22
  699.5 1.9 add_convert_fusion.11
  708.8 2.5 convolution_bitcast_fusion.22
  720.0 1.9 add_convert_fusion.11
  729.4 2.6 convolution_bitcast_fusion.22
  740.5 1.9 add_convert_fusion.11
  749.9 2.5 convolution_bitcast_fusion.22
  770.4 2.5 convolution_bitcast_fusion.22
  781.6 1.9 add_convert_fusion.11
  790.9 2.5 convolution_bitcast_fusion.22
  811.5 2.5 convolution_bitcast_fusion.22
  822.6 1.9 add_convert_fusion.11
  832.0 2.6 convolution_bitcast_fusion.22
  852.5 2.5 convolution_bitcast_fusion.22
  863.7 1.9 add_convert_fusion.11
  873.1 2.6 convolution_bitcast_fusion.22
  893.6 2.5 convolution_bitcast_fusion.22
  914.1 2.5 convolution_bitcast_fusion.22
  934.6 2.5 convolution_bitcast_fusion.22
  945.8 1.9 add_convert_fusion.11
  955.2 2.5 convolution_bitcast_fusion.22
  966.4 1.9 add_convert_fusion.11
  975.7 2.5 convolution_bitcast_fusion.22
  986.1 538.2 %all-reduce.5.cloned.1.call-done = f32[1280,320]{1,0:T(8,128)} async-done(((f32[1280,320]{1,0:T(8,128)}), f32[1280,320]{1,0:T(8,128)}) %all-reduce.5.cloned.1.call-update) | async-done | bytes 1638416
  1525.2 11.6 psum.8
  (3150 shorter events, 736.6 us)
Async XLA Ops:
  7.2 23.2 %copy-start.8 = (f32[20,320]{1,0:T(8,128)S(1)}, f32[20,320]{1,0:T(8,128)}, u32[]{:S(2)}) copy-start(f32[20,320]{1,0:T(8,128)} %param.20) | copy-start | bytes 76804
  8.8 113.8 %collective-permute-start = (f32[19,1,256]{2,1,0:T(1,128)}, f32[19,1,256]{2,1,0:T(1,128)S(1)}, u32[]{:S(2)}, u32[]{:S(2)}) collective-permute-start(f32[19,1,256]{2,1,0:T(1,128)} %get-tuple-element.302), channel_id=1, source_target_pairs={{0,1},{1,2},{2,3},{3,4},{4,5},{5,6},{6,7},{7,8},{8,9},{9,10},{10,1... | collective-permute-start | bytes 58376 | tf_op jit(solution)/shard_map/ppermute | solution.py:47
  8.8 114.2 %collective-permute-start.1 = (f32[19,1,256]{2,1,0:T(1,128)}, f32[19,1,256]{2,1,0:T(1,128)}, u32[]{:S(2)}, u32[]{:S(2)}) collective-permute-start(f32[19,1,256]{2,1,0:T(1,128)} %get-tuple-element.303), channel_id=1, source_target_pairs={{1,0},{2,1},{3,2},{4,3},{5,4},{6,5},{7,6},{8,7},{9,8},{10,9},{11,1... | collective-permute-start | bytes 58376 | tf_op jit(solution)/shard_map/ppermute | solution.py:48
  18.5 98.6 %copy-start.23 = (pred[32,32]{1,0:T(8,128)(4,1)}, pred[32,32]{1,0:T(8,128)(4,1)S(1)}, u32[]{:S(2)}) copy-start(pred[32,32]{1,0:T(8,128)(4,1)S(1)} %iota_compare_fusion.2) | copy-start | bytes 3076
  18.5 7.3 copy-start.27
  19.3 102.3 %all-to-all-start = ((bf16[32,1,2]{2,1,0:T(2,128)(2,1)}), bf16[32,1,2]{2,1,0:T(2,128)(2,1)S(1)}, u32[]{:S(2)}, u32[]{:S(2)}) async-start(bf16[32,1,2]{2,1,0:T(2,128)(2,1)} %copy.1740), calls=%async_computation | async-start | bytes 32768 | tf_op jit(solution)/shard_map/all_to_all | solution.py:224
  30.4 90.0 %copy-start.34 = (u32[128]{0:T(128)S(1)}, u32[128]{0:T(128)}, u32[]{:S(2)}) copy-start(u32[128]{0:T(128)} %constant.142) | copy-start | bytes 1540
  30.4 92.2 %copy-start.2 = (f32[19,16,256]{2,1,0:T(8,128)S(1)}, f32[19,16,256]{2,1,0:T(8,128)}, u32[]{:S(2)}) copy-start(f32[19,16,256]{2,1,0:T(8,128)} %param.14) | copy-start | bytes 933892
  138.7 6.9 copy-start.3
  142.8 14.9 copy-start.7
  142.9 7.0 copy-start.19
  144.7 14.2 copy-start.24
  144.8 14.2 copy-start.28
  147.2 16.7 %copy-start.18 = (f32[16,256]{1,0:T(8,128)S(1)}, f32[16,256]{1,0:T(8,128)}, u32[]{:S(2)}) copy-start(f32[16,256]{1,0:T(8,128)} %squeeze_stack_reshape.80) | copy-start | bytes 49156
  147.8 24.5 %copy-start.30 = (f32[64]{0:T(128)S(1)}, f32[64]{0:T(128)}, u32[]{:S(2)}) copy-start(f32[64]{0:T(128)} %copy-done.29) | copy-start | bytes 772
  147.8 24.5 %copy-start.31 = (f32[64]{0:T(128)S(1)}, f32[64]{0:T(128)}, u32[]{:S(2)}) copy-start(f32[64]{0:T(128)} %sub.267) | copy-start | bytes 772
  149.8 23.4 %copy-start.20 = (f32[32,2,320]{2,1,0:T(2,128)S(1)}, f32[32,2,320]{2,1,0:T(2,128)}, u32[]{:S(2)}) copy-start(f32[32,2,320]{2,1,0:T(2,128)} %custom-call.6) | copy-start | bytes 245764
  159.8 12.5 all-to-all-start.1
  163.7 1360.7 %all-reduce.5.cloned.1.call-start = ((), (), s32[]{:S(2)}) async-start(), calls=%async_computation.2 | async-start | bytes 3932160
  173.2 149.4 %copy-start.22 = (f32[320]{0:T(512)S(1)}, f32[320]{0:T(512)}, u32[]{:S(2)}) copy-start(f32[320]{0:T(512)} %param.18) | copy-start | bytes 3844
  173.2 149.4 %copy-start.32 = (bf16[3,320]{1,0:T(4,128)(2,1)S(1)}, bf16[3,320]{1,0:T(4,128)(2,1)}, u32[]{:S(2)}) copy-start(bf16[3,320]{1,0:T(4,128)(2,1)} %param.23) | copy-start | bytes 5764
  173.2 149.4 %copy-start.33 = (f32[320]{0:T(512)S(1)}, f32[320]{0:T(512)}, u32[]{:S(2)}) copy-start(f32[320]{0:T(512)} %param.19) | copy-start | bytes 3844
  327.8 6.1 copy-start.4
  329.7 4.3 copy-start.5
  348.4 6.1 copy-start.4
  368.9 6.1 copy-start.4
  389.4 6.1 copy-start.4
  410.0 6.1 copy-start.4
  430.5 6.1 copy-start.4
  451.1 6.1 copy-start.4
  471.6 6.1 copy-start.4
  492.1 6.1 copy-start.4
  512.7 6.1 copy-start.4
  533.2 6.1 copy-start.4
  553.7 6.1 copy-start.4
  574.3 6.1 copy-start.4
  576.2 4.3 copy-start.5
  594.8 6.1 copy-start.4
  596.7 4.3 copy-start.5
  615.4 6.1 copy-start.4
  635.9 6.1 copy-start.4
  656.5 6.1 copy-start.4
  658.3 4.3 copy-start.5
  677.0 6.1 copy-start.4
  697.6 6.1 copy-start.4
  718.1 6.1 copy-start.4
  738.6 6.1 copy-start.4
  759.2 6.1 copy-start.4
  779.7 6.1 copy-start.4
  800.2 6.1 copy-start.4
  820.8 6.1 copy-start.4
  841.3 6.1 copy-start.4
  861.8 6.1 copy-start.4
  882.3 6.1 copy-start.4
  902.9 6.1 copy-start.4
  923.4 6.1 copy-start.4
  943.9 6.1 copy-start.4
  964.5 6.1 copy-start.4
  979.9 4.4 copy-start.16
  979.9 5.0 copy-start.11
  979.9 5.6 copy-start.10
  979.9 556.8 %copy-start.9 = (f32[20,320]{1,0:T(8,128)S(1)}, f32[20,320]{1,0:T(8,128)}, u32[]{:S(2)}) copy-start(f32[20,320]{1,0:T(8,128)} %param.20) | copy-start | bytes 76804
  979.9 556.8 %copy-start.25 = (f32[20,320]{1,0:T(8,128)S(1)}, f32[20,320]{1,0:T(8,128)}, u32[]{:S(2)}) copy-start(f32[20,320]{1,0:T(8,128)} %param.21) | copy-start | bytes 76804
  979.9 556.8 %copy-start.26 = (f32[20,320]{1,0:T(8,128)S(1)}, f32[20,320]{1,0:T(8,128)}, u32[]{:S(2)}) copy-start(f32[20,320]{1,0:T(8,128)} %param.22) | copy-start | bytes 76804
  (100 other events, 276.8 us)
Sparse Core Ops, SparseCore 0:
  981.2 543.0 all-reduce.4
where the time goes:
time: 1560 us; the launch traced here: 1540 us
  waiting for transfers between devices  546 us (35%)
  matrix products  494 us (32%)
  local copies, waits for them, and re-layouts  290 us (19%)
  blocking collectives  97.1 us (6%)
  other arithmetic  77.3 us (5%)
  starting transfers between devices  16.1 us (1%)
  between operations  15.6 us (1%)
    unnamed x2, waiting for transfers between devices  538 us
    dot_general x128, matrix products, one_brick(): mixed = jnp.dot(mixing[layer], current, preferred_element_type=jnp.float32)  195 us
    dot_general x128, matrix products, one_brick(): lax.dot_general(inner, states[layer], (((1,), (1,)), ((), ())), preferred...  132 us
    while x1920, local copies, waits for them, and re-layouts  131 us
    all_gather x1, blocking collectives, body(): lax.all_gather(mix_master.astype(jnp.bfloat16), ('row', 'col'), axis=0, t...  85.5 us
    dot_general x64, matrix products, one_brick(): lax.dot_general(mixing[layer], inner, (((0,), (0,)), ((), ())), preferred...  79.8 us
    add x32, other arithmetic, one_brick(): return (total + jnp.stack(terms), None)  49.1 us
    dynamic_slice x64, local copies, waits for them, and re-layouts, body(): sums = lax.map(lambda single: brick_sums(single, lift_weight), held)  43.1 us
  transfers between devices with their start and end apart: 5, of which 2 were waited for; matrix products, arithmetic and copies ran while one was open for 1% of the time, Pallas kernels for 0%

commit v1 on v0

v1 whole, which is shorter than its diff:
```python
import functools

import jax
import jax.numpy as jnp
from jax import lax
from jax.experimental import pallas as pl
from jax.experimental.pallas import tpu as pltpu
from jax.sharding import PartitionSpec as P

BF = jnp.bfloat16
F4 = jnp.float32
I4 = jnp.int32
C = 320
CELLS = 4096
PIECE = 24
MIB = 1024 * 1024

VELOCITIES = (
    (0, 0, 0),
    (1, 0, 0),
    (-1, 0, 0),
    (0, 1, 0),
    (0, -1, 0),
    (0, 0, 1),
    (0, 0, -1),
    (1, 1, 0),
    (-1, -1, 0),
    (1, -1, 0),
    (-1, 1, 0),
    (1, 0, 1),
    (-1, 0, -1),
    (1, 0, -1),
    (-1, 0, 1),
    (0, 1, 1),
    (0, -1, -1),
    (0, 1, -1),
    (0, -1, 1),
)
LATTICE_WEIGHTS = (1.0 / 3.0,) + (1.0 / 18.0,) * 6 + (1.0 / 36.0,) * 12

TAIL_P = 0.3275911 * 0.7071067811865476
TAIL_A = (
    0.5 * 0.254829592,
    0.5 * -0.284496736,
    0.5 * 1.421413741,
    0.5 * -1.453152027,
    0.5 * 1.061405429,
)
EXP_SCALE = -0.5 * 1.4426950408889634


def iota(shape, dim):
    return lax.broadcasted_iota(I4, shape, dim)


def gelu_parts(z):
    size = jnp.abs(z)
    t = pl.reciprocal(1.0 + TAIL_P * size, approx=True)
    bell = jnp.exp2(z * z * EXP_SCALE)
    poly = (((TAIL_A[4] * t + TAIL_A[3]) * t + TAIL_A[2]) * t + TAIL_A[1]) * t + TAIL_A[0]
    return size, bell, poly * t * bell


def gelu_value(z):
    size, bell, tail = gelu_parts(z)
    return jnp.maximum(z, 0.0) - size * tail


def gelu_both(z):
    size, bell, tail = gelu_parts(z)
    value = jnp.maximum(z, 0.0) - size * tail
    below = tail - (size * 0.3989422804014327) * bell
    return value, jnp.where(z >= 0.0, 1.0 - below, below)


def moments(read):
    density = read[0]
    moment = [None, None, None]
    for index in range(1, 19):
        density = density + read[index]
        for axis in range(3):
            along = VELOCITIES[index][axis]
            if along:
                term = read[index] if along > 0 else -read[index]
                moment[axis] = term if moment[axis] is None else moment[axis] + term
    return density, [moment[axis] / density for axis in range(3)]


def brick_rows(fields):
    stacked = jnp.concatenate(fields, axis=0).astype(BF)
    lane = iota((256, 256), 1)
    source = (lane & 0xC0) | (((lane >> 3) & 3) << 4) | (((lane >> 5) & 1) << 3) | (lane & 7)
    lanes = (iota((256, 256), 0) == source).astype(F4).astype(BF)
    row = iota((128, 96), 0)
    wanted = ((row >> 2) & 7) * 16 + (row & 3) * 4 + (row >> 5)
    rows = (iota((128, 96), 1) == wanted).astype(F4).astype(BF)
    moved = jnp.dot(stacked, lanes, preferred_element_type=F4).astype(BF)
    moved = jnp.dot(rows, moved, preferred_element_type=F4)
    part = iota((32, 128), 1) >> 5
    flag = (iota((32, 128), 0) >> 2) == 6
    groups = []
    for group in range(8):
        tile, place = group // 4, group % 4
        total = None
        for low in range(4):
            piece = moved[low * 32 : (low + 1) * 32, tile * 128 : (tile + 1) * 128]
            turn = (low - place) * 32 % 128
            if turn:
                piece = pltpu.roll(piece, turn, 1)
            total = piece if total is None else jnp.where(part == low, piece, total)
        groups.append(jnp.where(flag, 1.0, total))
    return jnp.concatenate(groups, axis=0).astype(BF)


def route_rows(targets):
    across = jnp.broadcast_to(targets, (32, 32)).astype(F4)
    first, second = iota((32, 32), 0), iota((32, 32), 1)
    down = jnp.sum(jnp.where(first == second, across, 0.0), axis=1, keepdims=True)
    earlier = (down == across) & (first < second)
    rank = jnp.sum(jnp.where(earlier, 1.0, 0.0), axis=0, keepdims=True)
    code = (2.0 * across[0:16] + rank).astype(BF)
    lane = iota((32, 256), 1)
    spread = (iota((32, 256), 0) == 8 * (lane & 3) + (lane >> 5)).astype(F4).astype(BF)
    code = jnp.dot(code, spread, preferred_element_type=F4)[0:1].astype(I4)
    key = code * 8 + ((iota((1, 256), 1) >> 2) & 7)
    return (iota((512, 256), 0) == key).astype(F4).astype(BF)


def lattice_kernel(pop_ref, before_ref, behind_ref, relax_ref, lists_ref, after_ref, out_ref):
    row = iota((16, 256), 0)
    depth = iota((16, 256), 1) & 15
    read = []
    for index in range(19):
        along_x, along_y, along_z = VELOCITIES[index]
        plane = pop_ref[index]
        if along_x > 0:
            plane = jnp.where(row == 0, before_ref[index - 1 : index], pltpu.roll(plane, 1, 0))
        elif along_x < 0:
            plane = jnp.where(row == 15, behind_ref[index - 1 : index], pltpu.roll(plane, 15, 0))
        if along_y:
            plane = pltpu.roll(plane, along_y * 16 % 256, 1)
        if along_z > 0:
            plane = jnp.where(depth == 0, pltpu.roll(plane, 241, 1), pltpu.roll(plane, 1, 1))
        elif along_z < 0:
            plane = jnp.where(depth == 15, pltpu.roll(plane, 15, 1), pltpu.roll(plane, 255, 1))
        read.append(plane)
    density, flow = moments(read)
    speed = flow[0] * flow[0] + flow[1] * flow[1] + flow[2] * flow[2]
    relaxation = relax_ref[...]
    for index in range(19):
        project = None
        for axis in range(3):
            along = VELOCITIES[index][axis]
            if along:
                term = flow[axis] if along > 0 else -flow[axis]
                project = term if project is None else project + term
        if project is None:
            shape = 1.0 - 1.5 * speed
        else:
            shape = 1.0 + 3.0 * project + 4.5 * project * project - 1.5 * speed
        balance = LATTICE_WEIGHTS[index] * density * shape
        after_ref[index] = read[index] - relaxation * (read[index] - balance)
    unused, old_flow = moments([pop_ref[index] for index in range(19)])
    bricks = brick_rows(old_flow + flow)
    select = route_rows(lists_ref[...])
    out_ref[...] = jnp.dot(select, bricks, preferred_element_type=F4).astype(BF)


def lattice(populations, before, behind, relaxation, lists):
    return pl.pallas_call(
        lattice_kernel,
        out_shape=(
            jax.ShapeDtypeStruct((19, 16, 256), F4),
            jax.ShapeDtypeStruct((512, 128), BF),
        ),
        name="lattice",
        compiler_params=pltpu.CompilerParams(vmem_limit_bytes=24 * MIB),
    )(populations, before, behind, relaxation, lists)


def lift_kernel(arrived_ref, lift_ref, gain_ref, shift_ref, h_ref, target_ref, taps, lifted):
    arrived = arrived_ref[...]
    flags = (iota((32, 512), 1) == iota((32, 512), 0) * 16 + 6).astype(F4).astype(BF)
    flags = jnp.dot(flags, arrived, preferred_element_type=F4).astype(BF)
    source = iota((32, 512), 1) >> 4
    ahead = (iota((32, 512), 0) < source).astype(F4).astype(BF)
    same = (iota((32, 512), 0) == source).astype(F4).astype(BF)
    dims = (((0,), (0,)), ((), ()))
    place = lax.dot_general(flags, ahead, dims, preferred_element_type=F4)[0:1].astype(I4)
    live = lax.dot_general(flags, same, dims, preferred_element_type=F4)[0:1]
    lane = iota((1, 512), 1)
    key = jnp.where(live > 0.5, place * 16 + (lane & 15), -1)
    pick = (iota((256, 512), 0) == key).astype(F4).astype(BF)
    held = jnp.dot(pick, arrived, preferred_element_type=F4)
    for brick in range(32):
        target_ref[0:8, brick * 128 : (brick + 1) * 128] = held[brick * 8 : (brick + 1) * 8]
    target_ref[8:16, :] = jnp.zeros((8, CELLS), F4)
    cell = iota((8, 128), 1)
    cell_x, cell_y, cell_z = cell >> 5, (cell >> 3) & 3, cell & 7
    shifts = [(x, y, z) for x in (-1, 0, 1) for y in (-1, 0, 1) for z in (-1, 0, 1)]
    masks = []
    for x, y, z in shifts:
        inside = (cell_x + x >= 0) & (cell_x + x < 4) & (cell_y + y >= 0) & (cell_y + y < 4)
        masks.append(inside & (cell_z + z >= 0) & (cell_z + z < 8))
    for pair in range(14):
        for brick in range(32):
            own = held[brick * 8 : (brick + 1) * 8]
            halves = []
            for tap in (2 * pair, 2 * pair + 1):
                if tap == 27:
                    halves.append(jnp.zeros((8, 128), F4))
                    continue
                x, y, z = shifts[tap]
                turn = -(x * 32 + y * 8 + z) % 128
                moved = pltpu.roll(own, turn, 1) if turn else own
                halves.append(jnp.where(masks[tap], moved, 0.0))
            taps[pair * 16 : (pair + 1) * 16, brick * 128 : (brick + 1) * 128] = jnp.concatenate(
                halves, axis=0
            ).astype(BF)
    column = iota((81, 224), 1)
    feature = (column & 7) * 27 + (column >> 3)
    valid = ((column & 7) < 3) & (column < 216)
    spread = jnp.where(valid & (iota((81, 224), 0) == feature), 1.0, 0.0).astype(BF)
    weight = jnp.dot(lift_ref[...], spread, preferred_element_type=F4).astype(BF)
    for start in range(0, CELLS, 512):
        part = slice(start, start + 512)
        lifted[:, part] = jnp.dot(weight, taps[:, part], preferred_element_type=F4)

    @pl.loop(0, C // 16)
    def _(block):
        rows = pl.ds(pl.multiple_of(block * 16, 16), 16)
        total = jnp.zeros((16, 128), F4)
        square = jnp.zeros((16, 128), F4)
        for start in range(0, CELLS, 128):
            value = lifted[rows, start : start + 128]
            total = total + value
            square = square + value * value
        mean = jnp.sum(total, axis=1, keepdims=True) / CELLS
        spread = jnp.sum(square, axis=1, keepdims=True) / CELLS - mean * mean
        scale = lax.rsqrt(spread + 1e-05) * gain_ref[rows, :]
        shift = shift_ref[rows, :]
        for start in range(0, CELLS, 256):
            part = slice(start, start + 256)
            normed = (lifted[rows, part] - mean) * scale + shift
            h_ref[rows, part] = gelu_value(normed).astype(BF)


def lift(arrived, lift_weight, gain, shift):
    return pl.pallas_call(
        lift_kernel,
        out_shape=(
            jax.ShapeDtypeStruct((C, CELLS), BF),
            jax.ShapeDtypeStruct((16, CELLS), F4),
        ),
        scratch_shapes=[pltpu.VMEM((224, CELLS), BF), pltpu.VMEM((C, CELLS), F4)],
        name="lift",
        compiler_params=pltpu.CompilerParams(vmem_limit_bytes=40 * MIB),
    )(arrived, lift_weight, gain, shift)


def train_kernel(
    steps,
    layers,
    col_ref,
    h_ref,
    target_ref,
    mix_ref,
    out_ref,
    send_ref,
    keep_ref,
    mix_back,
    states,
    slopes,
    ahead,
    back,
    inner,
    total,
):
    step = pl.program_id(0)
    cells = h_ref.shape[1]
    parts = [slice(start, start + 256) for start in range(0, cells, 256)]

    @pl.when(step == 0)
    def _():
        total[...] = jnp.zeros_like(total)
        same = (iota((C, C), 0) == iota((C, C), 1)).astype(F4).astype(BF)
        for layer in range(1, layers):
            rows = slice(layer * C, (layer + 1) * C)
            mix_back[rows, :] = lax.dot_general(
                mix_ref[rows, :], same, (((0,), (0,)), ((), ())), preferred_element_type=F4
            ).astype(BF)

    def state(layer):
        return h_ref if layer == 0 else states.at[layer - 1]

    for layer in range(layers):
        for part in parts:
            ahead[:, part] = jnp.dot(
                mix_ref[layer * C : (layer + 1) * C, :],
                state(layer)[:, part],
                preferred_element_type=F4,
            )
        for part in parts:
            for start in range(0, C, 16):
                rows = slice(start, start + 16)
                value, slope = gelu_both(ahead[rows, part])
                slopes[layer, rows, part] = slope
                states[layer, rows, part] = (state(layer)[rows, part].astype(F4) + value).astype(BF)
    for part in parts:
        output = jnp.dot(out_ref[...], states[layers - 1, :, part], preferred_element_type=F4)
        delta = ((output - target_ref[:, part]) * (2.0 / 384.0)).astype(BF)
        back[:, part] = lax.dot_general(
            out_ref[...], delta, (((0,), (0,)), ((), ())), preferred_element_type=F4
        )
    for layer in range(layers - 1, -1, -1):
        rows_of = slice(layer * C, (layer + 1) * C)
        for part in parts:
            for start in range(0, C, 16):
                rows = slice(start, start + 16)
                inner[layer, rows, part] = (back[rows, part] * slopes[layer, rows, part]).astype(BF)
        if layer > 0:
            for part in parts:
                back[:, part] += jnp.dot(
                    mix_back[rows_of, :], inner[layer, :, part], preferred_element_type=F4
                )
        total[rows_of, :] += lax.dot_general(
            inner[layer], state(layer)[...], (((1,), (1,)), ((), ())), preferred_element_type=F4
        )

    @pl.when(step == steps - 1)
    def _():
        col = col_ref[0]
        for piece in range(32):
            own = pl.multiple_of(piece * 40 + 16 * col, 8)
            other = pl.multiple_of(piece * 40 + 16 * (1 - col), 8)
            rows = slice(piece * PIECE, (piece + 1) * PIECE)
            keep_ref[rows, :] = total[pl.ds(own, PIECE), :]
            send_ref[rows, :] = total[pl.ds(other, PIECE), :]


def train(col, h, target, mixing, out_weight):
    cells = 1024
    steps = CELLS // cells
    layers = mixing.shape[0] // C
    return pl.pallas_call(
        functools.partial(train_kernel, steps, layers),
        grid=(steps,),
        in_specs=[
            pl.BlockSpec(memory_space=pltpu.SMEM),
            pl.BlockSpec((C, cells), lambda i: (0, i)),
            pl.BlockSpec((16, cells), lambda i: (0, i)),
            pl.BlockSpec((layers * C, C), lambda i: (0, 0)),
            pl.BlockSpec((16, C), lambda i: (0, 0)),
        ],
        out_specs=(
            pl.BlockSpec((32 * PIECE, C), lambda i: (0, 0)),
            pl.BlockSpec((32 * PIECE, C), lambda i: (0, 0)),
        ),
        out_shape=(
            jax.ShapeDtypeStruct((32 * PIECE, C), F4),
            jax.ShapeDtypeStruct((32 * PIECE, C), F4),
        ),
        scratch_shapes=[
            pltpu.VMEM((layers * C, C), BF),
            pltpu.VMEM((layers, C, cells), BF),
            pltpu.VMEM((layers, C, cells), F4),
            pltpu.VMEM((C, cells), F4),
            pltpu.VMEM((C, cells), F4),
            pltpu.VMEM((layers, C, cells), BF),
            pltpu.VMEM((layers * C, C), F4),
        ],
        name="train",
        compiler_params=pltpu.CompilerParams(vmem_limit_bytes=48 * MIB),
    )(col, h, target, mixing, out_weight)


def adamw(master, gradient, first, second):
    first_next = 0.9 * first + 0.1 * gradient
    second_next = 0.999 * second + 0.001 * gradient * gradient
    ratio = first_next / (1.0 - 0.9**10) / (jnp.sqrt(second_next / (1.0 - 0.999**10)) + 1e-08)
    return (master - 0.01 * (ratio + 0.1 * master), first_next, second_next)


def body(
    populations,
    relaxation,
    send_lists,
    lift_weight,
    norm_gain,
    norm_shift,
    mix_master,
    mix_first,
    mix_second,
    out_weight,
):
    every = ("sec", "row", "col")
    size = lax.axis_size(every)
    swap = [(0, 1), (1, 0)]
    col = lax.axis_index("col")
    up = [(i, (i + 1) % size) for i in range(size)]
    before = lax.ppermute(populations[1:15, 15], every, up)
    behind = lax.ppermute(populations[1:15, 0], every, [(j, i) for i, j in up])
    shard = jnp.broadcast_to(mix_master.astype(BF), (32, 20, C))
    mine = lax.all_to_all(shard, "row", split_axis=0, concat_axis=0, tiled=True)
    other = lax.ppermute(mine, "col", swap)
    pair = [jnp.where(col == 0, mine, other), jnp.where(col == 0, other, mine)]
    mixing = jnp.stack(pair, axis=1).reshape(64 * 20, C)
    after, outgoing = lattice(populations, before, behind, relaxation, send_lists)
    arrived = lax.all_to_all(
        outgoing.reshape(32, 16, 128), "row", split_axis=0, concat_axis=0, tiled=True
    ).reshape(512, 128)
    h, target = lift(arrived, lift_weight, norm_gain[:, None], norm_shift[:, None])
    out_rows = jnp.pad(out_weight, ((3, 10), (0, 0)))
    send, keep = train(col.astype(I4)[None], h, target, mixing, out_rows)
    half = keep + lax.ppermute(send, "col", swap)
    terms = lax.all_to_all(
        half.reshape(32, PIECE, C), "row", split_axis=0, concat_axis=0, tiled=True
    )
    summed = jnp.sum(terms, axis=0)
    summed = jnp.where(col == 0, summed[0:20], summed[4:24])
    gradient = summed + lax.ppermute(summed, "sec", swap)
    new_master, new_first, new_second = adamw(mix_master, gradient, mix_first, mix_second)
    return (after, new_master, new_first, new_second)


def solution(mesh):
    in_specs = (
        P(None, ("sec", "row", "col"), None),
        P(("sec", "row", "col"), None),
        P(("sec", "row", "col"), None),
        P(),
        P(),
        P(),
        P(("row", "col"), None),
        P(("row", "col"), None),
        P(("row", "col"), None),
        P(),
    )
    out_specs = (
        P(None, ("sec", "row", "col"), None),
        P(("row", "col"), None),
        P(("row", "col"), None),
        P(("row", "col"), None),
    )
    return jax.shard_map(body, mesh=mesh, in_specs=in_specs, out_specs=out_specs, check_vma=False)
```

time: 1560 us -> 129 us (0.08)
  waiting for transfers between devices: 546 us -> 14.4 us
  matrix products: 494 us -> 0 us
  local copies, waits for them, and re-layouts: 290 us -> 4.98 us
  other arithmetic: 77.3 us -> 2.15 us
  blocking collectives: 97.1 us -> 44.6 us
  Pallas kernels: 0 us -> 44.2 us
    unnamed x2 -> x0, waiting for transfers between devices: 538 us -> none
    dot_general x418 -> x0, matrix products: 494 us -> none  [the longest x128 195 us: one_brick(): mixed = jnp.dot(mixing[layer], current, preferred_element_type=jnp.float32)]
    while x1920 -> x0, local copies, waits for them, and re-layouts: 131 us -> none
    all_gather x1 -> x0, blocking collectives: 85.5 us -> none  [body(): lax.all_gather(mix_master.astype(jnp.bfloat16), ('row', 'col'), axis=0, t...]
    dynamic_slice x96 -> x0, local copies, waits for them, and re-layouts: 67.2 us -> none  [the longest x64 43.1 us: body(): sums = lax.map(lambda single: brick_sums(single, lift_weight), held)]
    another operation x312 -> x1, local copies, waits for them, and re-layouts: 59.8 us -> 0.12 us  [body(): mixing = jnp.stack(pair, axis=1).reshape(64 * 20, C)]
    add x32 -> x1, other arithmetic: 49.1 us -> 0.12 us  [body(): half = keep + lax.ppermute(send, 'col', swap)]
    all_to_all x0 -> x2, blocking collectives: none -> 44.6 us  [the longest x1 23.2 us: body(): lax.all_to_all(half.reshape(32, PIECE, C), 'row', split_axis=0, concat_ax...]
  transfers between devices with their start and end apart: 5 -> 6, of which waited for: 2 -> 4; matrix products, arithmetic and copies ran while one was open for 1% -> 0% of each run, Pallas kernels for 0% -> 9%
where the time goes in v1:
time: 129 us; the launch traced here: 128 us
  blocking collectives  44.6 us (35%)
  Pallas kernels  44.2 us (34%)
  starting transfers between devices  16.9 us (13%)
  waiting for transfers between devices  14.4 us (11%)
  local copies, waits for them, and re-layouts  4.98 us (4%)
  other arithmetic  2.15 us (2%)
    pallas_call x1, Pallas kernels, train(): pl.pallas_call(functools.partial(train_kernel, steps, layers), grid=(step...  33 us
    all_to_all x1, blocking collectives, body(): lax.all_to_all(half.reshape(32, PIECE, C), 'row', split_axis=0, concat_ax...  23.2 us
    all_to_all x1, blocking collectives, body(): mine = lax.all_to_all(shard, 'row', split_axis=0, concat_axis=0, tiled=True)  21.4 us
    pallas_call x1, Pallas kernels, lift(): pl.pallas_call(lift_kernel, out_shape=(jax.ShapeDtypeStruct((C, CELLS), B...  9.59 us
    all_to_all x1, waiting for transfers between devices, body(): lax.all_to_all(outgoing.reshape(32, 16, 128), 'row', split_axis=0, concat...  8.19 us
    ppermute x1, starting transfers between devices, body(): behind = lax.ppermute(populations[1:15, 0], every, [(j, i) for i, j in up])  6.69 us
    all_to_all x1, starting transfers between devices, body(): lax.all_to_all(outgoing.reshape(32, 16, 128), 'row', split_axis=0, concat...  4.03 us
    ppermute x1, starting transfers between devices, body(): gradient = summed + lax.ppermute(summed, 'sec', swap)  3.12 us
  transfers between devices with their start and end apart: 6, of which 4 were waited for; matrix products, arithmetic and copies ran while one was open for 0% of the time, Pallas kernels for 9%

profile of v1, /device:TPU:0, one launch (start us, length us, event | category | flops | bytes accessed | tf_op | source)
XLA Modules:
  0.0 128.1 jit_solution(4835901072892952799)
XLA Ops:
  0.6 0.8 convert_element_type.5
  1.4 0.1 broadcast_in_dim.15
  1.5 0.0 copy-start.1
  1.5 0.0 copy-start.4
  1.5 0.0 copy-start.5
  1.5 21.4 %all_to_all.15 = bf16[32,20,320]{2,1,0:T(8,128)(2,1)S(1)} all-to-all(bf16[32,20,320]{2,1,0:T(8,128)(2,1)S(1)} %broadcast_in_dim.15), channel_id=1, replica_groups=mesh['sec'=2,'row'=32,'col'=2] {'row'}, dimensions={0} | all-to-all | bytes 819200 | tf_op jit(solution)/shard_map/all_to_all | solution.py:404
  22.9 0.0 copy-start.7
  22.9 0.0 copy-start.11
  22.9 0.0 copy-start.12
  22.9 0.0 copy-start.10
  22.9 0.1 copy.37
  23.0 0.1 collective-permute-start.2
  23.1 0.0 copy-done.1
  23.1 0.6 collective-permute-start
  23.7 6.7 %collective-permute-start.1 = (f32[14,256]{1,0:T(8,128)S(1)}, f32[14,256]{1,0:T(8,128)S(1)}, u32[]{:S(2)}, u32[]{:S(2)}) collective-permute-start(f32[14,256]{1,0:T(8,128)S(1)} %bitcast.17), channel_id=1, source_target_pairs={{1,0},{2,1},{3,2},{4,3},{5,4},{6,5},{7,6},{8,7},{9,8},{10,9},{11,1... | collective-permute-start | bytes 43016 | tf_op jit(solution)/shard_map/ppermute | solution.py:402
  30.4 1.4 %collective-permute-done.before_ref = f32[14,256]{1,0:T(8,128)S(1)} collective-permute-done((f32[14,256]{1,0:T(8,128)S(1)}, f32[14,256]{1,0:T(8,128)S(1)}, u32[]{:S(2)}, u32[]{:S(2)}) %collective-permute-start) | collective-permute-done | bytes 14368 | tf_op jit(solution)/shard_map/ppermute | solution.py:401
  31.8 0.0 collective-permute-done.1.behind_ref
  31.8 0.0 copy-done.4
  31.8 0.0 copy-done.5
  31.8 1.6 %lattice.1 = (f32[19,16,256]{2,1,0:T(8,128)}, bf16[512,128]{1,0:T(8,128)(2,1)}) custom-call(f32[19,16,256]{2,1,0:T(8,128)S(1)} %copy-done.1, f32[14,256]{1,0:T(8,128)S(1)} %collective-permute-done.before_ref, f32[14,256]{1,0:T(8,128)S(1)} %collective-permute-done.1.behind_ref, f32[16,256]{1,0:T(8,128)S(1)} %copy-done.4, s32[1,32]{1,0:T(1,128)S(1)} %copy-done.5), custom_call_target="tpu_custom_call" | custom-call | tf_op jit(solution)/shard_map/lattice/pallas_call | solution.py:170
  33.4 4.0 %all-to-all-start = ((bf16[32,16,128]{2,1,0:T(8,128)(2,1)}), bf16[32,16,128]{2,1,0:T(8,128)(2,1)S(1)}, u32[]{:S(2)}, u32[]{:S(2)}) async-start(bf16[32,16,128]{2,1,0:T(8,128)(2,1)} %bitcast.3), calls=%async_computation | async-start | bytes 262144 | tf_op jit(solution)/shard_map/all_to_all | solution.py:409
  37.5 0.0 copy-done.7
  37.5 0.1 copy.34.lift_ref
  37.6 0.0 copy-done.11
  37.6 0.1 broadcast_in_dim.16.gain_ref
  37.7 0.0 copy-done.12
  37.7 0.1 broadcast_in_dim.17.shift_ref
  37.8 0.0 copy-done.10
  37.9 8.2 %all-to-all-done = bf16[32,16,128]{2,1,0:T(8,128)(2,1)S(1)} async-done(((bf16[32,16,128]{2,1,0:T(8,128)(2,1)}), bf16[32,16,128]{2,1,0:T(8,128)(2,1)S(1)}, u32[]{:S(2)}, u32[]{:S(2)}) %all-to-all-start) | async-done | bytes 131104 | tf_op jit(solution)/shard_map/all_to_all | solution.py:409
  46.0 9.6 %lift.1 = (bf16[320,4096]{1,0:T(8,128)(2,1)S(1)}, f32[16,4096]{1,0:T(8,128)S(1)}) custom-call(bf16[512,128]{1,0:T(8,128)(2,1)S(1)} %bitcast.14, bf16[320,81]{1,0:T(8,128)(2,1)S(1)} %copy.34.lift_ref, f32[320,1]{1,0:T(8,128)S(1)} %broadcast_in_dim.16.gain_ref, f32[320,1]{1,0:T(8,128)S(1)} %broadcast_in_dim.17.shift_ref), custom_call_target="tpu_custom_call" | custom-call | tf_op jit(solution)/shard_map/lift/pallas_call | solution.py:249
  55.6 0.0 copy-start
  55.6 0.0 copy-start.2
  55.7 0.0 collective-permute-done.2
  55.7 0.2 select_bitcast_fusion.1
  55.9 0.3 pad_maximum_fusion
  56.2 1.0 copy-done
  57.1 0.1 copy-done.2
  57.2 0.1 copy.40
  57.3 0.4 reshape.22.mix_ref
  57.8 0.0 copy-start.3
  57.8 0.9 copy-done.3
  58.7 33.0 %train.1 = (f32[768,320]{1,0:T(8,128)S(1)}, f32[768,320]{1,0:T(8,128)S(1)}) custom-call(s32[1]{0:T(128)} %bitcast.2.col_ref, bf16[320,4096]{1,0:T(8,128)(2,1)} %copy-done, f32[16,4096]{1,0:T(8,128)S(1)} %copy-done.3, bf16[1280,320]{1,0:T(8,128)(2,1)S(1)} %reshape.22.mix_ref, bf16[16,320]{1,0:T(8,128)(2,1)S(1)} %pad.4.out_ref), custom_call_target="tpu_custom_call" | custom-call | tf_op jit(solution)/shard_map/train/pallas_call | solution.py:345
  91.8 0.3 copy.41
  92.1 2.4 %collective-permute-start.3 = (f32[768,320]{0,1:T(8,128)S(1)}, f32[768,320]{0,1:T(8,128)}, u32[]{:S(2)}, u32[]{:S(2)}) collective-permute-start(f32[768,320]{0,1:T(8,128)S(1)} %copy.41), channel_id=1, source_target_pairs={{0,1},{1,0},{2,3},{3,2},{4,5},{5,4},{6,7},{7,6},{8,9},{9,8},{10,11... | collective-permute-start | bytes 2949128 | tf_op jit(solution)/shard_map/ppermute | solution.py:415
  94.5 2.3 %collective-permute-done.3 = f32[768,320]{0,1:T(8,128)} collective-permute-done((f32[768,320]{0,1:T(8,128)S(1)}, f32[768,320]{0,1:T(8,128)}, u32[]{:S(2)}, u32[]{:S(2)}) %collective-permute-start.3) | collective-permute-done | bytes 983072 | tf_op jit(solution)/shard_map/ppermute | solution.py:415
  96.8 1.6 %copy.42 = f32[768,320]{1,0:T(8,128)S(1)} copy(f32[768,320]{0,1:T(8,128)} %collective-permute-done.3) | data formatting | bytes 1966080 | tf_op jit(solution)/shard_map/ppermute | solution.py:415
  98.4 0.1 add.23
  98.5 23.2 %all_to_all.16 = f32[32,24,320]{2,1,0:T(8,128)S(1)} all-to-all(f32[32,24,320]{2,1,0:T(8,128)S(1)} %bitcast.15), channel_id=1, replica_groups=mesh['sec'=2,'row'=32,'col'=2] {'row'}, dimensions={0} | all-to-all | bytes 1966080 | tf_op jit(solution)/shard_map/all_to_all | solution.py:416
  121.8 0.0 copy-start.6
  121.8 0.0 copy-start.8
  121.8 0.0 copy-start.9
  121.8 0.1 reduce_sum.9
  121.9 3.1 %collective-permute-start.4 = (f32[20,320]{1,0:T(8,128)S(1)}, f32[20,320]{1,0:T(8,128)S(1)}, u32[]{:S(2)}, u32[]{:S(2)}) collective-permute-start(f32[20,320]{1,0:T(8,128)S(1)} %slice_select_fusion), channel_id=1, source_target_pairs={{0,64},{64,0},{1,65},{65,1},{2,66},{66,2},{3,67},{67,3},{4,68},{68... | collective-permute-start | bytes 76808 | tf_op jit(solution)/shard_map/ppermute | solution.py:421
  125.0 2.4 %collective-permute-done.4 = f32[20,320]{1,0:T(8,128)S(1)} collective-permute-done((f32[20,320]{1,0:T(8,128)S(1)}, f32[20,320]{1,0:T(8,128)S(1)}, u32[]{:S(2)}, u32[]{:S(2)}) %collective-permute-start.4) | collective-permute-done | bytes 25632 | tf_op jit(solution)/shard_map/ppermute | solution.py:421
  127.4 0.0 copy-done.6
  127.4 0.0 copy-done.8
  127.4 0.0 copy-done.9
  127.4 0.7 multiply_subtract_fusion
  (5 shorter events, 0.0 us)
Async XLA Ops:
  1.5 21.6 %copy-start.1 = (f32[19,16,256]{2,1,0:T(8,128)S(1)}, f32[19,16,256]{2,1,0:T(8,128)}, u32[]{:S(2)}) copy-start(f32[19,16,256]{2,1,0:T(8,128)} %pop_ref.1) | copy-start | bytes 933892
  1.5 30.4 %copy-start.4 = (f32[16,256]{1,0:T(8,128)S(1)}, f32[16,256]{1,0:T(8,128)}, u32[]{:S(2)}) copy-start(f32[16,256]{1,0:T(8,128)} %relax_ref.1) | copy-start | bytes 49156
  1.5 30.3 %copy-start.5 = (s32[1,32]{1,0:T(1,128)S(1)}, s32[1,32]{1,0:T(1,128)}, u32[]{:S(2)}) copy-start(s32[1,32]{1,0:T(1,128)} %lists_ref.1) | copy-start | bytes 388
  22.9 14.5 %copy-start.7 = (bf16[320,81]{0,1:T(8,128)(2,1)S(1)}, bf16[320,81]{0,1:T(8,128)(2,1)}, u32[]{:S(2)}) copy-start(bf16[320,81]{0,1:T(8,128)(2,1)} %param.13) | copy-start | bytes 155524
  22.9 14.7 %copy-start.11 = (f32[320]{0:T(512)S(1)}, f32[320]{0:T(512)}, u32[]{:S(2)}) copy-start(f32[320]{0:T(512)} %param.14) | copy-start | bytes 3844
  22.9 14.8 %copy-start.12 = (f32[320]{0:T(512)S(1)}, f32[320]{0:T(512)}, u32[]{:S(2)}) copy-start(f32[320]{0:T(512)} %param.15) | copy-start | bytes 3844
  22.9 14.9 %copy-start.10 = (bf16[3,320]{1,0:T(4,128)(2,1)S(1)}, bf16[3,320]{1,0:T(4,128)(2,1)}, u32[]{:S(2)}) copy-start(bf16[3,320]{1,0:T(4,128)(2,1)} %param.19) | copy-start | bytes 5764
  23.0 32.7 %collective-permute-start.2 = (bf16[32,20,320]{2,0,1:T(8,128)(2,1)S(1)}, bf16[32,20,320]{2,0,1:T(8,128)(2,1)S(1)}, u32[]{:S(2)}, u32[]{:S(2)}) collective-permute-start(bf16[32,20,320]{2,0,1:T(8,128)(2,1)S(1)} %copy.37), channel_id=1, source_target_pairs={{0,1},{1,0},{2,3},{3,2},{4,5},{5,4},{6,7},{7,6},{8,9},{9,8},{10,11... | collective-permute-start | bytes 1228808 | tf_op jit(solution)/shard_map/ppermute | solution.py:405
  23.1 8.7 %collective-permute-start = (f32[14,256]{1,0:T(8,128)S(1)}, f32[14,256]{1,0:T(8,128)S(1)}, u32[]{:S(2)}, u32[]{:S(2)}) collective-permute-start(f32[14,256]{1,0:T(8,128)S(1)} %bitcast.16), channel_id=1, source_target_pairs={{0,1},{1,2},{2,3},{3,4},{4,5},{5,6},{6,7},{7,8},{8,9},{9,10},{10,1... | collective-permute-start | bytes 43016 | tf_op jit(solution)/shard_map/ppermute | solution.py:401
  23.7 8.1 %collective-permute-start.1 = (f32[14,256]{1,0:T(8,128)S(1)}, f32[14,256]{1,0:T(8,128)S(1)}, u32[]{:S(2)}, u32[]{:S(2)}) collective-permute-start(f32[14,256]{1,0:T(8,128)S(1)} %bitcast.17), channel_id=1, source_target_pairs={{1,0},{2,1},{3,2},{4,3},{5,4},{6,5},{7,6},{8,7},{9,8},{10,9},{11,1... | collective-permute-start | bytes 43016 | tf_op jit(solution)/shard_map/ppermute | solution.py:402
  33.4 12.6 %all-to-all-start = ((bf16[32,16,128]{2,1,0:T(8,128)(2,1)}), bf16[32,16,128]{2,1,0:T(8,128)(2,1)S(1)}, u32[]{:S(2)}, u32[]{:S(2)}) async-start(bf16[32,16,128]{2,1,0:T(8,128)(2,1)} %bitcast.3), calls=%async_computation | async-start | bytes 262144 | tf_op jit(solution)/shard_map/all_to_all | solution.py:409
  55.6 1.5 %copy-start = (bf16[320,4096]{1,0:T(8,128)(2,1)}, bf16[320,4096]{1,0:T(8,128)(2,1)S(1)}, u32[]{:S(2)}) copy-start(bf16[320,4096]{1,0:T(8,128)(2,1)S(1)} %get-tuple-element.12.h_ref) | copy-start | bytes 7864324
  55.6 1.6 %copy-start.2 = (f32[16,4096]{1,0:T(8,128)}, f32[16,4096]{1,0:T(8,128)S(1)}, u32[]{:S(2)}) copy-start(f32[16,4096]{1,0:T(8,128)S(1)} %get-tuple-element.13.target_ref) | copy-start | bytes 786436
  57.8 1.0 copy-start.3
  92.1 4.7 %collective-permute-start.3 = (f32[768,320]{0,1:T(8,128)S(1)}, f32[768,320]{0,1:T(8,128)}, u32[]{:S(2)}, u32[]{:S(2)}) collective-permute-start(f32[768,320]{0,1:T(8,128)S(1)} %copy.41), channel_id=1, source_target_pairs={{0,1},{1,0},{2,3},{3,2},{4,5},{5,4},{6,7},{7,6},{8,9},{9,8},{10,11... | collective-permute-start | bytes 2949128 | tf_op jit(solution)/shard_map/ppermute | solution.py:415
  121.8 5.7 %copy-start.6 = (f32[20,320]{1,0:T(8,128)S(1)}, f32[20,320]{1,0:T(8,128)}, u32[]{:S(2)}) copy-start(f32[20,320]{1,0:T(8,128)} %param.16) | copy-start | bytes 76804
  121.8 5.7 %copy-start.8 = (f32[20,320]{1,0:T(8,128)S(1)}, f32[20,320]{1,0:T(8,128)}, u32[]{:S(2)}) copy-start(f32[20,320]{1,0:T(8,128)} %param.17) | copy-start | bytes 76804
  121.8 5.7 %copy-start.9 = (f32[20,320]{1,0:T(8,128)S(1)}, f32[20,320]{1,0:T(8,128)}, u32[]{:S(2)}) copy-start(f32[20,320]{1,0:T(8,128)} %param.18) | copy-start | bytes 76804
  121.9 5.5 %collective-permute-start.4 = (f32[20,320]{1,0:T(8,128)S(1)}, f32[20,320]{1,0:T(8,128)S(1)}, u32[]{:S(2)}, u32[]{:S(2)}) collective-permute-start(f32[20,320]{1,0:T(8,128)S(1)} %slice_select_fusion), channel_id=1, source_target_pairs={{0,64},{64,0},{1,65},{65,1},{2,66},{66,2},{3,67},{67,3},{4,68},{68... | collective-permute-start | bytes 76808 | tf_op jit(solution)/shard_map/ppermute | solution.py:421

commit v2 on v1

--- a/solution.py
+++ b/solution.py
@@ -12,7 +12,9 @@
 I4 = jnp.int32
 C = 320
 CELLS = 4096
-PIECE = 24
+WEIGHT_ROWS = 56
+BLOCK_ROWS = 16 + WEIGHT_ROWS
+WIDE = 384
 MIB = 1024 * 1024
 
 VELOCITIES = (
@@ -126,7 +128,44 @@
     return (iota((512, 256), 0) == key).astype(F4).astype(BF)
 
 
-def lattice_kernel(pop_ref, before_ref, behind_ref, relax_ref, lists_ref, after_ref, out_ref):
+def own_half(col):
+    return (iota((8, 128), 0) < 4) == (col == 0)
+
+
+def pack_piece(tile, half):
+    low = iota((8, 128), 1) < 64
+    return [
+        tile(0, 0),
+        tile(0, 1),
+        tile(1, 0),
+        tile(1, 1),
+        jnp.where(low, tile(0, 2), pltpu.roll(tile(1, 2), 64, 1)),
+        jnp.where(half, tile(2, 0), pltpu.roll(tile(2, 1), 4, 0)),
+        tile(2, 2),
+    ]
+
+
+def unpack_piece(tiles):
+    return (
+        (tiles[0], tiles[1], tiles[4]),
+        (tiles[2], tiles[3], pltpu.roll(tiles[4], 64, 1)),
+        (tiles[5], pltpu.roll(tiles[5], 4, 0), tiles[6]),
+    )
+
+
+def lattice_kernel(
+    col_ref,
+    pop_ref,
+    before_ref,
+    behind_ref,
+    relax_ref,
+    lists_ref,
+    mix_ref,
+    after_ref,
+    out_ref,
+    window,
+    routed,
+):
     row = iota((16, 256), 0)
     depth = iota((16, 256), 1) & 15
     read = []
@@ -163,23 +202,55 @@
     unused, old_flow = moments([pop_ref[index] for index in range(19)])
     bricks = brick_rows(old_flow + flow)
     select = route_rows(lists_ref[...])
-    out_ref[...] = jnp.dot(select, bricks, preferred_element_type=F4).astype(BF)
-
-
-def lattice(populations, before, behind, relaxation, lists):
+    routed[...] = jnp.dot(select, bricks, preferred_element_type=F4)
+    col = col_ref[0]
+    window[...] = jnp.zeros_like(window)
+
+    @pl.when(col == 0)
+    def _():
+        window[0:20, 0:C] = mix_ref[...]
+
+    @pl.when(col != 0)
+    def _():
+        window[4:24, 0:C] = mix_ref[...]
+
+    def tile(index, lanes):
+        start = pl.multiple_of((index * 8 + 8 * col) % 24, 8)
+        return window[pl.ds(start, 8), lanes * 128 : (lanes + 1) * 128]
+
+    weights = jnp.concatenate(pack_piece(tile, own_half(col)), axis=0)
+    for pair in range(16):
+        start = pair * 2 * BLOCK_ROWS
+        first = routed[pair * 32 : pair * 32 + 16]
+        second = routed[pair * 32 + 16 : pair * 32 + 32]
+        out_ref[start : start + 2 * BLOCK_ROWS] = jnp.concatenate(
+            [first, weights, second, weights], axis=0
+        ).astype(BF)
+
+
+def lattice(col, populations, before, behind, relaxation, lists, master):
+    vector = pl.BlockSpec(memory_space=pltpu.VMEM)
     return pl.pallas_call(
         lattice_kernel,
+        in_specs=[pl.BlockSpec(memory_space=pltpu.SMEM)] + [vector] * 6,
+        out_specs=(vector, vector),
         out_shape=(
             jax.ShapeDtypeStruct((19, 16, 256), F4),
-            jax.ShapeDtypeStruct((512, 128), BF),
+            jax.ShapeDtypeStruct((32 * BLOCK_ROWS, 128), BF),
         ),
+        scratch_shapes=[pltpu.VMEM((24, WIDE), F4), pltpu.VMEM((512, 128), F4)],
         name="lattice",
         compiler_params=pltpu.CompilerParams(vmem_limit_bytes=24 * MIB),
-    )(populations, before, behind, relaxation, lists)
+    )(col, populations, before, behind, relaxation, lists, master)
 
 
 def lift_kernel(arrived_ref, lift_ref, gain_ref, shift_ref, h_ref, target_ref, taps, lifted):
-    arrived = arrived_ref[...]
+    parts = []
+    for pair in range(16):
+        start = pair * 2 * BLOCK_ROWS
+        block = arrived_ref[start : start + 2 * BLOCK_ROWS].astype(F4)
+        parts += [block[0:16], block[BLOCK_ROWS : BLOCK_ROWS + 16]]
+    arrived = jnp.concatenate(parts, axis=0).astype(BF)
     flags = (iota((32, 512), 1) == iota((32, 512), 0) * 16 + 6).astype(F4).astype(BF)
     flags = jnp.dot(flags, arrived, preferred_element_type=F4).astype(BF)
     source = iota((32, 512), 1) >> 4
@@ -264,10 +335,12 @@
     col_ref,
     h_ref,
     target_ref,
-    mix_ref,
+    mine_ref,
+    other_ref,
     out_ref,
     send_ref,
     keep_ref,
+    mix_ref,
     mix_back,
     states,
     slopes,
@@ -283,6 +356,28 @@
     @pl.when(step == 0)
     def _():
         total[...] = jnp.zeros_like(total)
+        even = col_ref[0] == 0
+        upper = iota((8, 128), 0) < 4
+        for pair in range(16):
+            rows = slice(pair * 2 * BLOCK_ROWS, (pair + 1) * 2 * BLOCK_ROWS)
+            mine = mine_ref[rows, :].astype(F4)
+            other = other_ref[rows, :].astype(F4)
+            tiles = []
+            for start in (16, BLOCK_ROWS + 16):
+                sides = ([], [])
+                for index in range(7):
+                    at = slice(start + index * 8, start + index * 8 + 8)
+                    sides[0].append(jnp.where(even, mine[at], other[at]))
+                    sides[1].append(jnp.where(even, other[at], mine[at]))
+                left, right = unpack_piece(sides[0]), unpack_piece(sides[1])
+                middle = [jnp.where(upper, a, b) for a, b in zip(left[2], right[2])]
+                tiles += [left[0], left[1], middle, right[0], right[1]]
+            for lanes in range(3):
+                width = min(C - lanes * 128, 128)
+                column = jnp.concatenate([tile[lanes] for tile in tiles], axis=0).astype(BF)
+                mix_ref[pair * 80 : (pair + 1) * 80, lanes * 128 : lanes * 128 + width] = column[
+                    :, 0:width
+                ]
         same = (iota((C, C), 0) == iota((C, C), 1)).astype(F4).astype(BF)
         for layer in range(1, layers):
             rows = slice(layer * C, (layer + 1) * C)
@@ -323,7 +418,7 @@
                 back[:, part] += jnp.dot(
                     mix_back[rows_of, :], inner[layer, :, part], preferred_element_type=F4
                 )
-        total[rows_of, :] += lax.dot_general(
+        total[rows_of, 0:C] += lax.dot_general(
             inner[layer], state(layer)[...], (((1,), (1,)), ((), ())), preferred_element_type=F4
         )
 
@@ -331,17 +426,25 @@
     def _():
         col = col_ref[0]
         for piece in range(32):
-            own = pl.multiple_of(piece * 40 + 16 * col, 8)
-            other = pl.multiple_of(piece * 40 + 16 * (1 - col), 8)
-            rows = slice(piece * PIECE, (piece + 1) * PIECE)
-            keep_ref[rows, :] = total[pl.ds(own, PIECE), :]
-            send_ref[rows, :] = total[pl.ds(other, PIECE), :]
-
-
-def train(col, h, target, mixing, out_weight):
+            for ref, side in ((keep_ref, col), (send_ref, 1 - col)):
+
+                def tile(index, lanes):
+                    start = piece * 40 + 16
+                    if index < 2:
+                        start = pl.multiple_of(piece * 40 + 24 * side + 8 * index, 8)
+                    return total[pl.ds(start, 8), lanes * 128 : (lanes + 1) * 128]
+
+                packed = pack_piece(tile, own_half(side))
+                for index in range(7):
+                    start = piece * WEIGHT_ROWS + index * 8
+                    ref[start : start + 8, :] = packed[index]
+
+
+def train(col, h, target, mine, other, out_weight):
     cells = 1024
     steps = CELLS // cells
-    layers = mixing.shape[0] // C
+    layers = 4
+    block = pl.BlockSpec((32 * BLOCK_ROWS, 128), lambda i: (0, 0))
     return pl.pallas_call(
         functools.partial(train_kernel, steps, layers),
         grid=(steps,),
@@ -349,36 +452,61 @@
             pl.BlockSpec(memory_space=pltpu.SMEM),
             pl.BlockSpec((C, cells), lambda i: (0, i)),
             pl.BlockSpec((16, cells), lambda i: (0, i)),
-            pl.BlockSpec((layers * C, C), lambda i: (0, 0)),
+            block,
+            block,
             pl.BlockSpec((16, C), lambda i: (0, 0)),
         ],
         out_specs=(
-            pl.BlockSpec((32 * PIECE, C), lambda i: (0, 0)),
-            pl.BlockSpec((32 * PIECE, C), lambda i: (0, 0)),
+            pl.BlockSpec((32 * WEIGHT_ROWS, 128), lambda i: (0, 0)),
+            pl.BlockSpec((32 * WEIGHT_ROWS, 128), lambda i: (0, 0)),
         ),
         out_shape=(
-            jax.ShapeDtypeStruct((32 * PIECE, C), F4),
-            jax.ShapeDtypeStruct((32 * PIECE, C), F4),
+            jax.ShapeDtypeStruct((32 * WEIGHT_ROWS, 128), F4),
+            jax.ShapeDtypeStruct((32 * WEIGHT_ROWS, 128), F4),
         ),
         scratch_shapes=[
+            pltpu.VMEM((layers * C, C), BF),
             pltpu.VMEM((layers * C, C), BF),
             pltpu.VMEM((layers, C, cells), BF),
             pltpu.VMEM((layers, C, cells), F4),
             pltpu.VMEM((C, cells), F4),
             pltpu.VMEM((C, cells), F4),
             pltpu.VMEM((layers, C, cells), BF),
-            pltpu.VMEM((layers * C, C), F4),
+            pltpu.VMEM((layers * C, WIDE), F4),
         ],
         name="train",
         compiler_params=pltpu.CompilerParams(vmem_limit_bytes=48 * MIB),
-    )(col, h, target, mixing, out_weight)
-
-
-def adamw(master, gradient, first, second):
-    first_next = 0.9 * first + 0.1 * gradient
-    second_next = 0.999 * second + 0.001 * gradient * gradient
+    )(col, h, target, mine, other, out_weight)
+
+
+def update_kernel(
+    col_ref, own_ref, other_ref, master_ref, first_ref, second_ref, new_ref, first_out, second_out
+):
+    packed = own_ref[...] + other_ref[...]
+    parts = unpack_piece([packed[index * 8 : index * 8 + 8] for index in range(7)])
+    full, rest, half = [jnp.concatenate(part, axis=1) for part in parts]
+    even = col_ref[0] == 0
+    lower = jnp.concatenate([full, rest, half], axis=0)
+    upper = pltpu.roll(jnp.concatenate([half, full, rest], axis=0), 20, 0)
+    gradient = jnp.where(even, lower, upper)[0:20, 0:C]
+    master = master_ref[...]
+    first_next = 0.9 * first_ref[...] + 0.1 * gradient
+    second_next = 0.999 * second_ref[...] + 0.001 * gradient * gradient
     ratio = first_next / (1.0 - 0.9**10) / (jnp.sqrt(second_next / (1.0 - 0.999**10)) + 1e-08)
-    return (master - 0.01 * (ratio + 0.1 * master), first_next, second_next)
+    new_ref[...] = master - 0.01 * (ratio + 0.1 * master)
+    first_out[...] = first_next
+    second_out[...] = second_next
+
+
+def update(col, own, other, master, first, second):
+    vector = pl.BlockSpec(memory_space=pltpu.VMEM)
+    return pl.pallas_call(
+        update_kernel,
+        in_specs=[pl.BlockSpec(memory_space=pltpu.SMEM)] + [vector] * 5,
+        out_specs=(vector,) * 3,
+        out_shape=(jax.ShapeDtypeStruct(master.shape, F4),) * 3,
+        name="update",
+    )(col, own, other, master, first, second)
 
 
 def body(
@@ -396,30 +524,29 @@
     every = ("sec", "row", "col")
     size = lax.axis_size(every)
     swap = [(0, 1), (1, 0)]
-    col = lax.axis_index("col")
+    col = lax.axis_index("col").astype(I4)[None]
     up = [(i, (i + 1) % size) for i in range(size)]
     before = lax.ppermute(populations[1:15, 15], every, up)
     behind = lax.ppermute(populations[1:15, 0], every, [(j, i) for i, j in up])
-    shard = jnp.broadcast_to(mix_master.astype(BF), (32, 20, C))
-    mine = lax.all_to_all(shard, "row", split_axis=0, concat_axis=0, tiled=True)
-    other = lax.ppermute(mine, "col", swap)
-    pair = [jnp.where(col == 0, mine, other), jnp.where(col == 0, other, mine)]
-    mixing = jnp.stack(pair, axis=1).reshape(64 * 20, C)
-    after, outgoing = lattice(populations, before, behind, relaxation, send_lists)
+    after, outgoing = lattice(
+        col, populations, before, behind, relaxation, send_lists, mix_master
+    )
     arrived = lax.all_to_all(
-        outgoing.reshape(32, 16, 128), "row", split_axis=0, concat_axis=0, tiled=True
-    ).reshape(512, 128)
+        outgoing.reshape(32, BLOCK_ROWS, 128), "row", split_axis=0, concat_axis=0, tiled=True
+    ).reshape(32 * BLOCK_ROWS, 128)
+    other = lax.ppermute(arrived, "col", swap)
     h, target = lift(arrived, lift_weight, norm_gain[:, None], norm_shift[:, None])
     out_rows = jnp.pad(out_weight, ((3, 10), (0, 0)))
-    send, keep = train(col.astype(I4)[None], h, target, mixing, out_rows)
+    send, keep = train(col, h, target, arrived, other, out_rows)
     half = keep + lax.ppermute(send, "col", swap)
     terms = lax.all_to_all(
-        half.reshape(32, PIECE, C), "row", split_axis=0, concat_axis=0, tiled=True
+        half.reshape(32, WEIGHT_ROWS, 128), "row", split_axis=0, concat_axis=0, tiled=True
     )
     summed = jnp.sum(terms, axis=0)
-    summed = jnp.where(col == 0, summed[0:20], summed[4:24])
-    gradient = summed + lax.ppermute(summed, "sec", swap)
-    new_master, new_first, new_second = adamw(mix_master, gradient, mix_first, mix_second)
+    across = lax.ppermute(summed, "sec", swap)
+    new_master, new_first, new_second = update(
+        col, summed, across, mix_master, mix_first, mix_second
+    )
     return (after, new_master, new_first, new_second)
 
 

time: 129 us -> 108 us (0.84)
  blocking collectives: 44.6 us -> 33.4 us
  waiting for transfers between devices: 14.4 us -> 6.21 us
  starting transfers between devices: 16.9 us -> 13.9 us
  local copies, waits for them, and re-layouts: 4.98 us -> 7.96 us
  other arithmetic: 2.15 us -> 0.16 us
    all_to_all x2, blocking collectives: 44.6 us -> 33.4 us  [the longest x1 19.2 us: body(): lax.all_to_all(half.reshape(32, WEIGHT_ROWS, 128), 'row', split_axis=0, c...]
    all_to_all x1 -> x0, waiting for transfers between devices: 8.19 us -> none  [body(): lax.all_to_all(outgoing.reshape(32, 16, 128), 'row', split_axis=0, concat...]
    all_to_all x1 -> x0, starting transfers between devices: 4.03 us -> none  [body(): lax.all_to_all(outgoing.reshape(32, 16, 128), 'row', split_axis=0, concat...]
    unnamed x29 -> x15, local copies, waits for them, and re-layouts: 2.16 us -> 4.72 us
    ppermute x1, starting transfers between devices: 2.41 us -> 0.09 us  [body(): half = keep + lax.ppermute(send, 'col', swap)]
    ppermute x2, starting transfers between devices: 3.21 us -> 5.45 us  [the longest x1 3.15 us: body(): across = lax.ppermute(summed, 'sec', swap)]
    pallas_call x1 -> x2, Pallas kernels: 1.58 us -> 3.24 us  [the longest x1 1.68 us: lattice(): pl.pallas_call(lattice_kernel, in_specs=[pl.BlockSpec(memory_space=pltpu....]
    ppermute x1, starting transfers between devices: 6.69 us -> 8.27 us  [body(): behind = lax.ppermute(populations[1:15, 0], every, [(j, i) for i, j in up])]
  transfers between devices with their start and end apart: 6 -> 5, of which waited for: 4 -> 4; matrix products, arithmetic and copies ran while one was open for 0% -> 3% of each run, Pallas kernels for 9% -> 9%
where the time goes in v2:
time: 108 us; the launch traced here: 107 us
  Pallas kernels  45 us (42%)
  blocking collectives  33.4 us (31%)
  starting transfers between devices  13.9 us (13%)
  local copies, waits for them, and re-layouts  7.96 us (7%)
  waiting for transfers between devices  6.21 us (6%)
    pallas_call x1, Pallas kernels, train(): pl.pallas_call(functools.partial(train_kernel, steps, layers), grid=(step...  32.2 us
    all_to_all x1, blocking collectives, body(): lax.all_to_all(half.reshape(32, WEIGHT_ROWS, 128), 'row', split_axis=0, c...  19.2 us
    all_to_all x1, blocking collectives, body(): lax.all_to_all(outgoing.reshape(32, BLOCK_ROWS, 128), 'row', split_axis=0...  14.1 us
    pallas_call x1, Pallas kernels, lift(): pl.pallas_call(lift_kernel, out_shape=(jax.ShapeDtypeStruct((C, CELLS), B...  9.59 us
    ppermute x1, starting transfers between devices, body(): behind = lax.ppermute(populations[1:15, 0], every, [(j, i) for i, j in up])  8.27 us
    unnamed x15, local copies, waits for them, and re-layouts  4.72 us
    ppermute x1, starting transfers between devices, body(): across = lax.ppermute(summed, 'sec', swap)  3.15 us
    ppermute x1, waiting for transfers between devices, body(): half = keep + lax.ppermute(send, 'col', swap)  2.46 us
  transfers between devices with their start and end apart: 5, of which 4 were waited for; matrix products, arithmetic and copies ran while one was open for 3% of the time, Pallas kernels for 9%

profile of v2, /device:TPU:0, one launch (start us, length us, event | category | flops | bytes accessed | tf_op | source)
XLA Modules:
  0.0 107.3 jit_solution(5299633348022422645)
XLA Ops:
  0.6 1.0 fusion
  1.6 0.1 collective-permute-start
  1.7 8.3 %collective-permute-start.1 = (f32[14,256]{1,0:T(8,128)S(1)}, f32[14,256]{1,0:T(8,128)S(1)}, u32[]{:S(2)}, u32[]{:S(2)}) collective-permute-start(f32[14,256]{1,0:T(8,128)S(1)} %bitcast.16), channel_id=1, source_target_pairs={{1,0},{2,1},{3,2},{4,3},{5,4},{6,5},{7,6},{8,7},{9,8},{10,9},{11,1... | collective-permute-start | bytes 43016 | tf_op jit(solution)/shard_map/ppermute | solution.py:530
  10.0 1.3 %collective-permute-done.before_ref = f32[14,256]{1,0:T(8,128)S(1)} collective-permute-done((f32[14,256]{1,0:T(8,128)S(1)}, f32[14,256]{1,0:T(8,128)S(1)}, u32[]{:S(2)}, u32[]{:S(2)}) %collective-permute-start) | collective-permute-done | bytes 14368 | tf_op jit(solution)/shard_map/ppermute | solution.py:529
  11.3 0.1 collective-permute-done.1.behind_ref
  11.4 0.0 copy-start
  11.4 1.0 copy-done
  12.4 0.0 copy-start.1
  12.4 0.8 copy-done.1
  13.2 0.0 copy-start.2
  13.2 0.7 copy-done.2
  13.9 0.0 copy-start.3
  13.9 0.7 copy-done.3
  14.5 1.7 %lattice.1 = (f32[19,16,256]{2,1,0:T(8,128)}, bf16[2304,128]{1,0:T(8,128)(2,1)S(1)}) custom-call(s32[1]{0:T(128)} %bitcast.col_ref, f32[19,16,256]{2,1,0:T(8,128)S(1)} %copy-done, f32[14,256]{1,0:T(8,128)S(1)} %collective-permute-done.before_ref, f32[14,256]{1,0:T(8,128)S(1)} %collective-permute-done.1.behind_ref, f32[16,256]{1,0:T(8,128)S(1)} %copy-done.2, ...), custom_call_target="tpu_custom_call" | custom-call | tf_op jit(solution)/shard_map/lattice/pallas_call | solution.py:233
  16.2 14.1 %all_to_all.10 = bf16[32,72,128]{2,1,0:T(8,128)(2,1)S(1)} all-to-all(bf16[32,72,128]{2,1,0:T(8,128)(2,1)S(1)} %bitcast.13), channel_id=1, replica_groups=mesh['sec'=2,'row'=32,'col'=2] {'row'}, dimensions={0} | all-to-all | bytes 1179648 | tf_op jit(solution)/shard_map/all_to_all | solution.py:534
  30.4 2.3 %collective-permute-start.2 = (bf16[2304,128]{1,0:T(8,128)(2,1)S(1)}, bf16[2304,128]{1,0:T(8,128)(2,1)S(1)}, u32[]{:S(2)}, u32[]{:S(2)}) collective-permute-start(bf16[2304,128]{1,0:T(8,128)(2,1)S(1)} %bitcast.10), channel_id=1, source_target_pairs={{0,1},{1,0},{2,3},{3,2},{4,5},{5,4},{6,7},{7,6},{8,9},{9,8},{10,11... | collective-permute-start | bytes 1769480 | tf_op jit(solution)/shard_map/ppermute | solution.py:537
  32.7 1.0 copy.19.lift_ref
  33.7 0.8 broadcast_in_dim.12.gain_ref
  34.5 0.8 broadcast_in_dim.13.shift_ref
  35.2 0.7 pad.4.out_ref
  35.9 9.6 %lift.1 = (bf16[320,4096]{1,0:T(8,128)(2,1)S(1)}, f32[16,4096]{1,0:T(8,128)S(1)}) custom-call(bf16[2304,128]{1,0:T(8,128)(2,1)S(1)} %bitcast.11, bf16[320,81]{1,0:T(8,128)(2,1)S(1)} %copy.19.lift_ref, f32[320,1]{1,0:T(8,128)S(1)} %broadcast_in_dim.12.gain_ref, f32[320,1]{1,0:T(8,128)S(1)} %broadcast_in_dim.13.shift_ref), custom_call_target="tpu_custom_call" | custom-call | tf_op jit(solution)/shard_map/lift/pallas_call | solution.py:320
  45.5 0.0 collective-permute-done.2.other_ref
  45.6 32.2 %train.1 = (f32[1792,128]{1,0:T(8,128)S(1)}, f32[1792,128]{1,0:T(8,128)S(1)}) custom-call(s32[1]{0:T(128)} %bitcast.col_ref, bf16[320,4096]{1,0:T(8,128)(2,1)S(1)} %get-tuple-element.15.h_ref, f32[16,4096]{1,0:T(8,128)S(1)} %get-tuple-element.16.target_ref, bf16[2304,128]{1,0:T(8,128)(2,1)S(1)} %bitcast.12, ...), custom_call_target="tpu_custom_call" | custom-call | tf_op jit(solution)/shard_map/train/pallas_call | solution.py:448
  77.7 0.1 collective-permute-start.3
  77.8 2.5 %collective-permute-done.3 = f32[1792,128]{1,0:T(8,128)S(1)} collective-permute-done((f32[1792,128]{1,0:T(8,128)S(1)}, f32[1792,128]{1,0:T(8,128)S(1)}, u32[]{:S(2)}, u32[]{:S(2)}) %collective-permute-start.3) | collective-permute-done | bytes 917536 | tf_op jit(solution)/shard_map/ppermute | solution.py:541
  80.3 0.1 add.5
  80.4 19.2 %all_to_all.11 = f32[32,56,128]{2,1,0:T(8,128)S(1)} all-to-all(f32[32,56,128]{2,1,0:T(8,128)S(1)} %bitcast.14), channel_id=1, replica_groups=mesh['sec'=2,'row'=32,'col'=2] {'row'}, dimensions={0} | all-to-all | bytes 1835008 | tf_op jit(solution)/shard_map/all_to_all | solution.py:542
  99.6 0.1 reduce_sum.9.own_ref
  99.7 0.0 copy-start.4
  99.7 3.1 %collective-permute-start.4 = (f32[56,128]{1,0:T(8,128)S(1)}, f32[56,128]{1,0:T(8,128)S(1)}, u32[]{:S(2)}, u32[]{:S(2)}) collective-permute-start(f32[56,128]{1,0:T(8,128)S(1)} %reduce_sum.9.own_ref), channel_id=1, source_target_pairs={{0,64},{64,0},{1,65},{65,1},{2,66},{66,2},{3,67},{67,3},{4,68},{68... | collective-permute-start | bytes 86024 | tf_op jit(solution)/shard_map/ppermute | solution.py:546
  102.8 2.3 %collective-permute-done.4.other_ref = f32[56,128]{1,0:T(8,128)S(1)} collective-permute-done((f32[56,128]{1,0:T(8,128)S(1)}, f32[56,128]{1,0:T(8,128)S(1)}, u32[]{:S(2)}, u32[]{:S(2)}) %collective-permute-start.4) | collective-permute-done | bytes 28704 | tf_op jit(solution)/shard_map/ppermute | solution.py:546
  105.1 0.0 copy-done.4
  105.1 0.0 copy-start.5
  105.2 0.6 copy-done.5
  105.7 1.6 %update.1 = (f32[20,320]{1,0:T(8,128)}, f32[20,320]{1,0:T(8,128)}, f32[20,320]{1,0:T(8,128)}) custom-call(s32[1]{0:T(128)} %bitcast.col_ref, f32[56,128]{1,0:T(8,128)} %copy-done.4, f32[56,128]{1,0:T(8,128)} %copy-done.5, f32[20,320]{1,0:T(8,128)} %master_ref.1, f32[20,320]{1,0:T(8,128)} %first_ref.1, f32[20,320]{1,0:T(8,128)} %second_ref.1), custom_call_target="tpu_custom_call" | custom-call | tf_op jit(solution)/shard_map/update/pallas_call | solution.py:503
  (2 shorter events, 0.0 us)
Async XLA Ops:
  1.6 9.7 %collective-permute-start = (f32[14,256]{1,0:T(8,128)S(1)}, f32[14,256]{1,0:T(8,128)S(1)}, u32[]{:S(2)}, u32[]{:S(2)}) collective-permute-start(f32[14,256]{1,0:T(8,128)S(1)} %bitcast.15), channel_id=1, source_target_pairs={{0,1},{1,2},{2,3},{3,4},{4,5},{5,6},{6,7},{7,8},{8,9},{9,10},{10,1... | collective-permute-start | bytes 43016 | tf_op jit(solution)/shard_map/ppermute | solution.py:529
  1.7 9.7 %collective-permute-start.1 = (f32[14,256]{1,0:T(8,128)S(1)}, f32[14,256]{1,0:T(8,128)S(1)}, u32[]{:S(2)}, u32[]{:S(2)}) collective-permute-start(f32[14,256]{1,0:T(8,128)S(1)} %bitcast.16), channel_id=1, source_target_pairs={{1,0},{2,1},{3,2},{4,3},{5,4},{6,5},{7,6},{8,7},{9,8},{10,9},{11,1... | collective-permute-start | bytes 43016 | tf_op jit(solution)/shard_map/ppermute | solution.py:530
  11.4 1.0 copy-start
  12.4 0.8 copy-start.1
  13.2 0.7 copy-start.2
  13.9 0.7 copy-start.3
  30.4 15.2 %collective-permute-start.2 = (bf16[2304,128]{1,0:T(8,128)(2,1)S(1)}, bf16[2304,128]{1,0:T(8,128)(2,1)S(1)}, u32[]{:S(2)}, u32[]{:S(2)}) collective-permute-start(bf16[2304,128]{1,0:T(8,128)(2,1)S(1)} %bitcast.10), channel_id=1, source_target_pairs={{0,1},{1,0},{2,3},{3,2},{4,5},{5,4},{6,7},{7,6},{8,9},{9,8},{10,11... | collective-permute-start | bytes 1769480 | tf_op jit(solution)/shard_map/ppermute | solution.py:537
  77.7 2.6 %collective-permute-start.3 = (f32[1792,128]{1,0:T(8,128)S(1)}, f32[1792,128]{1,0:T(8,128)S(1)}, u32[]{:S(2)}, u32[]{:S(2)}) collective-permute-start(f32[1792,128]{1,0:T(8,128)S(1)} %get-tuple-element.18), channel_id=1, source_target_pairs={{0,1},{1,0},{2,3},{3,2},{4,5},{5,4},{6,7},{7,6},{8,9},{9,8},{10,11... | collective-permute-start | bytes 2752520 | tf_op jit(solution)/shard_map/ppermute | solution.py:541
  99.7 5.5 %copy-start.4 = (f32[56,128]{1,0:T(8,128)}, f32[56,128]{1,0:T(8,128)S(1)}, u32[]{:S(2)}) copy-start(f32[56,128]{1,0:T(8,128)S(1)} %reduce_sum.9.own_ref) | copy-start | bytes 86020
  99.7 5.5 %collective-permute-start.4 = (f32[56,128]{1,0:T(8,128)S(1)}, f32[56,128]{1,0:T(8,128)S(1)}, u32[]{:S(2)}, u32[]{:S(2)}) collective-permute-start(f32[56,128]{1,0:T(8,128)S(1)} %reduce_sum.9.own_ref), channel_id=1, source_target_pairs={{0,64},{64,0},{1,65},{65,1},{2,66},{66,2},{3,67},{67,3},{4,68},{68... | collective-permute-start | bytes 86024 | tf_op jit(solution)/shard_map/ppermute | solution.py:546
  105.1 0.6 copy-start.5

commit v3 on v2

--- a/solution.py
+++ b/solution.py
@@ -15,6 +15,7 @@
 WEIGHT_ROWS = 56
 BLOCK_ROWS = 16 + WEIGHT_ROWS
 WIDE = 384
+SPAN = 1024
 MIB = 1024 * 1024
 
 VELOCITIES = (
@@ -40,14 +41,7 @@
 )
 LATTICE_WEIGHTS = (1.0 / 3.0,) + (1.0 / 18.0,) * 6 + (1.0 / 36.0,) * 12
 
-TAIL_P = 0.3275911 * 0.7071067811865476
-TAIL_A = (
-    0.5 * 0.254829592,
-    0.5 * -0.284496736,
-    0.5 * 1.421413741,
-    0.5 * -1.453152027,
-    0.5 * 1.061405429,
-)
+ROOT_HALF = 0.7071067811865476
 EXP_SCALE = -0.5 * 1.4426950408889634
 
 
@@ -55,24 +49,14 @@
     return lax.broadcasted_iota(I4, shape, dim)
 
 
-def gelu_parts(z):
-    size = jnp.abs(z)
-    t = pl.reciprocal(1.0 + TAIL_P * size, approx=True)
+def gelu_value(z):
+    return z * (0.5 + 0.5 * lax.erf(z * ROOT_HALF))
+
+
+def gelu_both(z):
+    share = 0.5 + 0.5 * lax.erf(z * ROOT_HALF)
     bell = jnp.exp2(z * z * EXP_SCALE)
-    poly = (((TAIL_A[4] * t + TAIL_A[3]) * t + TAIL_A[2]) * t + TAIL_A[1]) * t + TAIL_A[0]
-    return size, bell, poly * t * bell
-
-
-def gelu_value(z):
-    size, bell, tail = gelu_parts(z)
-    return jnp.maximum(z, 0.0) - size * tail
-
-
-def gelu_both(z):
-    size, bell, tail = gelu_parts(z)
-    value = jnp.maximum(z, 0.0) - size * tail
-    below = tail - (size * 0.3989422804014327) * bell
-    return value, jnp.where(z >= 0.0, 1.0 - below, below)
+    return z * share, share + (z * 0.3989422804014327) * bell
 
 
 def moments(read):
@@ -88,8 +72,7 @@
     return density, [moment[axis] / density for axis in range(3)]
 
 
-def brick_rows(fields):
-    stacked = jnp.concatenate(fields, axis=0).astype(BF)
+def brick_rows(stacked):
     lane = iota((256, 256), 1)
     source = (lane & 0xC0) | (((lane >> 3) & 3) << 4) | (((lane >> 5) & 1) << 3) | (lane & 7)
     lanes = (iota((256, 256), 0) == source).astype(F4).astype(BF)
@@ -153,19 +136,81 @@
     )
 
 
-def lattice_kernel(
+def prepare_kernel(
     col_ref,
     pop_ref,
-    before_ref,
-    behind_ref,
-    relax_ref,
     lists_ref,
     mix_ref,
-    after_ref,
+    lift_ref,
+    gain_ref,
+    shift_ref,
     out_ref,
+    old_ref,
+    select_ref,
+    weights_ref,
+    lift_out,
+    gain_out,
+    shift_out,
+    rows_out,
     window,
-    routed,
+    rows,
 ):
+    unused, old_flow = moments([pop_ref[index] for index in range(19)])
+    old_ref[...] = jnp.concatenate(old_flow, axis=0).astype(BF)
+    select_ref[...] = route_rows(lists_ref[...])
+    col = col_ref[0]
+    window[...] = jnp.zeros_like(window)
+
+    @pl.when(col == 0)
+    def _():
+        window[0:20, 0:C] = mix_ref[...]
+
+    @pl.when(col != 0)
+    def _():
+        window[4:24, 0:C] = mix_ref[...]
+
+    def tile(index, lanes):
+        start = pl.multiple_of((index * 8 + 8 * col) % 24, 8)
+        return window[pl.ds(start, 8), lanes * 128 : (lanes + 1) * 128]
+
+    weights_ref[...] = jnp.concatenate(pack_piece(tile, own_half(col)), axis=0)
+    column = iota((81, 224), 1)
+    feature = (column & 7) * 27 + (column >> 3)
+    valid = ((column & 7) < 3) & (column < 216)
+    spread = jnp.where(valid & (iota((81, 224), 0) == feature), 1.0, 0.0).astype(BF)
+    lift_out[...] = jnp.dot(lift_ref[...], spread, preferred_element_type=F4).astype(BF)
+    same = iota((C, C), 0) == iota((C, C), 1)
+    for source, target in ((gain_ref, gain_out), (shift_ref, shift_out)):
+        down = jnp.sum(jnp.where(same, source[...], 0.0), axis=1, keepdims=True)
+        target[...] = jnp.broadcast_to(down, (C, 128))
+    rows[...] = jnp.zeros_like(rows)
+    rows[3:6, :] = out_ref[...].astype(F4)
+    rows_out[...] = rows[...].astype(BF)
+
+
+def prepare(col, populations, lists, master, lift_weight, gain, shift, out_weight):
+    vector = pl.BlockSpec(memory_space=pltpu.VMEM)
+    return pl.pallas_call(
+        prepare_kernel,
+        in_specs=[pl.BlockSpec(memory_space=pltpu.SMEM)] + [vector] * 7,
+        out_specs=(vector,) * 7,
+        out_shape=(
+            jax.ShapeDtypeStruct((48, 256), BF),
+            jax.ShapeDtypeStruct((512, 256), BF),
+            jax.ShapeDtypeStruct((WEIGHT_ROWS, 128), F4),
+            jax.ShapeDtypeStruct((C, 224), BF),
+            jax.ShapeDtypeStruct((C, 128), F4),
+            jax.ShapeDtypeStruct((C, 128), F4),
+            jax.ShapeDtypeStruct((16, C), BF),
+        ),
+        scratch_shapes=[pltpu.VMEM((24, WIDE), F4), pltpu.VMEM((16, C), F4)],
+        name="prepare",
+        cost_estimate=pl.CostEstimate(flops=10**7, bytes_accessed=4 * 10**6, transcendentals=0),
+        compiler_params=pltpu.CompilerParams(vmem_limit_bytes=16 * MIB),
+    )(col, populations, lists, master, lift_weight, gain, shift, out_weight)
+
+
+def streamed(pop_ref, before_ref, behind_ref):
     row = iota((16, 256), 0)
     depth = iota((16, 256), 1) & 15
     read = []
@@ -183,6 +228,38 @@
         elif along_z < 0:
             plane = jnp.where(depth == 15, pltpu.roll(plane, 15, 1), pltpu.roll(plane, 255, 1))
         read.append(plane)
+    return read
+
+
+def route_kernel(
+    pop_ref, before_ref, behind_ref, old_ref, select_ref, weights_ref, out_ref, routed
+):
+    density, flow = moments(streamed(pop_ref, before_ref, behind_ref))
+    fields = jnp.concatenate([old_ref[...]] + [part.astype(BF) for part in flow], axis=0)
+    bricks = brick_rows(fields)
+    routed[...] = jnp.dot(select_ref[...], bricks, preferred_element_type=F4)
+    weights = weights_ref[...]
+    for pair in range(16):
+        start = pair * 2 * BLOCK_ROWS
+        first = routed[pair * 32 : pair * 32 + 16]
+        second = routed[pair * 32 + 16 : pair * 32 + 32]
+        out_ref[start : start + 2 * BLOCK_ROWS] = jnp.concatenate(
+            [first, weights, second, weights], axis=0
+        ).astype(BF)
+
+
+def route(populations, before, behind, old, select, weights):
+    return pl.pallas_call(
+        route_kernel,
+        out_shape=jax.ShapeDtypeStruct((32 * BLOCK_ROWS, 128), BF),
+        scratch_shapes=[pltpu.VMEM((512, 128), F4)],
+        name="route",
+        compiler_params=pltpu.CompilerParams(vmem_limit_bytes=16 * MIB),
+    )(populations, before, behind, old, select, weights)
+
+
+def collide_kernel(pop_ref, before_ref, behind_ref, relax_ref, after_ref):
+    read = streamed(pop_ref, before_ref, behind_ref)
     density, flow = moments(read)
     speed = flow[0] * flow[0] + flow[1] * flow[1] + flow[2] * flow[2]
     relaxation = relax_ref[...]
@@ -199,52 +276,32 @@
             shape = 1.0 + 3.0 * project + 4.5 * project * project - 1.5 * speed
         balance = LATTICE_WEIGHTS[index] * density * shape
         after_ref[index] = read[index] - relaxation * (read[index] - balance)
-    unused, old_flow = moments([pop_ref[index] for index in range(19)])
-    bricks = brick_rows(old_flow + flow)
-    select = route_rows(lists_ref[...])
-    routed[...] = jnp.dot(select, bricks, preferred_element_type=F4)
-    col = col_ref[0]
-    window[...] = jnp.zeros_like(window)
-
-    @pl.when(col == 0)
-    def _():
-        window[0:20, 0:C] = mix_ref[...]
-
-    @pl.when(col != 0)
-    def _():
-        window[4:24, 0:C] = mix_ref[...]
-
-    def tile(index, lanes):
-        start = pl.multiple_of((index * 8 + 8 * col) % 24, 8)
-        return window[pl.ds(start, 8), lanes * 128 : (lanes + 1) * 128]
-
-    weights = jnp.concatenate(pack_piece(tile, own_half(col)), axis=0)
-    for pair in range(16):
-        start = pair * 2 * BLOCK_ROWS
-        first = routed[pair * 32 : pair * 32 + 16]
-        second = routed[pair * 32 + 16 : pair * 32 + 32]
-        out_ref[start : start + 2 * BLOCK_ROWS] = jnp.concatenate(
-            [first, weights, second, weights], axis=0
-        ).astype(BF)
-
-
-def lattice(col, populations, before, behind, relaxation, lists, master):
-    vector = pl.BlockSpec(memory_space=pltpu.VMEM)
+
+
+def collide(populations, before, behind, relaxation):
     return pl.pallas_call(
-        lattice_kernel,
-        in_specs=[pl.BlockSpec(memory_space=pltpu.SMEM)] + [vector] * 6,
-        out_specs=(vector, vector),
-        out_shape=(
-            jax.ShapeDtypeStruct((19, 16, 256), F4),
-            jax.ShapeDtypeStruct((32 * BLOCK_ROWS, 128), BF),
-        ),
-        scratch_shapes=[pltpu.VMEM((24, WIDE), F4), pltpu.VMEM((512, 128), F4)],
-        name="lattice",
-        compiler_params=pltpu.CompilerParams(vmem_limit_bytes=24 * MIB),
-    )(col, populations, before, behind, relaxation, lists, master)
-
-
-def lift_kernel(arrived_ref, lift_ref, gain_ref, shift_ref, h_ref, target_ref, taps, lifted):
+        collide_kernel,
+        out_shape=jax.ShapeDtypeStruct((19, 16, 256), F4),
+        name="collide",
+        cost_estimate=pl.CostEstimate(flops=10**7, bytes_accessed=4 * 10**6, transcendentals=0),
+        compiler_params=pltpu.CompilerParams(vmem_limit_bytes=16 * MIB),
+    )(populations, before, behind, relaxation)
+
+
+def lift_kernel(
+    arrived_ref,
+    weight_ref,
+    gain_ref,
+    shift_ref,
+    h_ref,
+    target_ref,
+    taps,
+    lifted,
+    sums,
+    squares,
+    means,
+    scales,
+):
     parts = []
     for pair in range(16):
         start = pair * 2 * BLOCK_ROWS
@@ -273,60 +330,62 @@
     for x, y, z in shifts:
         inside = (cell_x + x >= 0) & (cell_x + x < 4) & (cell_y + y >= 0) & (cell_y + y < 4)
         masks.append(inside & (cell_z + z >= 0) & (cell_z + z < 8))
-    for pair in range(14):
-        for brick in range(32):
+    weight = weight_ref[...]
+    for start in range(0, CELLS, SPAN):
+        part = slice(start, start + SPAN)
+        for brick in range(start // 128, (start + SPAN) // 128):
             own = held[brick * 8 : (brick + 1) * 8]
-            halves = []
-            for tap in (2 * pair, 2 * pair + 1):
-                if tap == 27:
-                    halves.append(jnp.zeros((8, 128), F4))
-                    continue
-                x, y, z = shifts[tap]
-                turn = -(x * 32 + y * 8 + z) % 128
-                moved = pltpu.roll(own, turn, 1) if turn else own
-                halves.append(jnp.where(masks[tap], moved, 0.0))
-            taps[pair * 16 : (pair + 1) * 16, brick * 128 : (brick + 1) * 128] = jnp.concatenate(
-                halves, axis=0
-            ).astype(BF)
-    column = iota((81, 224), 1)
-    feature = (column & 7) * 27 + (column >> 3)
-    valid = ((column & 7) < 3) & (column < 216)
-    spread = jnp.where(valid & (iota((81, 224), 0) == feature), 1.0, 0.0).astype(BF)
-    weight = jnp.dot(lift_ref[...], spread, preferred_element_type=F4).astype(BF)
-    for start in range(0, CELLS, 512):
-        part = slice(start, start + 512)
+            for pair in range(14):
+                halves = []
+                for tap in (2 * pair, 2 * pair + 1):
+                    if tap == 27:
+                        halves.append(jnp.zeros((8, 128), F4))
+                        continue
+                    x, y, z = shifts[tap]
+                    turn = -(x * 32 + y * 8 + z) % 128
+                    moved = pltpu.roll(own, turn, 1) if turn else own
+                    halves.append(jnp.where(masks[tap], moved, 0.0))
+                taps[pair * 16 : (pair + 1) * 16, brick * 128 : (brick + 1) * 128] = (
+                    jnp.concatenate(halves, axis=0).astype(BF)
+                )
         lifted[:, part] = jnp.dot(weight, taps[:, part], preferred_element_type=F4)
-
-    @pl.loop(0, C // 16)
-    def _(block):
-        rows = pl.ds(pl.multiple_of(block * 16, 16), 16)
-        total = jnp.zeros((16, 128), F4)
-        square = jnp.zeros((16, 128), F4)
-        for start in range(0, CELLS, 128):
-            value = lifted[rows, start : start + 128]
-            total = total + value
-            square = square + value * value
-        mean = jnp.sum(total, axis=1, keepdims=True) / CELLS
-        spread = jnp.sum(square, axis=1, keepdims=True) / CELLS - mean * mean
-        scale = lax.rsqrt(spread + 1e-05) * gain_ref[rows, :]
-        shift = shift_ref[rows, :]
-        for start in range(0, CELLS, 256):
-            part = slice(start, start + 256)
-            normed = (lifted[rows, part] - mean) * scale + shift
-            h_ref[rows, part] = gelu_value(normed).astype(BF)
-
-
-def lift(arrived, lift_weight, gain, shift):
+        for row in range(0, C, 16):
+            rows = slice(row, row + 16)
+            total = None
+            for at in range(start, start + SPAN, 128):
+                value = lifted[rows, at : at + 128]
+                total = value if total is None else total + value
+                square = value * value if at == start else square + value * value
+            sums[rows, :] = total if start == 0 else sums[rows, :] + total
+            squares[rows, :] = square if start == 0 else squares[rows, :] + square
+    mean = jnp.sum(sums[...], axis=1, keepdims=True) / CELLS
+    spread = jnp.sum(squares[...], axis=1, keepdims=True) / CELLS - mean * mean
+    means[...] = jnp.broadcast_to(mean, (C, 128))
+    scales[...] = lax.rsqrt(spread + 1e-05) * gain_ref[...]
+
+    @pl.loop(0, CELLS // SPAN)
+    def _(index):
+        for row in range(0, C, 16):
+            rows = slice(row, row + 16)
+            mean, scale, shift = means[rows, :], scales[rows, :], shift_ref[rows, :]
+            for at in range(0, SPAN, 128):
+                part = pl.ds(pl.multiple_of(index * SPAN + at, 128), 128)
+                normed = (lifted[rows, part] - mean) * scale + shift
+                h_ref[rows, part] = gelu_value(normed).astype(BF)
+
+
+def lift(arrived, weight, gain, shift):
     return pl.pallas_call(
         lift_kernel,
         out_shape=(
             jax.ShapeDtypeStruct((C, CELLS), BF),
             jax.ShapeDtypeStruct((16, CELLS), F4),
         ),
-        scratch_shapes=[pltpu.VMEM((224, CELLS), BF), pltpu.VMEM((C, CELLS), F4)],
+        scratch_shapes=[pltpu.VMEM((224, CELLS), BF), pltpu.VMEM((C, CELLS), F4)]
+        + [pltpu.VMEM((C, 128), F4)] * 4,
         name="lift",
         compiler_params=pltpu.CompilerParams(vmem_limit_bytes=40 * MIB),
-    )(arrived, lift_weight, gain, shift)
+    )(arrived, weight, gain, shift)
 
 
 def train_kernel(
@@ -528,15 +587,23 @@
     up = [(i, (i + 1) % size) for i in range(size)]
     before = lax.ppermute(populations[1:15, 15], every, up)
     behind = lax.ppermute(populations[1:15, 0], every, [(j, i) for i, j in up])
-    after, outgoing = lattice(
-        col, populations, before, behind, relaxation, send_lists, mix_master
+    old, select, weights, lift_rows, gain, shift, out_rows = prepare(
+        col,
+        populations,
+        send_lists,
+        mix_master,
+        lift_weight,
+        norm_gain[None],
+        norm_shift[None],
+        out_weight,
     )
+    outgoing = route(populations, before, behind, old, select, weights)
     arrived = lax.all_to_all(
         outgoing.reshape(32, BLOCK_ROWS, 128), "row", split_axis=0, concat_axis=0, tiled=True
     ).reshape(32 * BLOCK_ROWS, 128)
+    after = collide(populations, before, behind, relaxation)
     other = lax.ppermute(arrived, "col", swap)
-    h, target = lift(arrived, lift_weight, norm_gain[:, None], norm_shift[:, None])
-    out_rows = jnp.pad(out_weight, ((3, 10), (0, 0)))
+    h, target = lift(arrived, lift_rows, gain, shift)
     send, keep = train(col, h, target, arrived, other, out_rows)
     half = keep + lax.ppermute(send, "col", swap)
     terms = lax.all_to_all(

time: 108 us -> 87.9 us (0.81)
  Pallas kernels: 45 us -> 29.6 us
  waiting for transfers between devices: 6.21 us -> 2.89 us
  starting transfers between devices: 13.9 us -> 12.6 us
    pallas_call x1, Pallas kernels: 32.2 us -> 22.2 us  [train(): pl.pallas_call(functools.partial(train_kernel, steps, layers), grid=(step...]
    pallas_call x1, Pallas kernels: 9.59 us -> 3.43 us  [lift(): pl.pallas_call(lift_kernel, out_shape=(jax.ShapeDtypeStruct((C, CELLS), B...]
    ppermute x1, starting transfers between devices: 2.3 us -> 0.01 us  [body(): other = lax.ppermute(arrived, 'col', swap)]
    ppermute x1, waiting for transfers between devices: 2.3 us -> 0.78 us  [body(): across = lax.ppermute(summed, 'sec', swap)]
    ppermute x1, waiting for transfers between devices: 1.33 us -> 0.01 us  [body(): before = lax.ppermute(populations[1:15, 15], every, up)]
    pallas_call x1 -> x3, Pallas kernels: 1.68 us -> 2.36 us  [the longest x1 1.06 us: collide(): pl.pallas_call(collide_kernel, out_shape=jax.ShapeDtypeStruct((19, 16, 25...]
    unnamed x15 -> x19, local copies, waits for them, and re-layouts: 4.72 us -> 4.7 us
  transfers between devices with their start and end apart: 5 -> 5, of which waited for: 4 -> 2; matrix products, arithmetic and copies ran while one was open for 3% -> 3% of each run, Pallas kernels for 9% -> 6%
where the time goes in v3:
time: 87.9 us; the launch traced here: 87 us
  blocking collectives  34 us (39%)
  Pallas kernels  29.6 us (34%)
  starting transfers between devices  12.6 us (14%)
  local copies, waits for them, and re-layouts  7.05 us (8%)
  waiting for transfers between devices  2.89 us (3%)
    pallas_call x1, Pallas kernels, train(): pl.pallas_call(functools.partial(train_kernel, steps, layers), grid=(step...  22.2 us
    all_to_all x1, blocking collectives, body(): lax.all_to_all(half.reshape(32, WEIGHT_ROWS, 128), 'row', split_axis=0, c...  19.3 us
    all_to_all x1, blocking collectives, body(): lax.all_to_all(outgoing.reshape(32, BLOCK_ROWS, 128), 'row', split_axis=0...  14.7 us
    ppermute x1, starting transfers between devices, body(): behind = lax.ppermute(populations[1:15, 0], every, [(j, i) for i, j in up])  8.27 us
    unnamed x19, local copies, waits for them, and re-layouts  4.7 us
    ppermute x1, starting transfers between devices, body(): across = lax.ppermute(summed, 'sec', swap)  3.65 us
    pallas_call x1, Pallas kernels, lift(): pl.pallas_call(lift_kernel, out_shape=(jax.ShapeDtypeStruct((C, CELLS), B...  3.43 us
    ppermute x1, waiting for transfers between devices, body(): half = keep + lax.ppermute(send, 'col', swap)  2.1 us
  transfers between devices with their start and end apart: 5, of which 2 were waited for; matrix products, arithmetic and copies ran while one was open for 3% of the time, Pallas kernels for 6%

profile of v3, /device:TPU:0, one launch (start us, length us, event | category | flops | bytes accessed | tf_op | source)
XLA Modules:
  0.0 87.0 jit_solution(14311635817062743643)
XLA Ops:
  0.6 1.0 %fusion = (f32[14,1,256]{2,1,0:T(1,128)S(1)}, f32[14,1,256]{2,1,0:T(1,128)S(1)}) fusion(f32[19,16,256]{2,1,0:T(8,128)} %pop_ref.5), kind=kLoop, calls=%fused_computation.2 | loop fusion | bytes 57344 | tf_op jit(solution)/shard_map/slice | solution.py:589
  1.6 0.1 collective-permute-start
  1.7 8.3 %collective-permute-start.1 = (f32[14,256]{1,0:T(8,128)S(1)}, f32[14,256]{1,0:T(8,128)S(1)}, u32[]{:S(2)}, u32[]{:S(2)}) collective-permute-start(f32[14,256]{1,0:T(8,128)S(1)} %bitcast.16), channel_id=1, source_target_pairs={{1,0},{2,1},{3,2},{4,3},{5,4},{6,5},{7,6},{8,7},{9,8},{10,9},{11,1... | collective-permute-start | bytes 43016 | tf_op jit(solution)/shard_map/ppermute | solution.py:589
  10.0 1.0 %copy.16.lift_ref = bf16[320,81]{1,0:T(8,128)(2,1)S(1)} copy(bf16[320,81]{0,1:T(8,128)(2,1)} %param.13) | data formatting | bytes 103680 | tf_op args[3]
  11.0 0.7 broadcast_in_dim.10.gain_ref
  11.7 0.7 broadcast_in_dim.11.shift_ref
  12.4 0.0 copy-start
  12.4 1.0 %copy-done = f32[19,16,256]{2,1,0:T(8,128)S(1)} copy-done((f32[19,16,256]{2,1,0:T(8,128)S(1)}, f32[19,16,256]{2,1,0:T(8,128)}, u32[]{:S(2)}) %copy-start) | copy-done | bytes 311320
  13.3 0.0 copy-start.2
  13.3 0.8 copy-done.2
  14.1 0.0 copy-start.4
  14.1 0.7 copy-done.4
  14.8 0.0 copy-start.5
  14.8 0.7 copy-done.5
  15.4 0.5 prepare.1
  16.0 0.0 collective-permute-done.before_ref
  16.0 0.0 collective-permute-done.1.behind_ref
  16.0 0.8 route.1
  16.8 14.7 %all_to_all.10 = bf16[32,72,128]{2,1,0:T(8,128)(2,1)S(1)} all-to-all(bf16[32,72,128]{2,1,0:T(8,128)(2,1)S(1)} %bitcast.13), channel_id=1, replica_groups=mesh['sec'=2,'row'=32,'col'=2] {'row'}, dimensions={0} | all-to-all | bytes 1179648 | tf_op jit(solution)/shard_map/all_to_all | solution.py:601
  31.5 0.0 collective-permute-start.2
  31.5 3.4 %lift.1 = (bf16[320,4096]{1,0:T(8,128)(2,1)S(1)}, f32[16,4096]{1,0:T(8,128)S(1)}) custom-call(bf16[2304,128]{1,0:T(8,128)(2,1)S(1)} %bitcast.11, bf16[320,224]{1,0:T(8,128)(2,1)S(1)} %get-tuple-element.21.weight_ref, f32[320,128]{1,0:T(8,128)S(1)} %get-tuple-element.22.gain_ref, f32[320,128]{1,0:T(8,128)S(1)} %get-tuple-element.23.shift_ref), custom_call_target="tpu_custom_call" | custom-call | tf_op jit(solution)/shard_map/lift/pallas_call | solution.py:378
  35.0 0.0 collective-permute-done.2.other_ref
  35.0 22.2 %train.1 = (f32[1792,128]{1,0:T(8,128)S(1)}, f32[1792,128]{1,0:T(8,128)S(1)}) custom-call(s32[1]{0:T(128)} %bitcast.2.col_ref, bf16[320,4096]{1,0:T(8,128)(2,1)S(1)} %get-tuple-element.24.h_ref, f32[16,4096]{1,0:T(8,128)S(1)} %get-tuple-element.25.target_ref, bf16[2304,128]{1,0:T(8,128)(2,1)S(1)} %bitcast.12, ...), custom_call_target="tpu_custom_call" | custom-call | tf_op jit(solution)/shard_map/train/pallas_call | solution.py:507
  57.2 0.6 collective-permute-start.3
  57.8 2.1 %collective-permute-done.3 = f32[1792,128]{1,0:T(8,128)S(1)} collective-permute-done((f32[1792,128]{1,0:T(8,128)S(1)}, f32[1792,128]{1,0:T(8,128)S(1)}, u32[]{:S(2)}, u32[]{:S(2)}) %collective-permute-start.3) | collective-permute-done | bytes 917536 | tf_op jit(solution)/shard_map/ppermute | solution.py:608
  59.9 0.0 copy-start.1
  59.9 0.0 copy-start.3
  59.9 0.1 add.3
  60.0 19.3 %all_to_all.11 = f32[32,56,128]{2,1,0:T(8,128)S(1)} all-to-all(f32[32,56,128]{2,1,0:T(8,128)S(1)} %bitcast.14), channel_id=1, replica_groups=mesh['sec'=2,'row'=32,'col'=2] {'row'}, dimensions={0} | all-to-all | bytes 1835008 | tf_op jit(solution)/shard_map/all_to_all | solution.py:609
  79.3 0.1 reduce_sum.9.own_ref
  79.3 0.0 copy-start.6
  79.4 3.6 %collective-permute-start.4 = (f32[56,128]{1,0:T(8,128)S(1)}, f32[56,128]{1,0:T(8,128)S(1)}, u32[]{:S(2)}, u32[]{:S(2)}) collective-permute-start(f32[56,128]{1,0:T(8,128)S(1)} %reduce_sum.9.own_ref), channel_id=1, source_target_pairs={{0,64},{64,0},{1,65},{65,1},{2,66},{66,2},{3,67},{67,3},{4,68},{68... | collective-permute-start | bytes 86024 | tf_op jit(solution)/shard_map/ppermute | solution.py:613
  83.0 0.0 copy-done.1
  83.0 0.0 copy-done.3
  83.0 1.1 %collide.1 = f32[19,16,256]{2,1,0:T(8,128)} custom-call(f32[19,16,256]{2,1,0:T(8,128)S(1)} %copy-done.1, f32[14,256]{1,0:T(8,128)S(1)} %collective-permute-done.before_ref, f32[14,256]{1,0:T(8,128)S(1)} %collective-permute-done.1.behind_ref, f32[16,256]{1,0:T(8,128)S(1)} %copy-done.3), custom_call_target="tpu_custom_call" | custom-call | flops 10000000 | bytes 4000000 | tf_op jit(solution)/shard_map/collide/pallas_call | solution.py:282
  84.1 0.8 collective-permute-done.4.other_ref
  84.9 0.0 copy-done.6
  84.9 0.0 copy-start.7
  84.9 0.6 copy-done.7
  85.5 1.6 %update.1 = (f32[20,320]{1,0:T(8,128)}, f32[20,320]{1,0:T(8,128)}, f32[20,320]{1,0:T(8,128)}) custom-call(s32[1]{0:T(128)} %bitcast.2.col_ref, f32[56,128]{1,0:T(8,128)} %copy-done.6, f32[56,128]{1,0:T(8,128)} %copy-done.7, f32[20,320]{1,0:T(8,128)} %master_ref.1, f32[20,320]{1,0:T(8,128)} %first_ref.1, f32[20,320]{1,0:T(8,128)} %second_ref.1), custom_call_target="tpu_custom_call" | custom-call | tf_op jit(solution)/shard_map/update/pallas_call | solution.py:562
  (2 shorter events, 0.0 us)
Async XLA Ops:
  1.6 14.3 %collective-permute-start = (f32[14,256]{1,0:T(8,128)S(1)}, f32[14,256]{1,0:T(8,128)S(1)}, u32[]{:S(2)}, u32[]{:S(2)}) collective-permute-start(f32[14,256]{1,0:T(8,128)S(1)} %bitcast.15), channel_id=1, source_target_pairs={{0,1},{1,2},{2,3},{3,4},{4,5},{5,6},{6,7},{7,8},{8,9},{9,10},{10,1... | collective-permute-start | bytes 43016 | tf_op jit(solution)/shard_map/ppermute | solution.py:588
  1.7 14.3 %collective-permute-start.1 = (f32[14,256]{1,0:T(8,128)S(1)}, f32[14,256]{1,0:T(8,128)S(1)}, u32[]{:S(2)}, u32[]{:S(2)}) collective-permute-start(f32[14,256]{1,0:T(8,128)S(1)} %bitcast.16), channel_id=1, source_target_pairs={{1,0},{2,1},{3,2},{4,3},{5,4},{6,5},{7,6},{8,7},{9,8},{10,9},{11,1... | collective-permute-start | bytes 43016 | tf_op jit(solution)/shard_map/ppermute | solution.py:589
  12.4 1.0 %copy-start = (f32[19,16,256]{2,1,0:T(8,128)S(1)}, f32[19,16,256]{2,1,0:T(8,128)}, u32[]{:S(2)}) copy-start(f32[19,16,256]{2,1,0:T(8,128)} %pop_ref.5) | copy-start | bytes 933892
  13.3 0.8 copy-start.2
  14.1 0.7 copy-start.4
  14.8 0.7 copy-start.5
  31.5 3.4 %collective-permute-start.2 = (bf16[2304,128]{1,0:T(8,128)(2,1)S(1)}, bf16[2304,128]{1,0:T(8,128)(2,1)S(1)}, u32[]{:S(2)}, u32[]{:S(2)}) collective-permute-start(bf16[2304,128]{1,0:T(8,128)(2,1)S(1)} %bitcast.10), channel_id=1, source_target_pairs={{0,1},{1,0},{2,3},{3,2},{4,5},{5,4},{6,7},{7,6},{8,9},{9,8},{10,11... | collective-permute-start | bytes 1769480 | tf_op jit(solution)/shard_map/ppermute | solution.py:605
  57.2 2.7 %collective-permute-start.3 = (f32[1792,128]{1,0:T(8,128)S(1)}, f32[1792,128]{1,0:T(8,128)S(1)}, u32[]{:S(2)}, u32[]{:S(2)}) collective-permute-start(f32[1792,128]{1,0:T(8,128)S(1)} %get-tuple-element.28), channel_id=1, source_target_pairs={{0,1},{1,0},{2,3},{3,2},{4,5},{5,4},{6,7},{7,6},{8,9},{9,8},{10,11... | collective-permute-start | bytes 2752520 | tf_op jit(solution)/shard_map/ppermute | solution.py:608
  59.9 23.1 %copy-start.1 = (f32[19,16,256]{2,1,0:T(8,128)S(1)}, f32[19,16,256]{2,1,0:T(8,128)}, u32[]{:S(2)}) copy-start(f32[19,16,256]{2,1,0:T(8,128)} %pop_ref.5) | copy-start | bytes 933892
  59.9 23.1 %copy-start.3 = (f32[16,256]{1,0:T(8,128)S(1)}, f32[16,256]{1,0:T(8,128)}, u32[]{:S(2)}) copy-start(f32[16,256]{1,0:T(8,128)} %relax_ref.1) | copy-start | bytes 49156
  79.3 5.5 %copy-start.6 = (f32[56,128]{1,0:T(8,128)}, f32[56,128]{1,0:T(8,128)S(1)}, u32[]{:S(2)}) copy-start(f32[56,128]{1,0:T(8,128)S(1)} %reduce_sum.9.own_ref) | copy-start | bytes 86020
  79.4 5.5 %collective-permute-start.4 = (f32[56,128]{1,0:T(8,128)S(1)}, f32[56,128]{1,0:T(8,128)S(1)}, u32[]{:S(2)}, u32[]{:S(2)}) collective-permute-start(f32[56,128]{1,0:T(8,128)S(1)} %reduce_sum.9.own_ref), channel_id=1, source_target_pairs={{0,64},{64,0},{1,65},{65,1},{2,66},{66,2},{3,67},{67,3},{4,68},{68... | collective-permute-start | bytes 86024 | tf_op jit(solution)/shard_map/ppermute | solution.py:613
  84.9 0.6 copy-start.7

commit v4 on v3

--- a/solution.py
+++ b/solution.py
@@ -136,15 +136,37 @@
     )
 
 
+def planes_kernel(pop_ref, last_ref, initial_ref, own_ref):
+    own_ref[...] = pop_ref[...]
+    for index in range(1, 15):
+        last_ref[index - 1 : index, :] = pop_ref[index, 15:16, :]
+        initial_ref[index - 1 : index, :] = pop_ref[index, 0:1, :]
+
+
+def planes(populations):
+    return pl.pallas_call(
+        planes_kernel,
+        out_shape=(jax.ShapeDtypeStruct((14, 256), F4),) * 2
+        + (jax.ShapeDtypeStruct((19, 16, 256), F4),),
+        name="planes",
+        compiler_params=pltpu.CompilerParams(vmem_limit_bytes=16 * MIB),
+    )(populations)
+
+
+def gathered_rows(gain, shift, lists, out_weight, master, lift_weight):
+    def placed(array, start):
+        rows, lanes = array.shape
+        return jnp.pad(array, ((start, 120 - start - rows), (0, C - lanes))).astype(F4)
+
+    row = iota((120, C), 0)
+    total = placed(lists, 2) + placed(out_weight, 3) + placed(master, 8) + placed(lift_weight.T, 32)
+    return jnp.where(row == 0, gain, jnp.where(row == 1, shift, total))
+
+
 def prepare_kernel(
     col_ref,
     pop_ref,
-    lists_ref,
-    mix_ref,
-    lift_ref,
-    gain_ref,
-    shift_ref,
-    out_ref,
+    small_ref,
     old_ref,
     select_ref,
     weights_ref,
@@ -153,46 +175,51 @@
     shift_out,
     rows_out,
     window,
-    rows,
 ):
     unused, old_flow = moments([pop_ref[index] for index in range(19)])
     old_ref[...] = jnp.concatenate(old_flow, axis=0).astype(BF)
-    select_ref[...] = route_rows(lists_ref[...])
+    select_ref[...] = route_rows(small_ref[2:3, 0:32])
     col = col_ref[0]
     window[...] = jnp.zeros_like(window)
 
     @pl.when(col == 0)
     def _():
-        window[0:20, 0:C] = mix_ref[...]
+        window[0:20, 0:C] = small_ref[8:28, :]
 
     @pl.when(col != 0)
     def _():
-        window[4:24, 0:C] = mix_ref[...]
+        window[4:24, 0:C] = small_ref[8:28, :]
 
     def tile(index, lanes):
         start = pl.multiple_of((index * 8 + 8 * col) % 24, 8)
         return window[pl.ds(start, 8), lanes * 128 : (lanes + 1) * 128]
 
     weights_ref[...] = jnp.concatenate(pack_piece(tile, own_half(col)), axis=0)
-    column = iota((81, 224), 1)
+    column = iota((88, 224), 1)
     feature = (column & 7) * 27 + (column >> 3)
     valid = ((column & 7) < 3) & (column < 216)
-    spread = jnp.where(valid & (iota((81, 224), 0) == feature), 1.0, 0.0).astype(BF)
-    lift_out[...] = jnp.dot(lift_ref[...], spread, preferred_element_type=F4).astype(BF)
+    spread = jnp.where(valid & (iota((88, 224), 0) == feature), 1.0, 0.0).astype(BF)
+    lift_out[...] = lax.dot_general(
+        small_ref[32:120, :].astype(BF),
+        spread,
+        (((0,), (0,)), ((), ())),
+        preferred_element_type=F4,
+    ).astype(BF)
     same = iota((C, C), 0) == iota((C, C), 1)
-    for source, target in ((gain_ref, gain_out), (shift_ref, shift_out)):
-        down = jnp.sum(jnp.where(same, source[...], 0.0), axis=1, keepdims=True)
+    for index, target in ((0, gain_out), (1, shift_out)):
+        across = small_ref[index : index + 1, :]
+        down = jnp.sum(jnp.where(same, across, 0.0), axis=1, keepdims=True)
         target[...] = jnp.broadcast_to(down, (C, 128))
-    rows[...] = jnp.zeros_like(rows)
-    rows[3:6, :] = out_ref[...].astype(F4)
-    rows_out[...] = rows[...].astype(BF)
-
-
-def prepare(col, populations, lists, master, lift_weight, gain, shift, out_weight):
+    row = iota((8, C), 0)
+    rows = jnp.where((row >= 3) & (row < 6), small_ref[0:8, :], 0.0)
+    rows_out[...] = jnp.concatenate([rows, jnp.zeros_like(rows)], axis=0).astype(BF)
+
+
+def prepare(col, populations, small):
     vector = pl.BlockSpec(memory_space=pltpu.VMEM)
     return pl.pallas_call(
         prepare_kernel,
-        in_specs=[pl.BlockSpec(memory_space=pltpu.SMEM)] + [vector] * 7,
+        in_specs=[pl.BlockSpec(memory_space=pltpu.SMEM)] + [vector] * 2,
         out_specs=(vector,) * 7,
         out_shape=(
             jax.ShapeDtypeStruct((48, 256), BF),
@@ -203,11 +230,11 @@
             jax.ShapeDtypeStruct((C, 128), F4),
             jax.ShapeDtypeStruct((16, C), BF),
         ),
-        scratch_shapes=[pltpu.VMEM((24, WIDE), F4), pltpu.VMEM((16, C), F4)],
+        scratch_shapes=[pltpu.VMEM((24, WIDE), F4)],
         name="prepare",
         cost_estimate=pl.CostEstimate(flops=10**7, bytes_accessed=4 * 10**6, transcendentals=0),
         compiler_params=pltpu.CompilerParams(vmem_limit_bytes=16 * MIB),
-    )(col, populations, lists, master, lift_weight, gain, shift, out_weight)
+    )(col, populations, small)
 
 
 def streamed(pop_ref, before_ref, behind_ref):
@@ -258,7 +285,18 @@
     )(populations, before, behind, old, select, weights)
 
 
-def collide_kernel(pop_ref, before_ref, behind_ref, relax_ref, after_ref):
+def collide_kernel(
+    pop_ref,
+    before_ref,
+    behind_ref,
+    relax_ref,
+    master_ref,
+    first_ref,
+    second_ref,
+    after_ref,
+    state_ref,
+):
+    state_ref[0], state_ref[1], state_ref[2] = master_ref[...], first_ref[...], second_ref[...]
     read = streamed(pop_ref, before_ref, behind_ref)
     density, flow = moments(read)
     speed = flow[0] * flow[0] + flow[1] * flow[1] + flow[2] * flow[2]
@@ -278,14 +316,17 @@
         after_ref[index] = read[index] - relaxation * (read[index] - balance)
 
 
-def collide(populations, before, behind, relaxation):
+def collide(populations, before, behind, relaxation, *state):
     return pl.pallas_call(
         collide_kernel,
-        out_shape=jax.ShapeDtypeStruct((19, 16, 256), F4),
+        out_shape=(
+            jax.ShapeDtypeStruct((19, 16, 256), F4),
+            jax.ShapeDtypeStruct((3, 20, C), F4),
+        ),
         name="collide",
         cost_estimate=pl.CostEstimate(flops=10**7, bytes_accessed=4 * 10**6, transcendentals=0),
         compiler_params=pltpu.CompilerParams(vmem_limit_bytes=16 * MIB),
-    )(populations, before, behind, relaxation)
+    )(populations, before, behind, relaxation, *state)
 
 
 def lift_kernel(
@@ -538,9 +579,7 @@
     )(col, h, target, mine, other, out_weight)
 
 
-def update_kernel(
-    col_ref, own_ref, other_ref, master_ref, first_ref, second_ref, new_ref, first_out, second_out
-):
+def update_kernel(col_ref, own_ref, other_ref, state_ref, new_ref, first_out, second_out):
     packed = own_ref[...] + other_ref[...]
     parts = unpack_piece([packed[index * 8 : index * 8 + 8] for index in range(7)])
     full, rest, half = [jnp.concatenate(part, axis=1) for part in parts]
@@ -548,24 +587,24 @@
     lower = jnp.concatenate([full, rest, half], axis=0)
     upper = pltpu.roll(jnp.concatenate([half, full, rest], axis=0), 20, 0)
     gradient = jnp.where(even, lower, upper)[0:20, 0:C]
-    master = master_ref[...]
-    first_next = 0.9 * first_ref[...] + 0.1 * gradient
-    second_next = 0.999 * second_ref[...] + 0.001 * gradient * gradient
+    master = state_ref[0]
+    first_next = 0.9 * state_ref[1] + 0.1 * gradient
+    second_next = 0.999 * state_ref[2] + 0.001 * gradient * gradient
     ratio = first_next / (1.0 - 0.9**10) / (jnp.sqrt(second_next / (1.0 - 0.999**10)) + 1e-08)
     new_ref[...] = master - 0.01 * (ratio + 0.1 * master)
     first_out[...] = first_next
     second_out[...] = second_next
 
 
-def update(col, own, other, master, first, second):
+def update(col, own, other, state):
     vector = pl.BlockSpec(memory_space=pltpu.VMEM)
     return pl.pallas_call(
         update_kernel,
-        in_specs=[pl.BlockSpec(memory_space=pltpu.SMEM)] + [vector] * 5,
+        in_specs=[pl.BlockSpec(memory_space=pltpu.SMEM)] + [vector] * 3,
         out_specs=(vector,) * 3,
-        out_shape=(jax.ShapeDtypeStruct(master.shape, F4),) * 3,
+        out_shape=(jax.ShapeDtypeStruct((20, C), F4),) * 3,
         name="update",
-    )(col, own, other, master, first, second)
+    )(col, own, other, state)
 
 
 def body(
@@ -585,23 +624,18 @@
     swap = [(0, 1), (1, 0)]
     col = lax.axis_index("col").astype(I4)[None]
     up = [(i, (i + 1) % size) for i in range(size)]
-    before = lax.ppermute(populations[1:15, 15], every, up)
-    behind = lax.ppermute(populations[1:15, 0], every, [(j, i) for i, j in up])
-    old, select, weights, lift_rows, gain, shift, out_rows = prepare(
-        col,
-        populations,
-        send_lists,
-        mix_master,
-        lift_weight,
-        norm_gain[None],
-        norm_shift[None],
-        out_weight,
-    )
+    last, initial, populations = planes(populations)
+    before = lax.ppermute(last, every, up)
+    behind = lax.ppermute(initial, every, [(j, i) for i, j in up])
+    small = gathered_rows(norm_gain, norm_shift, send_lists, out_weight, mix_master, lift_weight)
+    old, select, weights, lift_rows, gain, shift, out_rows = prepare(col, populations, small)
     outgoing = route(populations, before, behind, old, select, weights)
     arrived = lax.all_to_all(
         outgoing.reshape(32, BLOCK_ROWS, 128), "row", split_axis=0, concat_axis=0, tiled=True
     ).reshape(32 * BLOCK_ROWS, 128)
-    after = collide(populations, before, behind, relaxation)
+    after, state = collide(
+        populations, before, behind, relaxation, mix_master, mix_first, mix_second
+    )
     other = lax.ppermute(arrived, "col", swap)
     h, target = lift(arrived, lift_rows, gain, shift)
     send, keep = train(col, h, target, arrived, other, out_rows)
@@ -611,9 +645,7 @@
     )
     summed = jnp.sum(terms, axis=0)
     across = lax.ppermute(summed, "sec", swap)
-    new_master, new_first, new_second = update(
-        col, summed, across, mix_master, mix_first, mix_second
-    )
+    new_master, new_first, new_second = update(col, summed, across, state)
     return (after, new_master, new_first, new_second)
 
 

time: 87.9 us -> 84.7 us (0.964)
  local copies, waits for them, and re-layouts: 7.05 us -> 2.24 us
  other arithmetic: 0.16 us -> 1.2 us
  starting transfers between devices: 12.6 us -> 13.6 us
    unnamed x19 -> x16, local copies, waits for them, and re-layouts: 4.7 us -> 2.24 us
    ppermute x1, starting transfers between devices: 0.01 us -> 2.21 us  [body(): other = lax.ppermute(arrived, 'col', swap)]
    broadcast_in_dim x2 -> x0, local copies, waits for them, and re-layouts: 1.37 us -> none  [the longest x1 0.68 us: body(): norm_gain[None]]
    select_n x0 -> x1, other arithmetic: none -> 1.04 us  [gathered_rows(): return jnp.where(row == 0, gain, jnp.where(row == 1, shift, total))]
    slice x1 -> x0, local copies, waits for them, and re-layouts: 0.98 us -> none  [body(): behind = lax.ppermute(populations[1:15, 0], every, [(j, i) for i, j in up])]
  transfers between devices with their start and end apart: 5 -> 5, of which waited for: 2 -> 2; matrix products, arithmetic and copies ran while one was open for 3% -> 1% of each run, Pallas kernels for 6% -> 6%
where the time goes in v4:
time: 84.7 us; the launch traced here: 84.3 us
  blocking collectives  33.5 us (40%)
  Pallas kernels  29.8 us (35%)
  starting transfers between devices  13.6 us (16%)
  waiting for transfers between devices  3.24 us (4%)
  local copies, waits for them, and re-layouts  2.24 us (3%)
  other arithmetic  1.2 us (1%)
    pallas_call x1, Pallas kernels, train(): pl.pallas_call(functools.partial(train_kernel, steps, layers), grid=(step...  22.2 us
    all_to_all x1, blocking collectives, body(): lax.all_to_all(half.reshape(32, WEIGHT_ROWS, 128), 'row', split_axis=0, c...  19.3 us
    all_to_all x1, blocking collectives, body(): lax.all_to_all(outgoing.reshape(32, BLOCK_ROWS, 128), 'row', split_axis=0...  14.2 us
    ppermute x1, starting transfers between devices, body(): behind = lax.ppermute(initial, every, [(j, i) for i, j in up])  8.27 us
    pallas_call x1, Pallas kernels, lift(): pl.pallas_call(lift_kernel, out_shape=(jax.ShapeDtypeStruct((C, CELLS), B...  3.43 us
    ppermute x1, starting transfers between devices, body(): across = lax.ppermute(summed, 'sec', swap)  2.96 us
    ppermute x1, waiting for transfers between devices, body(): half = keep + lax.ppermute(send, 'col', swap)  2.46 us
    unnamed x16, local copies, waits for them, and re-layouts  2.24 us
  transfers between devices with their start and end apart: 5, of which 2 were waited for; matrix products, arithmetic and copies ran while one was open for 1% of the time, Pallas kernels for 6%

profile of v4, /device:TPU:0, one launch (start us, length us, event | category | flops | bytes accessed | tf_op | source)
XLA Modules:
  0.0 84.3 jit_solution(17459062238359441078)
XLA Ops:
  0.6 0.0 copy-start
  0.6 1.0 %copy-done = f32[19,16,256]{2,1,0:T(8,128)S(1)} copy-done((f32[19,16,256]{2,1,0:T(8,128)S(1)}, f32[19,16,256]{2,1,0:T(8,128)}, u32[]{:S(2)}) %copy-start) | copy-done | bytes 311320
  1.6 0.1 collective-permute-start
  1.7 8.3 %collective-permute-start.1 = (f32[14,256]{1,0:T(8,128)S(1)}, f32[14,256]{1,0:T(8,128)S(1)}, u32[]{:S(2)}, u32[]{:S(2)}) collective-permute-start(f32[14,256]{1,0:T(8,128)S(1)} %get-tuple-element.25), channel_id=1, source_target_pairs={{1,0},{2,1},{3,2},{4,3},{5,4},{6,5},{7,6},{8,7},{9,8},{10,9},{11,1... | collective-permute-start | bytes 43016 | tf_op jit(solution)/shard_map/ppermute | solution.py:629
  10.0 1.0 %select_select_fusion.small_ref = f32[120,320]{1,0:T(8,128)S(1)} fusion(f32[20,320]{1,0:T(8,128)} %master_ref.1, s32[1,32]{1,0:T(1,128)} %param.12, bf16[81,320]{1,0:T(8,128)(2,1)} %bitcast.10, bf16[3,320]{1,0:T(4,128)(2,1)} %param.19, f32[320]{0:T(512)} %param.15, f32[320]{0:T(512)} %param.14, pred[120]{0:T(512)(128)(4,1)S(1)} %get-tuple-element.42, ...), kind=kLoop, calls=%fused_computation | loop fusion | flops 307200 | bytes 235888 | tf_op jit(solution)/shard_map/jit(_where)/select_n | solution.py:163
  11.1 0.6 prepare.1
  11.6 0.0 collective-permute-done.before_ref
  11.6 0.0 collective-permute-done.1.behind_ref
  11.6 0.8 route.1
  12.4 14.2 %all_to_all.10 = bf16[32,72,128]{2,1,0:T(8,128)(2,1)S(1)} all-to-all(bf16[32,72,128]{2,1,0:T(8,128)(2,1)S(1)} %bitcast.8), channel_id=1, replica_groups=mesh['sec'=2,'row'=32,'col'=2] {'row'}, dimensions={0} | all-to-all | bytes 1179648 | tf_op jit(solution)/shard_map/all_to_all | solution.py:633
  26.7 2.2 %collective-permute-start.2 = (bf16[2304,128]{1,0:T(8,128)(2,1)S(1)}, bf16[2304,128]{1,0:T(8,128)(2,1)S(1)}, u32[]{:S(2)}, u32[]{:S(2)}) collective-permute-start(bf16[2304,128]{1,0:T(8,128)(2,1)S(1)} %bitcast.5), channel_id=1, source_target_pairs={{0,1},{1,0},{2,3},{3,2},{4,5},{5,4},{6,7},{7,6},{8,9},{9,8},{10,11... | collective-permute-start | bytes 1769480 | tf_op jit(solution)/shard_map/ppermute | solution.py:639
  28.9 3.4 %lift.1 = (bf16[320,4096]{1,0:T(8,128)(2,1)S(1)}, f32[16,4096]{1,0:T(8,128)S(1)}) custom-call(bf16[2304,128]{1,0:T(8,128)(2,1)S(1)} %bitcast.6, bf16[320,224]{1,0:T(8,128)(2,1)S(1)} %get-tuple-element.30.weight_ref, f32[320,128]{1,0:T(8,128)S(1)} %get-tuple-element.31.gain_ref, f32[320,128]{1,0:T(8,128)S(1)} %get-tuple-element.32.shift_ref), custom_call_target="tpu_custom_call" | custom-call | tf_op jit(solution)/shard_map/lift/pallas_call | solution.py:419
  32.3 0.0 collective-permute-done.2.other_ref
  32.3 22.2 %train.1 = (f32[1792,128]{1,0:T(8,128)S(1)}, f32[1792,128]{1,0:T(8,128)S(1)}) custom-call(s32[1]{0:T(128)} %bitcast.col_ref, bf16[320,4096]{1,0:T(8,128)(2,1)S(1)} %get-tuple-element.33.h_ref, f32[16,4096]{1,0:T(8,128)S(1)} %get-tuple-element.34.target_ref, bf16[2304,128]{1,0:T(8,128)(2,1)S(1)} %bitcast.7, ...), custom_call_target="tpu_custom_call" | custom-call | tf_op jit(solution)/shard_map/train/pallas_call | solution.py:548
  54.6 0.1 collective-permute-start.3
  54.7 2.5 %collective-permute-done.3 = f32[1792,128]{1,0:T(8,128)S(1)} collective-permute-done((f32[1792,128]{1,0:T(8,128)S(1)}, f32[1792,128]{1,0:T(8,128)S(1)}, u32[]{:S(2)}, u32[]{:S(2)}) %collective-permute-start.3) | collective-permute-done | bytes 917536 | tf_op jit(solution)/shard_map/ppermute | solution.py:642
  57.1 0.0 copy-start.1
  57.1 0.0 copy-start.3
  57.1 0.0 copy-start.4
  57.1 0.0 copy-start.5
  57.1 0.1 add.23
  57.2 19.3 %all_to_all.11 = f32[32,56,128]{2,1,0:T(8,128)S(1)} all-to-all(f32[32,56,128]{2,1,0:T(8,128)S(1)} %bitcast.9), channel_id=1, replica_groups=mesh['sec'=2,'row'=32,'col'=2] {'row'}, dimensions={0} | all-to-all | bytes 1835008 | tf_op jit(solution)/shard_map/all_to_all | solution.py:643
  76.5 0.1 reduce_sum.9.own_ref
  76.6 0.0 copy-start.6
  76.6 3.0 %collective-permute-start.4 = (f32[56,128]{1,0:T(8,128)S(1)}, f32[56,128]{1,0:T(8,128)S(1)}, u32[]{:S(2)}, u32[]{:S(2)}) collective-permute-start(f32[56,128]{1,0:T(8,128)S(1)} %reduce_sum.9.own_ref), channel_id=1, source_target_pairs={{0,64},{64,0},{1,65},{65,1},{2,66},{66,2},{3,67},{67,3},{4,68},{68... | collective-permute-start | bytes 86024 | tf_op jit(solution)/shard_map/ppermute | solution.py:647
  79.6 0.0 copy-done.1
  79.6 0.0 copy-done.3
  79.6 0.0 copy-done.4
  79.6 0.0 copy-done.5
  79.6 1.1 %collide.1 = (f32[19,16,256]{2,1,0:T(8,128)}, f32[3,20,320]{2,1,0:T(8,128)S(1)}) custom-call(f32[19,16,256]{2,1,0:T(8,128)S(1)} %get-tuple-element.23.pop_ref, f32[14,256]{1,0:T(8,128)S(1)} %collective-permute-done.before_ref, f32[14,256]{1,0:T(8,128)S(1)} %collective-permute-done.1.behind_ref, f32[16,256]{1,0:T(8,128)S(1)} %copy-done.5, ...), custom_call_target="tpu_custom_call" | custom-call | flops 10000000 | bytes 4000000 | tf_op jit(solution)/shard_map/collide/pallas_call | solution.py:320
  80.7 0.0 copy-start.2
  80.7 0.6 copy-done.2
  81.3 0.8 collective-permute-done.4.other_ref
  82.1 0.0 copy-start.7
  82.1 0.0 copy-done.6
  82.1 0.6 copy-done.7
  82.7 1.7 %update.1 = (f32[20,320]{1,0:T(8,128)}, f32[20,320]{1,0:T(8,128)}, f32[20,320]{1,0:T(8,128)}) custom-call(s32[1]{0:T(128)} %bitcast.col_ref, f32[56,128]{1,0:T(8,128)} %copy-done.6, f32[56,128]{1,0:T(8,128)} %copy-done.7, f32[3,20,320]{2,1,0:T(8,128)} %copy-done.2), custom_call_target="tpu_custom_call" | custom-call | tf_op jit(solution)/shard_map/update/pallas_call | solution.py:601
  (2 shorter events, 0.0 us)
Async XLA Ops:
  0.6 1.0 %copy-start = (f32[19,16,256]{2,1,0:T(8,128)S(1)}, f32[19,16,256]{2,1,0:T(8,128)}, u32[]{:S(2)}) copy-start(f32[19,16,256]{2,1,0:T(8,128)} %pop_ref.1) | copy-start | bytes 933892
  1.6 10.0 %collective-permute-start = (f32[14,256]{1,0:T(8,128)S(1)}, f32[14,256]{1,0:T(8,128)S(1)}, u32[]{:S(2)}, u32[]{:S(2)}) collective-permute-start(f32[14,256]{1,0:T(8,128)S(1)} %get-tuple-element.24), channel_id=1, source_target_pairs={{0,1},{1,2},{2,3},{3,4},{4,5},{5,6},{6,7},{7,8},{8,9},{9,10},{10,1... | collective-permute-start | bytes 43016 | tf_op jit(solution)/shard_map/ppermute | solution.py:628
  1.7 9.9 %collective-permute-start.1 = (f32[14,256]{1,0:T(8,128)S(1)}, f32[14,256]{1,0:T(8,128)S(1)}, u32[]{:S(2)}, u32[]{:S(2)}) collective-permute-start(f32[14,256]{1,0:T(8,128)S(1)} %get-tuple-element.25), channel_id=1, source_target_pairs={{1,0},{2,1},{3,2},{4,3},{5,4},{6,5},{7,6},{8,7},{9,8},{10,9},{11,1... | collective-permute-start | bytes 43016 | tf_op jit(solution)/shard_map/ppermute | solution.py:629
  26.7 5.7 %collective-permute-start.2 = (bf16[2304,128]{1,0:T(8,128)(2,1)S(1)}, bf16[2304,128]{1,0:T(8,128)(2,1)S(1)}, u32[]{:S(2)}, u32[]{:S(2)}) collective-permute-start(bf16[2304,128]{1,0:T(8,128)(2,1)S(1)} %bitcast.5), channel_id=1, source_target_pairs={{0,1},{1,0},{2,3},{3,2},{4,5},{5,4},{6,7},{7,6},{8,9},{9,8},{10,11... | collective-permute-start | bytes 1769480 | tf_op jit(solution)/shard_map/ppermute | solution.py:639
  54.6 2.6 %collective-permute-start.3 = (f32[1792,128]{1,0:T(8,128)S(1)}, f32[1792,128]{1,0:T(8,128)S(1)}, u32[]{:S(2)}, u32[]{:S(2)}) collective-permute-start(f32[1792,128]{1,0:T(8,128)S(1)} %get-tuple-element.37), channel_id=1, source_target_pairs={{0,1},{1,0},{2,3},{3,2},{4,5},{5,4},{6,7},{7,6},{8,9},{9,8},{10,11... | collective-permute-start | bytes 2752520 | tf_op jit(solution)/shard_map/ppermute | solution.py:642
  57.1 22.5 %copy-start.1 = (f32[20,320]{1,0:T(8,128)S(1)}, f32[20,320]{1,0:T(8,128)}, u32[]{:S(2)}) copy-start(f32[20,320]{1,0:T(8,128)} %master_ref.1) | copy-start | bytes 76804
  57.1 22.5 %copy-start.3 = (f32[20,320]{1,0:T(8,128)S(1)}, f32[20,320]{1,0:T(8,128)}, u32[]{:S(2)}) copy-start(f32[20,320]{1,0:T(8,128)} %first_ref.1) | copy-start | bytes 76804
  57.1 22.5 %copy-start.4 = (f32[20,320]{1,0:T(8,128)S(1)}, f32[20,320]{1,0:T(8,128)}, u32[]{:S(2)}) copy-start(f32[20,320]{1,0:T(8,128)} %second_ref.1) | copy-start | bytes 76804
  57.1 22.5 %copy-start.5 = (f32[16,256]{1,0:T(8,128)S(1)}, f32[16,256]{1,0:T(8,128)}, u32[]{:S(2)}) copy-start(f32[16,256]{1,0:T(8,128)} %relax_ref.1) | copy-start | bytes 49156
  76.6 5.5 %copy-start.6 = (f32[56,128]{1,0:T(8,128)}, f32[56,128]{1,0:T(8,128)S(1)}, u32[]{:S(2)}) copy-start(f32[56,128]{1,0:T(8,128)S(1)} %reduce_sum.9.own_ref) | copy-start | bytes 86020
  76.6 5.5 %collective-permute-start.4 = (f32[56,128]{1,0:T(8,128)S(1)}, f32[56,128]{1,0:T(8,128)S(1)}, u32[]{:S(2)}, u32[]{:S(2)}) collective-permute-start(f32[56,128]{1,0:T(8,128)S(1)} %reduce_sum.9.own_ref), channel_id=1, source_target_pairs={{0,64},{64,0},{1,65},{65,1},{2,66},{66,2},{3,67},{67,3},{4,68},{68... | collective-permute-start | bytes 86024 | tf_op jit(solution)/shard_map/ppermute | solution.py:647
  80.7 0.6 copy-start.2
  82.1 0.6 copy-start.7

commit v5 on v4

--- a/solution.py
+++ b/solution.py
@@ -501,26 +501,34 @@
                 value, slope = gelu_both(ahead[rows, part])
                 slopes[layer, rows, part] = slope
                 states[layer, rows, part] = (state(layer)[rows, part].astype(F4) + value).astype(BF)
+    def descend(layer, part, change, first):
+        for start in range(0, C, 16):
+            rows = slice(start, start + 16)
+            value = change[start : start + 16]
+            if not first:
+                value = back[rows, part] + value
+            if layer > 0:
+                back[rows, part] = value
+            inner[layer, rows, part] = (value * slopes[layer, rows, part]).astype(BF)
+
     for part in parts:
         output = jnp.dot(out_ref[...], states[layers - 1, :, part], preferred_element_type=F4)
         delta = ((output - target_ref[:, part]) * (2.0 / 384.0)).astype(BF)
-        back[:, part] = lax.dot_general(
+        change = lax.dot_general(
             out_ref[...], delta, (((0,), (0,)), ((), ())), preferred_element_type=F4
         )
+        descend(layers - 1, part, change, True)
     for layer in range(layers - 1, -1, -1):
         rows_of = slice(layer * C, (layer + 1) * C)
-        for part in parts:
-            for start in range(0, C, 16):
-                rows = slice(start, start + 16)
-                inner[layer, rows, part] = (back[rows, part] * slopes[layer, rows, part]).astype(BF)
-        if layer > 0:
-            for part in parts:
-                back[:, part] += jnp.dot(
-                    mix_back[rows_of, :], inner[layer, :, part], preferred_element_type=F4
-                )
         total[rows_of, 0:C] += lax.dot_general(
             inner[layer], state(layer)[...], (((1,), (1,)), ((), ())), preferred_element_type=F4
         )
+        if layer > 0:
+            for part in parts:
+                change = jnp.dot(
+                    mix_back[rows_of, :], inner[layer, :, part], preferred_element_type=F4
+                )
+                descend(layer - 1, part, change, False)
 
     @pl.when(step == steps - 1)
     def _():
@@ -604,6 +612,7 @@
         out_specs=(vector,) * 3,
         out_shape=(jax.ShapeDtypeStruct((20, C), F4),) * 3,
         name="update",
+        compiler_params=pltpu.CompilerParams(vmem_limit_bytes=16 * MIB),
     )(col, own, other, state)
 
 

time: 84.7 us -> 82.1 us (0.969)
  Pallas kernels: 29.8 us -> 27.9 us
  local copies, waits for them, and re-layouts: 2.24 us -> 0.98 us
    unnamed x16 -> x10, local copies, waits for them, and re-layouts: 2.24 us -> 0.98 us
    pallas_call x1, Pallas kernels: 22.2 us -> 21.3 us  [train(): pl.pallas_call(functools.partial(train_kernel, steps, layers), grid=(step...]
    pallas_call x1, Pallas kernels: 1.65 us -> 0.72 us  [update(): pl.pallas_call(update_kernel, in_specs=[pl.BlockSpec(memory_space=pltpu.S...]
where the time goes in v5:
time: 82.1 us; the launch traced here: 81.8 us
  blocking collectives  33.5 us (41%)
  Pallas kernels  27.9 us (34%)
  starting transfers between devices  13.6 us (17%)
  waiting for transfers between devices  3.89 us (5%)
  other arithmetic  1.2 us (1%)
  local copies, waits for them, and re-layouts  0.98 us (1%)
    pallas_call x1, Pallas kernels, train(): pl.pallas_call(functools.partial(train_kernel, steps, layers), grid=(step...  21.3 us
    all_to_all x1, blocking collectives, body(): lax.all_to_all(half.reshape(32, WEIGHT_ROWS, 128), 'row', split_axis=0, c...  19.3 us
    all_to_all x1, blocking collectives, body(): lax.all_to_all(outgoing.reshape(32, BLOCK_ROWS, 128), 'row', split_axis=0...  14.2 us
    ppermute x1, starting transfers between devices, body(): behind = lax.ppermute(initial, every, [(j, i) for i, j in up])  8.27 us
    pallas_call x1, Pallas kernels, lift(): pl.pallas_call(lift_kernel, out_shape=(jax.ShapeDtypeStruct((C, CELLS), B...  3.43 us
    ppermute x1, starting transfers between devices, body(): across = lax.ppermute(summed, 'sec', swap)  2.96 us
    ppermute x1, waiting for transfers between devices, body(): half = keep + lax.ppermute(send, 'col', swap)  2.46 us
    ppermute x1, starting transfers between devices, body(): other = lax.ppermute(arrived, 'col', swap)  2.21 us
  transfers between devices with their start and end apart: 5, of which 2 were waited for; matrix products, arithmetic and copies ran while one was open for 1% of the time, Pallas kernels for 6%

profile of v5, /device:TPU:0, one launch (start us, length us, event | category | flops | bytes accessed | tf_op | source)
XLA Modules:
  0.0 81.8 jit_solution(13265857708066369970)
XLA Ops:
  0.6 0.0 copy-start
  0.6 1.0 %copy-done = f32[19,16,256]{2,1,0:T(8,128)S(1)} copy-done((f32[19,16,256]{2,1,0:T(8,128)S(1)}, f32[19,16,256]{2,1,0:T(8,128)}, u32[]{:S(2)}) %copy-start) | copy-done | bytes 311320
  1.6 0.1 collective-permute-start
  1.7 8.3 %collective-permute-start.1 = (f32[14,256]{1,0:T(8,128)S(1)}, f32[14,256]{1,0:T(8,128)S(1)}, u32[]{:S(2)}, u32[]{:S(2)}) collective-permute-start(f32[14,256]{1,0:T(8,128)S(1)} %get-tuple-element.25), channel_id=1, source_target_pairs={{1,0},{2,1},{3,2},{4,3},{5,4},{6,5},{7,6},{8,7},{9,8},{10,9},{11,1... | collective-permute-start | bytes 43016 | tf_op jit(solution)/shard_map/ppermute | solution.py:638
  10.0 1.0 %select_select_fusion.small_ref = f32[120,320]{1,0:T(8,128)S(1)} fusion(f32[20,320]{1,0:T(8,128)} %master_ref.1, s32[1,32]{1,0:T(1,128)} %param.12, bf16[81,320]{1,0:T(8,128)(2,1)} %bitcast.10, bf16[3,320]{1,0:T(4,128)(2,1)} %param.19, f32[320]{0:T(512)} %param.15, f32[320]{0:T(512)} %param.14, pred[120]{0:T(512)(128)(4,1)S(1)} %get-tuple-element.42, ...), kind=kLoop, calls=%fused_computation | loop fusion | flops 307200 | bytes 235888 | tf_op jit(solution)/shard_map/jit(_where)/select_n | solution.py:163
  11.1 0.6 prepare.1
  11.6 0.0 collective-permute-done.before_ref
  11.6 0.0 collective-permute-done.1.behind_ref
  11.6 0.8 route.1
  12.4 14.2 %all_to_all.10 = bf16[32,72,128]{2,1,0:T(8,128)(2,1)S(1)} all-to-all(bf16[32,72,128]{2,1,0:T(8,128)(2,1)S(1)} %bitcast.8), channel_id=1, replica_groups=mesh['sec'=2,'row'=32,'col'=2] {'row'}, dimensions={0} | all-to-all | bytes 1179648 | tf_op jit(solution)/shard_map/all_to_all | solution.py:642
  26.7 2.2 %collective-permute-start.2 = (bf16[2304,128]{1,0:T(8,128)(2,1)S(1)}, bf16[2304,128]{1,0:T(8,128)(2,1)S(1)}, u32[]{:S(2)}, u32[]{:S(2)}) collective-permute-start(bf16[2304,128]{1,0:T(8,128)(2,1)S(1)} %bitcast.5), channel_id=1, source_target_pairs={{0,1},{1,0},{2,3},{3,2},{4,5},{5,4},{6,7},{7,6},{8,9},{9,8},{10,11... | collective-permute-start | bytes 1769480 | tf_op jit(solution)/shard_map/ppermute | solution.py:648
  28.9 3.4 %lift.1 = (bf16[320,4096]{1,0:T(8,128)(2,1)S(1)}, f32[16,4096]{1,0:T(8,128)S(1)}) custom-call(bf16[2304,128]{1,0:T(8,128)(2,1)S(1)} %bitcast.6, bf16[320,224]{1,0:T(8,128)(2,1)S(1)} %get-tuple-element.30.weight_ref, f32[320,128]{1,0:T(8,128)S(1)} %get-tuple-element.31.gain_ref, f32[320,128]{1,0:T(8,128)S(1)} %get-tuple-element.32.shift_ref), custom_call_target="tpu_custom_call" | custom-call | tf_op jit(solution)/shard_map/lift/pallas_call | solution.py:419
  32.3 0.0 collective-permute-done.2.other_ref
  32.3 21.3 %train.1 = (f32[1792,128]{1,0:T(8,128)S(1)}, f32[1792,128]{1,0:T(8,128)S(1)}) custom-call(s32[1]{0:T(128)} %bitcast.col_ref, bf16[320,4096]{1,0:T(8,128)(2,1)S(1)} %get-tuple-element.33.h_ref, f32[16,4096]{1,0:T(8,128)S(1)} %get-tuple-element.34.target_ref, bf16[2304,128]{1,0:T(8,128)(2,1)S(1)} %bitcast.7, ...), custom_call_target="tpu_custom_call" | custom-call | tf_op jit(solution)/shard_map/train/pallas_call | solution.py:556
  53.6 0.1 collective-permute-start.3
  53.7 2.5 %collective-permute-done.3 = f32[1792,128]{1,0:T(8,128)S(1)} collective-permute-done((f32[1792,128]{1,0:T(8,128)S(1)}, f32[1792,128]{1,0:T(8,128)S(1)}, u32[]{:S(2)}, u32[]{:S(2)}) %collective-permute-start.3) | collective-permute-done | bytes 917536 | tf_op jit(solution)/shard_map/ppermute | solution.py:651
  56.2 0.0 copy-start.1
  56.2 0.0 copy-start.2
  56.2 0.0 copy-start.3
  56.2 0.0 copy-start.4
  56.2 0.1 add.23
  56.3 19.3 %all_to_all.11 = f32[32,56,128]{2,1,0:T(8,128)S(1)} all-to-all(f32[32,56,128]{2,1,0:T(8,128)S(1)} %bitcast.9), channel_id=1, replica_groups=mesh['sec'=2,'row'=32,'col'=2] {'row'}, dimensions={0} | all-to-all | bytes 1835008 | tf_op jit(solution)/shard_map/all_to_all | solution.py:652
  75.6 0.1 reduce_sum.9.own_ref
  75.6 3.0 %collective-permute-start.4 = (f32[56,128]{1,0:T(8,128)S(1)}, f32[56,128]{1,0:T(8,128)S(1)}, u32[]{:S(2)}, u32[]{:S(2)}) collective-permute-start(f32[56,128]{1,0:T(8,128)S(1)} %reduce_sum.9.own_ref), channel_id=1, source_target_pairs={{0,64},{64,0},{1,65},{65,1},{2,66},{66,2},{3,67},{67,3},{4,68},{68... | collective-permute-start | bytes 86024 | tf_op jit(solution)/shard_map/ppermute | solution.py:656
  78.6 0.0 copy-done.1
  78.6 0.0 copy-done.2
  78.6 0.0 copy-done.3
  78.6 0.0 copy-done.4
  78.6 1.1 %collide.1 = (f32[19,16,256]{2,1,0:T(8,128)}, f32[3,20,320]{2,1,0:T(8,128)S(1)}) custom-call(f32[19,16,256]{2,1,0:T(8,128)S(1)} %get-tuple-element.23.pop_ref, f32[14,256]{1,0:T(8,128)S(1)} %collective-permute-done.before_ref, f32[14,256]{1,0:T(8,128)S(1)} %collective-permute-done.1.behind_ref, f32[16,256]{1,0:T(8,128)S(1)} %copy-done.4, ...), custom_call_target="tpu_custom_call" | custom-call | flops 10000000 | bytes 4000000 | tf_op jit(solution)/shard_map/collide/pallas_call | solution.py:320
  79.7 1.4 %collective-permute-done.4.other_ref = f32[56,128]{1,0:T(8,128)S(1)} collective-permute-done((f32[56,128]{1,0:T(8,128)S(1)}, f32[56,128]{1,0:T(8,128)S(1)}, u32[]{:S(2)}, u32[]{:S(2)}) %collective-permute-start.4) | collective-permute-done | bytes 28704 | tf_op jit(solution)/shard_map/ppermute | solution.py:656
  81.1 0.7 update.1
  (2 shorter events, 0.0 us)
Async XLA Ops:
  0.6 1.0 %copy-start = (f32[19,16,256]{2,1,0:T(8,128)S(1)}, f32[19,16,256]{2,1,0:T(8,128)}, u32[]{:S(2)}) copy-start(f32[19,16,256]{2,1,0:T(8,128)} %pop_ref.1) | copy-start | bytes 933892
  1.6 10.0 %collective-permute-start = (f32[14,256]{1,0:T(8,128)S(1)}, f32[14,256]{1,0:T(8,128)S(1)}, u32[]{:S(2)}, u32[]{:S(2)}) collective-permute-start(f32[14,256]{1,0:T(8,128)S(1)} %get-tuple-element.24), channel_id=1, source_target_pairs={{0,1},{1,2},{2,3},{3,4},{4,5},{5,6},{6,7},{7,8},{8,9},{9,10},{10,1... | collective-permute-start | bytes 43016 | tf_op jit(solution)/shard_map/ppermute | solution.py:637
  1.7 9.9 %collective-permute-start.1 = (f32[14,256]{1,0:T(8,128)S(1)}, f32[14,256]{1,0:T(8,128)S(1)}, u32[]{:S(2)}, u32[]{:S(2)}) collective-permute-start(f32[14,256]{1,0:T(8,128)S(1)} %get-tuple-element.25), channel_id=1, source_target_pairs={{1,0},{2,1},{3,2},{4,3},{5,4},{6,5},{7,6},{8,7},{9,8},{10,9},{11,1... | collective-permute-start | bytes 43016 | tf_op jit(solution)/shard_map/ppermute | solution.py:638
  26.7 5.7 %collective-permute-start.2 = (bf16[2304,128]{1,0:T(8,128)(2,1)S(1)}, bf16[2304,128]{1,0:T(8,128)(2,1)S(1)}, u32[]{:S(2)}, u32[]{:S(2)}) collective-permute-start(bf16[2304,128]{1,0:T(8,128)(2,1)S(1)} %bitcast.5), channel_id=1, source_target_pairs={{0,1},{1,0},{2,3},{3,2},{4,5},{5,4},{6,7},{7,6},{8,9},{9,8},{10,11... | collective-permute-start | bytes 1769480 | tf_op jit(solution)/shard_map/ppermute | solution.py:648
  53.6 2.6 %collective-permute-start.3 = (f32[1792,128]{1,0:T(8,128)S(1)}, f32[1792,128]{1,0:T(8,128)S(1)}, u32[]{:S(2)}, u32[]{:S(2)}) collective-permute-start(f32[1792,128]{1,0:T(8,128)S(1)} %get-tuple-element.37), channel_id=1, source_target_pairs={{0,1},{1,0},{2,3},{3,2},{4,5},{5,4},{6,7},{7,6},{8,9},{9,8},{10,11... | collective-permute-start | bytes 2752520 | tf_op jit(solution)/shard_map/ppermute | solution.py:651
  56.2 22.4 %copy-start.1 = (f32[20,320]{1,0:T(8,128)S(1)}, f32[20,320]{1,0:T(8,128)}, u32[]{:S(2)}) copy-start(f32[20,320]{1,0:T(8,128)} %master_ref.1) | copy-start | bytes 76804
  56.2 22.4 %copy-start.2 = (f32[20,320]{1,0:T(8,128)S(1)}, f32[20,320]{1,0:T(8,128)}, u32[]{:S(2)}) copy-start(f32[20,320]{1,0:T(8,128)} %first_ref.1) | copy-start | bytes 76804
  56.2 22.4 %copy-start.3 = (f32[20,320]{1,0:T(8,128)S(1)}, f32[20,320]{1,0:T(8,128)}, u32[]{:S(2)}) copy-start(f32[20,320]{1,0:T(8,128)} %second_ref.1) | copy-start | bytes 76804
  56.2 22.4 %copy-start.4 = (f32[16,256]{1,0:T(8,128)S(1)}, f32[16,256]{1,0:T(8,128)}, u32[]{:S(2)}) copy-start(f32[16,256]{1,0:T(8,128)} %relax_ref.1) | copy-start | bytes 49156
  75.6 5.5 %collective-permute-start.4 = (f32[56,128]{1,0:T(8,128)S(1)}, f32[56,128]{1,0:T(8,128)S(1)}, u32[]{:S(2)}, u32[]{:S(2)}) collective-permute-start(f32[56,128]{1,0:T(8,128)S(1)} %reduce_sum.9.own_ref), channel_id=1, source_target_pairs={{0,64},{64,0},{1,65},{65,1},{2,66},{66,2},{3,67},{67,3},{4,68},{68... | collective-permute-start | bytes 86024 | tf_op jit(solution)/shard_map/ppermute | solution.py:656

commit v6 on v5

--- a/solution.py
+++ b/solution.py
@@ -39,6 +39,8 @@
     (0, 1, -1),
     (0, -1, 1),
 )
+FORWARD = [index for index in range(19) if VELOCITIES[index][0] > 0]
+BACKWARD = [index for index in range(19) if VELOCITIES[index][0] < 0]
 LATTICE_WEIGHTS = (1.0 / 3.0,) + (1.0 / 18.0,) * 6 + (1.0 / 36.0,) * 12
 
 ROOT_HALF = 0.7071067811865476
@@ -138,15 +140,16 @@
 
 def planes_kernel(pop_ref, last_ref, initial_ref, own_ref):
     own_ref[...] = pop_ref[...]
-    for index in range(1, 15):
-        last_ref[index - 1 : index, :] = pop_ref[index, 15:16, :]
-        initial_ref[index - 1 : index, :] = pop_ref[index, 0:1, :]
+    for ref, indices, row in ((last_ref, FORWARD, 15), (initial_ref, BACKWARD, 0)):
+        ref[...] = jnp.zeros_like(ref)
+        for slot, index in enumerate(indices):
+            ref[slot : slot + 1, :] = pop_ref[index, row : row + 1, :]
 
 
 def planes(populations):
     return pl.pallas_call(
         planes_kernel,
-        out_shape=(jax.ShapeDtypeStruct((14, 256), F4),) * 2
+        out_shape=(jax.ShapeDtypeStruct((8, 256), F4),) * 2
         + (jax.ShapeDtypeStruct((19, 16, 256), F4),),
         name="planes",
         compiler_params=pltpu.CompilerParams(vmem_limit_bytes=16 * MIB),
@@ -245,9 +248,11 @@
         along_x, along_y, along_z = VELOCITIES[index]
         plane = pop_ref[index]
         if along_x > 0:
-            plane = jnp.where(row == 0, before_ref[index - 1 : index], pltpu.roll(plane, 1, 0))
+            at = FORWARD.index(index)
+            plane = jnp.where(row == 0, before_ref[at : at + 1], pltpu.roll(plane, 1, 0))
         elif along_x < 0:
-            plane = jnp.where(row == 15, behind_ref[index - 1 : index], pltpu.roll(plane, 15, 0))
+            at = BACKWARD.index(index)
+            plane = jnp.where(row == 15, behind_ref[at : at + 1], pltpu.roll(plane, 15, 0))
         if along_y:
             plane = pltpu.roll(plane, along_y * 16 % 256, 1)
         if along_z > 0:
@@ -634,8 +639,8 @@
     col = lax.axis_index("col").astype(I4)[None]
     up = [(i, (i + 1) % size) for i in range(size)]
     last, initial, populations = planes(populations)
+    behind = lax.ppermute(initial, every, [(j, i) for i, j in up])
     before = lax.ppermute(last, every, up)
-    behind = lax.ppermute(initial, every, [(j, i) for i, j in up])
     small = gathered_rows(norm_gain, norm_shift, send_lists, out_weight, mix_master, lift_weight)
     old, select, weights, lift_rows, gain, shift, out_rows = prepare(col, populations, small)
     outgoing = route(populations, before, behind, old, select, weights)

time: 82.1 us -> 82.1 us (level)
  no operation moved by 1% of the time
where the time goes in v6:
time: 82.1 us; the launch traced here: 81.8 us
  blocking collectives  33.6 us (41%)
  Pallas kernels  27.9 us (34%)
  starting transfers between devices  13.5 us (16%)
  waiting for transfers between devices  3.97 us (5%)
  other arithmetic  1.2 us (1%)
  local copies, waits for them, and re-layouts  0.98 us (1%)
    pallas_call x1, Pallas kernels, train(): pl.pallas_call(functools.partial(train_kernel, steps, layers), grid=(step...  21.3 us
    all_to_all x1, blocking collectives, body(): lax.all_to_all(half.reshape(32, WEIGHT_ROWS, 128), 'row', split_axis=0, c...  19.3 us
    all_to_all x1, blocking collectives, body(): lax.all_to_all(outgoing.reshape(32, BLOCK_ROWS, 128), 'row', split_axis=0...  14.3 us
    ppermute x1, starting transfers between devices, body(): behind = lax.ppermute(initial, every, [(j, i) for i, j in up])  8.27 us
    pallas_call x1, Pallas kernels, lift(): pl.pallas_call(lift_kernel, out_shape=(jax.ShapeDtypeStruct((C, CELLS), B...  3.43 us
    ppermute x1, starting transfers between devices, body(): across = lax.ppermute(summed, 'sec', swap)  2.87 us
    ppermute x1, waiting for transfers between devices, body(): half = keep + lax.ppermute(send, 'col', swap)  2.46 us
    ppermute x1, starting transfers between devices, body(): other = lax.ppermute(arrived, 'col', swap)  2.17 us
  transfers between devices with their start and end apart: 5, of which 2 were waited for; matrix products, arithmetic and copies ran while one was open for 1% of the time, Pallas kernels for 6%

profile of v6, /device:TPU:0, one launch (start us, length us, event | category | flops | bytes accessed | tf_op | source)
XLA Modules:
  0.0 81.8 jit_solution(9099892382641505258)
XLA Ops:
  0.6 0.0 copy-start
  0.6 1.0 %copy-done = f32[19,16,256]{2,1,0:T(8,128)S(1)} copy-done((f32[19,16,256]{2,1,0:T(8,128)S(1)}, f32[19,16,256]{2,1,0:T(8,128)}, u32[]{:S(2)}) %copy-start) | copy-done | bytes 311320
  1.6 0.1 collective-permute-start
  1.7 8.3 %collective-permute-start.1 = (f32[8,256]{1,0:T(8,128)S(1)}, f32[8,256]{1,0:T(8,128)S(1)}, u32[]{:S(2)}, u32[]{:S(2)}) collective-permute-start(f32[8,256]{1,0:T(8,128)S(1)} %get-tuple-element.25), channel_id=1, source_target_pairs={{1,0},{2,1},{3,2},{4,3},{5,4},{6,5},{7,6},{8,7},{9,8},{10,9},{11,1... | collective-permute-start | bytes 24584 | tf_op jit(solution)/shard_map/ppermute | solution.py:642
  10.0 1.0 %select_select_fusion.small_ref = f32[120,320]{1,0:T(8,128)S(1)} fusion(f32[20,320]{1,0:T(8,128)} %master_ref.1, s32[1,32]{1,0:T(1,128)} %param.12, bf16[81,320]{1,0:T(8,128)(2,1)} %bitcast.10, bf16[3,320]{1,0:T(4,128)(2,1)} %param.19, f32[320]{0:T(512)} %param.15, f32[320]{0:T(512)} %param.14, pred[120]{0:T(512)(128)(4,1)S(1)} %get-tuple-element.42, ...), kind=kLoop, calls=%fused_computation | loop fusion | flops 307200 | bytes 235888 | tf_op jit(solution)/shard_map/jit(_where)/select_n | solution.py:166
  11.0 0.6 prepare.1
  11.6 0.0 collective-permute-done.before_ref
  11.6 0.0 collective-permute-done.1.behind_ref
  11.6 0.8 route.1
  12.4 14.3 %all_to_all.10 = bf16[32,72,128]{2,1,0:T(8,128)(2,1)S(1)} all-to-all(bf16[32,72,128]{2,1,0:T(8,128)(2,1)S(1)} %bitcast.8), channel_id=1, replica_groups=mesh['sec'=2,'row'=32,'col'=2] {'row'}, dimensions={0} | all-to-all | bytes 1179648 | tf_op jit(solution)/shard_map/all_to_all | solution.py:647
  26.7 2.2 %collective-permute-start.2 = (bf16[2304,128]{1,0:T(8,128)(2,1)S(1)}, bf16[2304,128]{1,0:T(8,128)(2,1)S(1)}, u32[]{:S(2)}, u32[]{:S(2)}) collective-permute-start(bf16[2304,128]{1,0:T(8,128)(2,1)S(1)} %bitcast.5), channel_id=1, source_target_pairs={{0,1},{1,0},{2,3},{3,2},{4,5},{5,4},{6,7},{7,6},{8,9},{9,8},{10,11... | collective-permute-start | bytes 1769480 | tf_op jit(solution)/shard_map/ppermute | solution.py:653
  28.9 3.4 %lift.1 = (bf16[320,4096]{1,0:T(8,128)(2,1)S(1)}, f32[16,4096]{1,0:T(8,128)S(1)}) custom-call(bf16[2304,128]{1,0:T(8,128)(2,1)S(1)} %bitcast.6, bf16[320,224]{1,0:T(8,128)(2,1)S(1)} %get-tuple-element.30.weight_ref, f32[320,128]{1,0:T(8,128)S(1)} %get-tuple-element.31.gain_ref, f32[320,128]{1,0:T(8,128)S(1)} %get-tuple-element.32.shift_ref), custom_call_target="tpu_custom_call" | custom-call | tf_op jit(solution)/shard_map/lift/pallas_call | solution.py:424
  32.3 0.0 collective-permute-done.2.other_ref
  32.3 21.3 %train.1 = (f32[1792,128]{1,0:T(8,128)S(1)}, f32[1792,128]{1,0:T(8,128)S(1)}) custom-call(s32[1]{0:T(128)} %bitcast.col_ref, bf16[320,4096]{1,0:T(8,128)(2,1)S(1)} %get-tuple-element.33.h_ref, f32[16,4096]{1,0:T(8,128)S(1)} %get-tuple-element.34.target_ref, bf16[2304,128]{1,0:T(8,128)(2,1)S(1)} %bitcast.7, ...), custom_call_target="tpu_custom_call" | custom-call | tf_op jit(solution)/shard_map/train/pallas_call | solution.py:561
  53.6 0.1 collective-permute-start.3
  53.7 2.5 %collective-permute-done.3 = f32[1792,128]{1,0:T(8,128)S(1)} collective-permute-done((f32[1792,128]{1,0:T(8,128)S(1)}, f32[1792,128]{1,0:T(8,128)S(1)}, u32[]{:S(2)}, u32[]{:S(2)}) %collective-permute-start.3) | collective-permute-done | bytes 917536 | tf_op jit(solution)/shard_map/ppermute | solution.py:656
  56.1 0.0 copy-start.1
  56.1 0.0 copy-start.2
  56.1 0.0 copy-start.3
  56.2 0.0 copy-start.4
  56.2 0.1 add.23
  56.3 19.3 %all_to_all.11 = f32[32,56,128]{2,1,0:T(8,128)S(1)} all-to-all(f32[32,56,128]{2,1,0:T(8,128)S(1)} %bitcast.9), channel_id=1, replica_groups=mesh['sec'=2,'row'=32,'col'=2] {'row'}, dimensions={0} | all-to-all | bytes 1835008 | tf_op jit(solution)/shard_map/all_to_all | solution.py:657
  75.6 0.1 reduce_sum.9.own_ref
  75.6 2.9 %collective-permute-start.4 = (f32[56,128]{1,0:T(8,128)S(1)}, f32[56,128]{1,0:T(8,128)S(1)}, u32[]{:S(2)}, u32[]{:S(2)}) collective-permute-start(f32[56,128]{1,0:T(8,128)S(1)} %reduce_sum.9.own_ref), channel_id=1, source_target_pairs={{0,64},{64,0},{1,65},{65,1},{2,66},{66,2},{3,67},{67,3},{4,68},{68... | collective-permute-start | bytes 86024 | tf_op jit(solution)/shard_map/ppermute | solution.py:661
  78.5 0.0 copy-done.1
  78.5 0.0 copy-done.2
  78.5 0.0 copy-done.3
  78.5 0.0 copy-done.4
  78.5 1.1 %collide.1 = (f32[19,16,256]{2,1,0:T(8,128)}, f32[3,20,320]{2,1,0:T(8,128)S(1)}) custom-call(f32[19,16,256]{2,1,0:T(8,128)S(1)} %get-tuple-element.23.pop_ref, f32[8,256]{1,0:T(8,128)S(1)} %collective-permute-done.before_ref, f32[8,256]{1,0:T(8,128)S(1)} %collective-permute-done.1.behind_ref, f32[16,256]{1,0:T(8,128)S(1)} %copy-done.4, ...), custom_call_target="tpu_custom_call" | custom-call | flops 10000000 | bytes 4000000 | tf_op jit(solution)/shard_map/collide/pallas_call | solution.py:325
  79.6 1.5 %collective-permute-done.4.other_ref = f32[56,128]{1,0:T(8,128)S(1)} collective-permute-done((f32[56,128]{1,0:T(8,128)S(1)}, f32[56,128]{1,0:T(8,128)S(1)}, u32[]{:S(2)}, u32[]{:S(2)}) %collective-permute-start.4) | collective-permute-done | bytes 28704 | tf_op jit(solution)/shard_map/ppermute | solution.py:661
  81.1 0.7 update.1
  (2 shorter events, 0.0 us)
Async XLA Ops:
  0.6 1.0 %copy-start = (f32[19,16,256]{2,1,0:T(8,128)S(1)}, f32[19,16,256]{2,1,0:T(8,128)}, u32[]{:S(2)}) copy-start(f32[19,16,256]{2,1,0:T(8,128)} %pop_ref.1) | copy-start | bytes 933892
  1.6 10.0 %collective-permute-start = (f32[8,256]{1,0:T(8,128)S(1)}, f32[8,256]{1,0:T(8,128)S(1)}, u32[]{:S(2)}, u32[]{:S(2)}) collective-permute-start(f32[8,256]{1,0:T(8,128)S(1)} %get-tuple-element.24), channel_id=1, source_target_pairs={{0,1},{1,2},{2,3},{3,4},{4,5},{5,6},{6,7},{7,8},{8,9},{9,10},{10,1... | collective-permute-start | bytes 24584 | tf_op jit(solution)/shard_map/ppermute | solution.py:643
  1.7 9.9 %collective-permute-start.1 = (f32[8,256]{1,0:T(8,128)S(1)}, f32[8,256]{1,0:T(8,128)S(1)}, u32[]{:S(2)}, u32[]{:S(2)}) collective-permute-start(f32[8,256]{1,0:T(8,128)S(1)} %get-tuple-element.25), channel_id=1, source_target_pairs={{1,0},{2,1},{3,2},{4,3},{5,4},{6,5},{7,6},{8,7},{9,8},{10,9},{11,1... | collective-permute-start | bytes 24584 | tf_op jit(solution)/shard_map/ppermute | solution.py:642
  26.7 5.6 %collective-permute-start.2 = (bf16[2304,128]{1,0:T(8,128)(2,1)S(1)}, bf16[2304,128]{1,0:T(8,128)(2,1)S(1)}, u32[]{:S(2)}, u32[]{:S(2)}) collective-permute-start(bf16[2304,128]{1,0:T(8,128)(2,1)S(1)} %bitcast.5), channel_id=1, source_target_pairs={{0,1},{1,0},{2,3},{3,2},{4,5},{5,4},{6,7},{7,6},{8,9},{9,8},{10,11... | collective-permute-start | bytes 1769480 | tf_op jit(solution)/shard_map/ppermute | solution.py:653
  53.6 2.6 %collective-permute-start.3 = (f32[1792,128]{1,0:T(8,128)S(1)}, f32[1792,128]{1,0:T(8,128)S(1)}, u32[]{:S(2)}, u32[]{:S(2)}) collective-permute-start(f32[1792,128]{1,0:T(8,128)S(1)} %get-tuple-element.37), channel_id=1, source_target_pairs={{0,1},{1,0},{2,3},{3,2},{4,5},{5,4},{6,7},{7,6},{8,9},{9,8},{10,11... | collective-permute-start | bytes 2752520 | tf_op jit(solution)/shard_map/ppermute | solution.py:656
  56.1 22.4 %copy-start.1 = (f32[20,320]{1,0:T(8,128)S(1)}, f32[20,320]{1,0:T(8,128)}, u32[]{:S(2)}) copy-start(f32[20,320]{1,0:T(8,128)} %master_ref.1) | copy-start | bytes 76804
  56.1 22.4 %copy-start.2 = (f32[20,320]{1,0:T(8,128)S(1)}, f32[20,320]{1,0:T(8,128)}, u32[]{:S(2)}) copy-start(f32[20,320]{1,0:T(8,128)} %first_ref.1) | copy-start | bytes 76804
  56.1 22.4 %copy-start.3 = (f32[20,320]{1,0:T(8,128)S(1)}, f32[20,320]{1,0:T(8,128)}, u32[]{:S(2)}) copy-start(f32[20,320]{1,0:T(8,128)} %second_ref.1) | copy-start | bytes 76804
  56.2 22.4 %copy-start.4 = (f32[16,256]{1,0:T(8,128)S(1)}, f32[16,256]{1,0:T(8,128)}, u32[]{:S(2)}) copy-start(f32[16,256]{1,0:T(8,128)} %relax_ref.1) | copy-start | bytes 49156
  75.6 5.5 %collective-permute-start.4 = (f32[56,128]{1,0:T(8,128)S(1)}, f32[56,128]{1,0:T(8,128)S(1)}, u32[]{:S(2)}, u32[]{:S(2)}) collective-permute-start(f32[56,128]{1,0:T(8,128)S(1)} %reduce_sum.9.own_ref), channel_id=1, source_target_pairs={{0,64},{64,0},{1,65},{65,1},{2,66},{66,2},{3,67},{67,3},{4,68},{68... | collective-permute-start | bytes 86024 | tf_op jit(solution)/shard_map/ppermute | solution.py:661

commit v7 on v6

--- a/solution.py
+++ b/solution.py
@@ -16,6 +16,7 @@
 BLOCK_ROWS = 16 + WEIGHT_ROWS
 WIDE = 384
 SPAN = 1024
+TOP_POWER = 14.0
 MIB = 1024 * 1024
 
 VELOCITIES = (
@@ -592,6 +593,33 @@
     )(col, h, target, mine, other, out_weight)
 
 
+def scale_kernel(keep_ref, other_ref, out_ref):
+    peak = jnp.zeros((8, 128), F4)
+    for start in range(0, 32 * WEIGHT_ROWS, 8):
+        value = keep_ref[start : start + 8, :] + other_ref[start : start + 8, :]
+        out_ref[start : start + 8, :] = value
+        peak = jnp.maximum(peak, jnp.abs(value))
+    peak = jnp.max(jnp.max(peak, axis=1, keepdims=True), axis=0, keepdims=True)
+    power = jnp.ceil(jnp.log2(jnp.maximum(peak, 1e-30)))
+    scale = jnp.broadcast_to(jnp.exp2(TOP_POWER - power), (8, 128))
+    power = jnp.broadcast_to(power, (8, 128))
+    free = iota((8, 128), 1) == 127
+    for start in range(0, 32 * WEIGHT_ROWS, 8):
+        value = out_ref[start : start + 8, :] * scale
+        if start % WEIGHT_ROWS == 48:
+            value = jnp.where(free, power, value)
+        out_ref[start : start + 8, :] = value
+
+
+def scaled(keep, other):
+    return pl.pallas_call(
+        scale_kernel,
+        out_shape=jax.ShapeDtypeStruct((32 * WEIGHT_ROWS, 128), F4),
+        name="scaled",
+        compiler_params=pltpu.CompilerParams(vmem_limit_bytes=16 * MIB),
+    )(keep, other)
+
+
 def update_kernel(col_ref, own_ref, other_ref, state_ref, new_ref, first_out, second_out):
     packed = own_ref[...] + other_ref[...]
     parts = unpack_piece([packed[index * 8 : index * 8 + 8] for index in range(7)])
@@ -653,11 +681,11 @@
     other = lax.ppermute(arrived, "col", swap)
     h, target = lift(arrived, lift_rows, gain, shift)
     send, keep = train(col, h, target, arrived, other, out_rows)
-    half = keep + lax.ppermute(send, "col", swap)
+    half = scaled(keep, lax.ppermute(send, "col", swap)).reshape(32, WEIGHT_ROWS, 128)
     terms = lax.all_to_all(
-        half.reshape(32, WEIGHT_ROWS, 128), "row", split_axis=0, concat_axis=0, tiled=True
-    )
-    summed = jnp.sum(terms, axis=0)
+        half.astype(jnp.float16), "row", split_axis=0, concat_axis=0, tiled=True
+    ).astype(F4)
+    summed = jnp.sum(terms * jnp.exp2(terms[:, 48:49, 127:128] - TOP_POWER), axis=0)
     across = lax.ppermute(summed, "sec", swap)
     new_master, new_first, new_second = update(col, summed, across, state)
     return (after, new_master, new_first, new_second)

time: 82.1 us -> 79 us (0.962)
  blocking collectives: 33.6 us -> 29.5 us
    all_to_all x1, blocking collectives: 19.3 us -> 15.2 us  [body(): lax.all_to_all(half.astype(jnp.float16), 'row', split_axis=0, concat_axis...]
where the time goes in v7:
time: 79 us; the launch traced here: 78.7 us
  blocking collectives  29.5 us (37%)
  Pallas kernels  28.2 us (36%)
  starting transfers between devices  13.5 us (17%)
  waiting for transfers between devices  3.97 us (5%)
  other arithmetic  1.82 us (2%)
  local copies, waits for them, and re-layouts  0.99 us (1%)
  between operations  0.79 us (1%)
    pallas_call x1, Pallas kernels, train(): pl.pallas_call(functools.partial(train_kernel, steps, layers), grid=(step...  21.3 us
    all_to_all x1, blocking collectives, body(): lax.all_to_all(half.astype(jnp.float16), 'row', split_axis=0, concat_axis...  15.2 us
    all_to_all x1, blocking collectives, body(): lax.all_to_all(outgoing.reshape(32, BLOCK_ROWS, 128), 'row', split_axis=0...  14.3 us
    ppermute x1, starting transfers between devices, body(): behind = lax.ppermute(initial, every, [(j, i) for i, j in up])  8.27 us
    pallas_call x1, Pallas kernels, lift(): pl.pallas_call(lift_kernel, out_shape=(jax.ShapeDtypeStruct((C, CELLS), B...  3.43 us
    ppermute x1, starting transfers between devices, body(): across = lax.ppermute(summed, 'sec', swap)  2.87 us
    ppermute x1, waiting for transfers between devices, body(): lax.ppermute(send, 'col', swap)  2.46 us
    ppermute x1, starting transfers between devices, body(): other = lax.ppermute(arrived, 'col', swap)  2.17 us
  transfers between devices with their start and end apart: 5, of which 2 were waited for; matrix products, arithmetic and copies ran while one was open for 1% of the time, Pallas kernels for 6%

profile of v7, /device:TPU:0, one launch (start us, length us, event | category | flops | bytes accessed | tf_op | source)
XLA Modules:
  0.0 78.7 jit_solution(14821696516900003395)
XLA Ops:
  0.6 0.0 copy-start
  0.6 1.0 %copy-done = f32[19,16,256]{2,1,0:T(8,128)S(1)} copy-done((f32[19,16,256]{2,1,0:T(8,128)S(1)}, f32[19,16,256]{2,1,0:T(8,128)}, u32[]{:S(2)}) %copy-start) | copy-done | bytes 311320
  1.6 0.1 collective-permute-start
  1.7 8.3 %collective-permute-start.1 = (f32[8,256]{1,0:T(8,128)S(1)}, f32[8,256]{1,0:T(8,128)S(1)}, u32[]{:S(2)}, u32[]{:S(2)}) collective-permute-start(f32[8,256]{1,0:T(8,128)S(1)} %get-tuple-element.25), channel_id=1, source_target_pairs={{1,0},{2,1},{3,2},{4,3},{5,4},{6,5},{7,6},{8,7},{9,8},{10,9},{11,1... | collective-permute-start | bytes 24584 | tf_op jit(solution)/shard_map/ppermute | solution.py:670
  10.0 1.0 %select_select_fusion.small_ref = f32[120,320]{1,0:T(8,128)S(1)} fusion(f32[20,320]{1,0:T(8,128)} %master_ref.1, s32[1,32]{1,0:T(1,128)} %param.12, bf16[81,320]{1,0:T(8,128)(2,1)} %bitcast.10, bf16[3,320]{1,0:T(4,128)(2,1)} %param.19, f32[320]{0:T(512)} %param.15, f32[320]{0:T(512)} %param.14, pred[120]{0:T(512)(128)(4,1)S(1)} %get-tuple-element.42, ...), kind=kLoop, calls=%fused_computation.1 | loop fusion | flops 307200 | bytes 235888 | tf_op jit(solution)/shard_map/jit(_where)/select_n | solution.py:167
  11.0 0.6 prepare.1
  11.6 0.0 collective-permute-done.before_ref
  11.6 0.0 collective-permute-done.1.behind_ref
  11.6 0.8 route.1
  12.4 14.3 %all_to_all.10 = bf16[32,72,128]{2,1,0:T(8,128)(2,1)S(1)} all-to-all(bf16[32,72,128]{2,1,0:T(8,128)(2,1)S(1)} %bitcast.8), channel_id=1, replica_groups=mesh['sec'=2,'row'=32,'col'=2] {'row'}, dimensions={0} | all-to-all | bytes 1179648 | tf_op jit(solution)/shard_map/all_to_all | solution.py:675
  26.7 2.2 %collective-permute-start.2 = (bf16[2304,128]{1,0:T(8,128)(2,1)S(1)}, bf16[2304,128]{1,0:T(8,128)(2,1)S(1)}, u32[]{:S(2)}, u32[]{:S(2)}) collective-permute-start(bf16[2304,128]{1,0:T(8,128)(2,1)S(1)} %bitcast.5), channel_id=1, source_target_pairs={{0,1},{1,0},{2,3},{3,2},{4,5},{5,4},{6,7},{7,6},{8,9},{9,8},{10,11... | collective-permute-start | bytes 1769480 | tf_op jit(solution)/shard_map/ppermute | solution.py:681
  28.9 3.4 %lift.1 = (bf16[320,4096]{1,0:T(8,128)(2,1)S(1)}, f32[16,4096]{1,0:T(8,128)S(1)}) custom-call(bf16[2304,128]{1,0:T(8,128)(2,1)S(1)} %bitcast.6, bf16[320,224]{1,0:T(8,128)(2,1)S(1)} %get-tuple-element.30.weight_ref, f32[320,128]{1,0:T(8,128)S(1)} %get-tuple-element.31.gain_ref, f32[320,128]{1,0:T(8,128)S(1)} %get-tuple-element.32.shift_ref), custom_call_target="tpu_custom_call" | custom-call | tf_op jit(solution)/shard_map/lift/pallas_call | solution.py:425
  32.3 0.0 collective-permute-done.2.other_ref
  32.3 21.3 %train.1 = (f32[1792,128]{1,0:T(8,128)S(1)}, f32[1792,128]{1,0:T(8,128)S(1)}) custom-call(s32[1]{0:T(128)} %bitcast.col_ref, bf16[320,4096]{1,0:T(8,128)(2,1)S(1)} %get-tuple-element.33.h_ref, f32[16,4096]{1,0:T(8,128)S(1)} %get-tuple-element.34.target_ref, bf16[2304,128]{1,0:T(8,128)(2,1)S(1)} %bitcast.7, ...), custom_call_target="tpu_custom_call" | custom-call | tf_op jit(solution)/shard_map/train/pallas_call | solution.py:562
  53.6 0.1 collective-permute-start.3
  53.7 2.5 %collective-permute-done.3.other_ref = f32[1792,128]{1,0:T(8,128)S(1)} collective-permute-done((f32[1792,128]{1,0:T(8,128)S(1)}, f32[1792,128]{1,0:T(8,128)S(1)}, u32[]{:S(2)}, u32[]{:S(2)}) %collective-permute-start.3) | collective-permute-done | bytes 917536 | tf_op jit(solution)/shard_map/ppermute | solution.py:684
  56.1 0.4 scaled.1
  56.5 0.0 copy-start.1
  56.6 0.0 copy-start.2
  56.6 0.0 copy-start.3
  56.6 0.0 copy-start.4
  56.6 0.1 convert_element_type.27
  56.7 15.2 %all_to_all.11 = f16[32,56,128]{2,1,0:T(8,128)(2,1)S(1)} all-to-all(f16[32,56,128]{2,1,0:T(8,128)(2,1)S(1)} %bitcast.9), channel_id=1, replica_groups=mesh['sec'=2,'row'=32,'col'=2] {'row'}, dimensions={0} | all-to-all | bytes 917504 | tf_op jit(solution)/shard_map/all_to_all | solution.py:685
  71.8 0.1 convert_element_type.29
  71.9 0.5 fusion.2
  72.4 0.2 multiply_reduce_fusion.own_ref
  72.6 2.9 %collective-permute-start.4 = (f32[56,128]{1,0:T(8,128)S(1)}, f32[56,128]{1,0:T(8,128)S(1)}, u32[]{:S(2)}, u32[]{:S(2)}) collective-permute-start(f32[56,128]{1,0:T(8,128)S(1)} %multiply_reduce_fusion.own_ref), channel_id=1, source_target_pairs={{0,64},{64,0},{1,65},{65,1},{2,66},{66,2},{3,67},{67,3},{4,68},{68... | collective-permute-start | bytes 86024 | tf_op jit(solution)/shard_map/ppermute | solution.py:689
  75.4 0.0 copy-done.1
  75.4 0.0 copy-done.2
  75.4 0.0 copy-done.3
  75.4 0.0 copy-done.4
  75.4 1.1 %collide.1 = (f32[19,16,256]{2,1,0:T(8,128)}, f32[3,20,320]{2,1,0:T(8,128)S(1)}) custom-call(f32[19,16,256]{2,1,0:T(8,128)S(1)} %get-tuple-element.23.pop_ref, f32[8,256]{1,0:T(8,128)S(1)} %collective-permute-done.before_ref, f32[8,256]{1,0:T(8,128)S(1)} %collective-permute-done.1.behind_ref, f32[16,256]{1,0:T(8,128)S(1)} %copy-done.4, ...), custom_call_target="tpu_custom_call" | custom-call | flops 10000000 | bytes 4000000 | tf_op jit(solution)/shard_map/collide/pallas_call | solution.py:326
  76.5 1.5 %collective-permute-done.4.other_ref = f32[56,128]{1,0:T(8,128)S(1)} collective-permute-done((f32[56,128]{1,0:T(8,128)S(1)}, f32[56,128]{1,0:T(8,128)S(1)}, u32[]{:S(2)}, u32[]{:S(2)}) %collective-permute-start.4) | collective-permute-done | bytes 28704 | tf_op jit(solution)/shard_map/ppermute | solution.py:689
  78.0 0.7 update.1
  (2 shorter events, 0.0 us)
Async XLA Ops:
  0.6 1.0 %copy-start = (f32[19,16,256]{2,1,0:T(8,128)S(1)}, f32[19,16,256]{2,1,0:T(8,128)}, u32[]{:S(2)}) copy-start(f32[19,16,256]{2,1,0:T(8,128)} %pop_ref.1) | copy-start | bytes 933892
  1.6 10.0 %collective-permute-start = (f32[8,256]{1,0:T(8,128)S(1)}, f32[8,256]{1,0:T(8,128)S(1)}, u32[]{:S(2)}, u32[]{:S(2)}) collective-permute-start(f32[8,256]{1,0:T(8,128)S(1)} %get-tuple-element.24), channel_id=1, source_target_pairs={{0,1},{1,2},{2,3},{3,4},{4,5},{5,6},{6,7},{7,8},{8,9},{9,10},{10,1... | collective-permute-start | bytes 24584 | tf_op jit(solution)/shard_map/ppermute | solution.py:671
  1.7 9.9 %collective-permute-start.1 = (f32[8,256]{1,0:T(8,128)S(1)}, f32[8,256]{1,0:T(8,128)S(1)}, u32[]{:S(2)}, u32[]{:S(2)}) collective-permute-start(f32[8,256]{1,0:T(8,128)S(1)} %get-tuple-element.25), channel_id=1, source_target_pairs={{1,0},{2,1},{3,2},{4,3},{5,4},{6,5},{7,6},{8,7},{9,8},{10,9},{11,1... | collective-permute-start | bytes 24584 | tf_op jit(solution)/shard_map/ppermute | solution.py:670
  26.7 5.6 %collective-permute-start.2 = (bf16[2304,128]{1,0:T(8,128)(2,1)S(1)}, bf16[2304,128]{1,0:T(8,128)(2,1)S(1)}, u32[]{:S(2)}, u32[]{:S(2)}) collective-permute-start(bf16[2304,128]{1,0:T(8,128)(2,1)S(1)} %bitcast.5), channel_id=1, source_target_pairs={{0,1},{1,0},{2,3},{3,2},{4,5},{5,4},{6,7},{7,6},{8,9},{9,8},{10,11... | collective-permute-start | bytes 1769480 | tf_op jit(solution)/shard_map/ppermute | solution.py:681
  53.6 2.6 %collective-permute-start.3 = (f32[1792,128]{1,0:T(8,128)S(1)}, f32[1792,128]{1,0:T(8,128)S(1)}, u32[]{:S(2)}, u32[]{:S(2)}) collective-permute-start(f32[1792,128]{1,0:T(8,128)S(1)} %get-tuple-element.37), channel_id=1, source_target_pairs={{0,1},{1,0},{2,3},{3,2},{4,5},{5,4},{6,7},{7,6},{8,9},{9,8},{10,11... | collective-permute-start | bytes 2752520 | tf_op jit(solution)/shard_map/ppermute | solution.py:684
  56.5 18.9 %copy-start.1 = (f32[20,320]{1,0:T(8,128)S(1)}, f32[20,320]{1,0:T(8,128)}, u32[]{:S(2)}) copy-start(f32[20,320]{1,0:T(8,128)} %master_ref.1) | copy-start | bytes 76804
  56.6 18.9 %copy-start.2 = (f32[20,320]{1,0:T(8,128)S(1)}, f32[20,320]{1,0:T(8,128)}, u32[]{:S(2)}) copy-start(f32[20,320]{1,0:T(8,128)} %first_ref.1) | copy-start | bytes 76804
  56.6 18.9 %copy-start.3 = (f32[20,320]{1,0:T(8,128)S(1)}, f32[20,320]{1,0:T(8,128)}, u32[]{:S(2)}) copy-start(f32[20,320]{1,0:T(8,128)} %second_ref.1) | copy-start | bytes 76804
  56.6 18.9 %copy-start.4 = (f32[16,256]{1,0:T(8,128)S(1)}, f32[16,256]{1,0:T(8,128)}, u32[]{:S(2)}) copy-start(f32[16,256]{1,0:T(8,128)} %relax_ref.1) | copy-start | bytes 49156
  72.6 5.5 %collective-permute-start.4 = (f32[56,128]{1,0:T(8,128)S(1)}, f32[56,128]{1,0:T(8,128)S(1)}, u32[]{:S(2)}, u32[]{:S(2)}) collective-permute-start(f32[56,128]{1,0:T(8,128)S(1)} %multiply_reduce_fusion.own_ref), channel_id=1, source_target_pairs={{0,64},{64,0},{1,65},{65,1},{2,66},{66,2},{3,67},{67,3},{4,68},{68... | collective-permute-start | bytes 86024 | tf_op jit(solution)/shard_map/ppermute | solution.py:689

commit v8 on v7

--- a/solution.py
+++ b/solution.py
@@ -265,7 +265,7 @@
 
 
 def route_kernel(
-    pop_ref, before_ref, behind_ref, old_ref, select_ref, weights_ref, out_ref, routed
+    pop_ref, behind_ref, before_ref, old_ref, select_ref, weights_ref, out_ref, routed
 ):
     density, flow = moments(streamed(pop_ref, before_ref, behind_ref))
     fields = jnp.concatenate([old_ref[...]] + [part.astype(BF) for part in flow], axis=0)
@@ -288,13 +288,13 @@
         scratch_shapes=[pltpu.VMEM((512, 128), F4)],
         name="route",
         compiler_params=pltpu.CompilerParams(vmem_limit_bytes=16 * MIB),
-    )(populations, before, behind, old, select, weights)
+    )(populations, behind, before, old, select, weights)
 
 
 def collide_kernel(
     pop_ref,
+    behind_ref,
     before_ref,
-    behind_ref,
     relax_ref,
     master_ref,
     first_ref,
@@ -332,7 +332,7 @@
         name="collide",
         cost_estimate=pl.CostEstimate(flops=10**7, bytes_accessed=4 * 10**6, transcendentals=0),
         compiler_params=pltpu.CompilerParams(vmem_limit_bytes=16 * MIB),
-    )(populations, before, behind, relaxation, *state)
+    )(populations, behind, before, relaxation, *state)
 
 
 def lift_kernel(

time: 79 us -> 83.2 us (1.053)
  waiting for transfers between devices: 3.97 us -> 10.8 us
  starting transfers between devices: 13.5 us -> 11.4 us
    ppermute x1, waiting for transfers between devices: 0.01 us -> 6.87 us  [body(): before = lax.ppermute(last, every, up)]
    ppermute x1, starting transfers between devices: 2.17 us -> 0.01 us  [body(): other = lax.ppermute(arrived, 'col', swap)]
  transfers between devices with their start and end apart: 5 -> 5, of which waited for: 2 -> 3; matrix products, arithmetic and copies ran while one was open for 1% -> 1% of each run, Pallas kernels for 6% -> 6%
where the time goes in v8:
time: 83.2 us; the launch traced here: 82.9 us
  blocking collectives  28.9 us (35%)
  Pallas kernels  28.3 us (34%)
  starting transfers between devices  11.4 us (14%)
  waiting for transfers between devices  10.8 us (13%)
  other arithmetic  1.82 us (2%)
  local copies, waits for them, and re-layouts  0.99 us (1%)
    pallas_call x1, Pallas kernels, train(): pl.pallas_call(functools.partial(train_kernel, steps, layers), grid=(step...  21.3 us
    all_to_all x1, blocking collectives, body(): lax.all_to_all(half.astype(jnp.float16), 'row', split_axis=0, concat_axis...  15.4 us
    all_to_all x1, blocking collectives, body(): lax.all_to_all(outgoing.reshape(32, BLOCK_ROWS, 128), 'row', split_axis=0...  13.5 us
    ppermute x1, starting transfers between devices, body(): behind = lax.ppermute(initial, every, [(j, i) for i, j in up])  8.27 us
    ppermute x1, waiting for transfers between devices, body(): before = lax.ppermute(last, every, up)  6.87 us
    pallas_call x1, Pallas kernels, lift(): pl.pallas_call(lift_kernel, out_shape=(jax.ShapeDtypeStruct((C, CELLS), B...  3.43 us
    ppermute x1, starting transfers between devices, body(): across = lax.ppermute(summed, 'sec', swap)  2.56 us
    ppermute x1, waiting for transfers between devices, body(): lax.ppermute(send, 'col', swap)  2.1 us
  transfers between devices with their start and end apart: 5, of which 3 were waited for; matrix products, arithmetic and copies ran while one was open for 1% of the time, Pallas kernels for 6%

profile of v8, /device:TPU:0, one launch (start us, length us, event | category | flops | bytes accessed | tf_op | source)
XLA Modules:
  0.0 82.9 jit_solution(13080427986866720122)
XLA Ops:
  0.6 0.0 copy-start
  0.6 1.0 %copy-done = f32[19,16,256]{2,1,0:T(8,128)S(1)} copy-done((f32[19,16,256]{2,1,0:T(8,128)S(1)}, f32[19,16,256]{2,1,0:T(8,128)}, u32[]{:S(2)}) %copy-start) | copy-done | bytes 311320
  1.6 8.3 %collective-permute-start = (f32[8,256]{1,0:T(8,128)S(1)}, f32[8,256]{1,0:T(8,128)S(1)}, u32[]{:S(2)}, u32[]{:S(2)}) collective-permute-start(f32[8,256]{1,0:T(8,128)S(1)} %get-tuple-element.24), channel_id=1, source_target_pairs={{1,0},{2,1},{3,2},{4,3},{5,4},{6,5},{7,6},{8,7},{9,8},{10,9},{11,1... | collective-permute-start | bytes 24584 | tf_op jit(solution)/shard_map/ppermute | solution.py:670
  9.9 0.0 collective-permute-start.1
  9.9 1.0 %select_select_fusion.small_ref = f32[120,320]{1,0:T(8,128)S(1)} fusion(f32[20,320]{1,0:T(8,128)} %master_ref.1, s32[1,32]{1,0:T(1,128)} %param.12, bf16[81,320]{1,0:T(8,128)(2,1)} %bitcast.10, bf16[3,320]{1,0:T(4,128)(2,1)} %param.19, f32[320]{0:T(512)} %param.15, f32[320]{0:T(512)} %param.14, pred[120]{0:T(512)(128)(4,1)S(1)} %get-tuple-element.42, ...), kind=kLoop, calls=%fused_computation.1 | loop fusion | flops 307200 | bytes 235888 | tf_op jit(solution)/shard_map/jit(_where)/select_n | solution.py:167
  11.0 0.6 prepare.1
  11.5 0.0 collective-permute-done.behind_ref
  11.5 6.9 %collective-permute-done.1.before_ref = f32[8,256]{1,0:T(8,128)S(1)} collective-permute-done((f32[8,256]{1,0:T(8,128)S(1)}, f32[8,256]{1,0:T(8,128)S(1)}, u32[]{:S(2)}, u32[]{:S(2)}) %collective-permute-start.1) | collective-permute-done | bytes 8224 | tf_op jit(solution)/shard_map/ppermute | solution.py:671
  18.4 0.8 route.1
  19.2 13.5 %all_to_all.10 = bf16[32,72,128]{2,1,0:T(8,128)(2,1)S(1)} all-to-all(bf16[32,72,128]{2,1,0:T(8,128)(2,1)S(1)} %bitcast.8), channel_id=1, replica_groups=mesh['sec'=2,'row'=32,'col'=2] {'row'}, dimensions={0} | all-to-all | bytes 1179648 | tf_op jit(solution)/shard_map/all_to_all | solution.py:675
  32.7 0.0 collective-permute-start.2
  32.7 3.4 %lift.1 = (bf16[320,4096]{1,0:T(8,128)(2,1)S(1)}, f32[16,4096]{1,0:T(8,128)S(1)}) custom-call(bf16[2304,128]{1,0:T(8,128)(2,1)S(1)} %bitcast.6, bf16[320,224]{1,0:T(8,128)(2,1)S(1)} %get-tuple-element.30.weight_ref, f32[320,128]{1,0:T(8,128)S(1)} %get-tuple-element.31.gain_ref, f32[320,128]{1,0:T(8,128)S(1)} %get-tuple-element.32.shift_ref), custom_call_target="tpu_custom_call" | custom-call | tf_op jit(solution)/shard_map/lift/pallas_call | solution.py:425
  36.1 0.0 collective-permute-done.2.other_ref
  36.1 21.3 %train.1 = (f32[1792,128]{1,0:T(8,128)S(1)}, f32[1792,128]{1,0:T(8,128)S(1)}) custom-call(s32[1]{0:T(128)} %bitcast.col_ref, bf16[320,4096]{1,0:T(8,128)(2,1)S(1)} %get-tuple-element.33.h_ref, f32[16,4096]{1,0:T(8,128)S(1)} %get-tuple-element.34.target_ref, bf16[2304,128]{1,0:T(8,128)(2,1)S(1)} %bitcast.7, ...), custom_call_target="tpu_custom_call" | custom-call | tf_op jit(solution)/shard_map/train/pallas_call | solution.py:562
  57.4 0.6 collective-permute-start.3
  58.0 2.1 %collective-permute-done.3.other_ref = f32[1792,128]{1,0:T(8,128)S(1)} collective-permute-done((f32[1792,128]{1,0:T(8,128)S(1)}, f32[1792,128]{1,0:T(8,128)S(1)}, u32[]{:S(2)}, u32[]{:S(2)}) %collective-permute-start.3) | collective-permute-done | bytes 917536 | tf_op jit(solution)/shard_map/ppermute | solution.py:684
  60.1 0.4 scaled.1
  60.5 0.0 copy-start.1
  60.5 0.0 copy-start.2
  60.5 0.0 copy-start.3
  60.5 0.0 copy-start.4
  60.5 0.1 convert_element_type.27
  60.6 15.4 %all_to_all.11 = f16[32,56,128]{2,1,0:T(8,128)(2,1)S(1)} all-to-all(f16[32,56,128]{2,1,0:T(8,128)(2,1)S(1)} %bitcast.9), channel_id=1, replica_groups=mesh['sec'=2,'row'=32,'col'=2] {'row'}, dimensions={0} | all-to-all | bytes 917504 | tf_op jit(solution)/shard_map/all_to_all | solution.py:685
  76.0 0.1 convert_element_type.29
  76.1 0.5 fusion.2
  76.6 0.2 multiply_reduce_fusion.own_ref
  76.7 2.6 %collective-permute-start.4 = (f32[56,128]{1,0:T(8,128)S(1)}, f32[56,128]{1,0:T(8,128)S(1)}, u32[]{:S(2)}, u32[]{:S(2)}) collective-permute-start(f32[56,128]{1,0:T(8,128)S(1)} %multiply_reduce_fusion.own_ref), channel_id=1, source_target_pairs={{0,64},{64,0},{1,65},{65,1},{2,66},{66,2},{3,67},{67,3},{4,68},{68... | collective-permute-start | bytes 86024 | tf_op jit(solution)/shard_map/ppermute | solution.py:689
  79.3 0.0 copy-done.1
  79.3 0.0 copy-done.2
  79.3 0.0 copy-done.3
  79.3 0.0 copy-done.4
  79.3 1.1 %collide.1 = (f32[19,16,256]{2,1,0:T(8,128)}, f32[3,20,320]{2,1,0:T(8,128)S(1)}) custom-call(f32[19,16,256]{2,1,0:T(8,128)S(1)} %get-tuple-element.23.pop_ref, f32[8,256]{1,0:T(8,128)S(1)} %collective-permute-done.behind_ref, f32[8,256]{1,0:T(8,128)S(1)} %collective-permute-done.1.before_ref, f32[16,256]{1,0:T(8,128)S(1)} %copy-done.4, ...), custom_call_target="tpu_custom_call" | custom-call | flops 10000000 | bytes 4000000 | tf_op jit(solution)/shard_map/collide/pallas_call | solution.py:326
  80.4 1.8 %collective-permute-done.4.other_ref = f32[56,128]{1,0:T(8,128)S(1)} collective-permute-done((f32[56,128]{1,0:T(8,128)S(1)}, f32[56,128]{1,0:T(8,128)S(1)}, u32[]{:S(2)}, u32[]{:S(2)}) %collective-permute-start.4) | collective-permute-done | bytes 28704 | tf_op jit(solution)/shard_map/ppermute | solution.py:689
  82.2 0.7 update.1
  (2 shorter events, 0.0 us)
Async XLA Ops:
  0.6 1.0 %copy-start = (f32[19,16,256]{2,1,0:T(8,128)S(1)}, f32[19,16,256]{2,1,0:T(8,128)}, u32[]{:S(2)}) copy-start(f32[19,16,256]{2,1,0:T(8,128)} %pop_ref.1) | copy-start | bytes 933892
  1.6 9.9 %collective-permute-start = (f32[8,256]{1,0:T(8,128)S(1)}, f32[8,256]{1,0:T(8,128)S(1)}, u32[]{:S(2)}, u32[]{:S(2)}) collective-permute-start(f32[8,256]{1,0:T(8,128)S(1)} %get-tuple-element.24), channel_id=1, source_target_pairs={{1,0},{2,1},{3,2},{4,3},{5,4},{6,5},{7,6},{8,7},{9,8},{10,9},{11,1... | collective-permute-start | bytes 24584 | tf_op jit(solution)/shard_map/ppermute | solution.py:670
  9.9 8.5 %collective-permute-start.1 = (f32[8,256]{1,0:T(8,128)S(1)}, f32[8,256]{1,0:T(8,128)S(1)}, u32[]{:S(2)}, u32[]{:S(2)}) collective-permute-start(f32[8,256]{1,0:T(8,128)S(1)} %get-tuple-element.25), channel_id=1, source_target_pairs={{0,1},{1,2},{2,3},{3,4},{4,5},{5,6},{6,7},{7,8},{8,9},{9,10},{10,1... | collective-permute-start | bytes 24584 | tf_op jit(solution)/shard_map/ppermute | solution.py:671
  32.7 3.4 %collective-permute-start.2 = (bf16[2304,128]{1,0:T(8,128)(2,1)S(1)}, bf16[2304,128]{1,0:T(8,128)(2,1)S(1)}, u32[]{:S(2)}, u32[]{:S(2)}) collective-permute-start(bf16[2304,128]{1,0:T(8,128)(2,1)S(1)} %bitcast.5), channel_id=1, source_target_pairs={{0,1},{1,0},{2,3},{3,2},{4,5},{5,4},{6,7},{7,6},{8,9},{9,8},{10,11... | collective-permute-start | bytes 1769480 | tf_op jit(solution)/shard_map/ppermute | solution.py:681
  57.4 2.7 %collective-permute-start.3 = (f32[1792,128]{1,0:T(8,128)S(1)}, f32[1792,128]{1,0:T(8,128)S(1)}, u32[]{:S(2)}, u32[]{:S(2)}) collective-permute-start(f32[1792,128]{1,0:T(8,128)S(1)} %get-tuple-element.37), channel_id=1, source_target_pairs={{0,1},{1,0},{2,3},{3,2},{4,5},{5,4},{6,7},{7,6},{8,9},{9,8},{10,11... | collective-permute-start | bytes 2752520 | tf_op jit(solution)/shard_map/ppermute | solution.py:684
  60.5 18.8 %copy-start.1 = (f32[20,320]{1,0:T(8,128)S(1)}, f32[20,320]{1,0:T(8,128)}, u32[]{:S(2)}) copy-start(f32[20,320]{1,0:T(8,128)} %master_ref.1) | copy-start | bytes 76804
  60.5 18.8 %copy-start.2 = (f32[20,320]{1,0:T(8,128)S(1)}, f32[20,320]{1,0:T(8,128)}, u32[]{:S(2)}) copy-start(f32[20,320]{1,0:T(8,128)} %first_ref.1) | copy-start | bytes 76804
  60.5 18.8 %copy-start.3 = (f32[20,320]{1,0:T(8,128)S(1)}, f32[20,320]{1,0:T(8,128)}, u32[]{:S(2)}) copy-start(f32[20,320]{1,0:T(8,128)} %second_ref.1) | copy-start | bytes 76804
  60.5 18.8 %copy-start.4 = (f32[16,256]{1,0:T(8,128)S(1)}, f32[16,256]{1,0:T(8,128)}, u32[]{:S(2)}) copy-start(f32[16,256]{1,0:T(8,128)} %relax_ref.1) | copy-start | bytes 49156
  76.7 5.5 %collective-permute-start.4 = (f32[56,128]{1,0:T(8,128)S(1)}, f32[56,128]{1,0:T(8,128)S(1)}, u32[]{:S(2)}, u32[]{:S(2)}) collective-permute-start(f32[56,128]{1,0:T(8,128)S(1)} %multiply_reduce_fusion.own_ref), channel_id=1, source_target_pairs={{0,64},{64,0},{1,65},{65,1},{2,66},{66,2},{3,67},{67,3},{4,68},{68... | collective-permute-start | bytes 86024 | tf_op jit(solution)/shard_map/ppermute | solution.py:689
